TPU v7x, 32 devices: a whole 2x2x4 slice. The times are simulated.
32 devices in a mesh: tile: 8 (over y, x, core), wave: 4 (over z).
Axes of the slice: x: 2, y: 2, z: 4, core: 2. Of those that a mesh axis runs over, the one named last changes fastest.
Arguments:
- maps: float32 [4, 128, 1024], P(None, None, 'tile'), may hold values from 0 to 2
- measured: float32 [16, 128, 128], P('tile'), may hold values from 0 to 8
- offsets: int32 [16], P('tile'), may hold values from -64 to 64, as said below
- probe: float32 [48, 2, 128, 128], P('wave'), may hold values from -6 to 6
- spectrum: float32 [48], P('wave'), may hold values from 0.05 to 0.5
- wave_index: int32 [48], P('wave'), may hold values from 0 to 47, each once
- edge_band: int32 [48, 4], P('wave'), may hold values from 0 to 2
- band_coef: float32 [2, 3, 4], replicated, may hold values from 0.1 to 0.8
Outputs:
- new_maps: float32 [4, 128, 1024], P(None, None, 'tile')
Inputs may be any that keep to these rules, and one draw needn't show every extreme that they name: `offsets`: a frame reaches at most 64 columns into either neighbouring tile; in every tile one frame starts exactly 64 columns before the tile and another ends exactly 64 columns after it. `wave_index`: each wavelength is held by exactly one slot.
All inputs are finite; a program needn't handle non-finite values.
Results may differ from a plain program's by a relative error of at most 0.0024.
Values sent between devices are 32-bit elements; how exact they have to be, the bound alone decides.
No kernel may reach another device: no remote copies, remote signals or barrier semaphores. Data moves between devices by JAX's collectives and lax.ppermute only.
A program may use at most 64 MiB of HBM per device.

v0:
```python
import math

import jax
import jax.numpy as jnp
from jax import lax
from jax.sharding import PartitionSpec as P

WAVES = 48


relax = 4.0
floor_level = 1.0


def padded(block, sides, width):
    for axis, dim in sides:
        count = lax.axis_size(axis)
        forward = [(i, i + 1) for i in range(count - 1)]
        backward = [(target, source) for source, target in forward]
        low = lax.ppermute(
            lax.slice_in_dim(block, block.shape[dim] - width, None, axis=dim), axis, forward
        )
        high = lax.ppermute(lax.slice_in_dim(block, 0, width, axis=dim), axis, backward)
        block = jnp.concatenate([low, block, high], axis=dim)
    return block


def chirp_table(which_wave, length):
    centred = jnp.arange(length, dtype=jnp.int32) - length // 2
    product = (centred[:, None] * centred[None, :]).astype(jnp.float32)
    sampling = 0.6 + 0.4 * which_wave.astype(jnp.float32) / (WAVES - 1)
    phase_angle = -2.0 * math.pi / length * sampling[..., None, None] * product
    normaliser = 1.0 / math.sqrt(length)
    return (
        (jnp.cos(phase_angle) * normaliser).astype(jnp.bfloat16),
        (jnp.sin(phase_angle) * normaliser).astype(jnp.bfloat16),
    )


def left_product(table, data):
    return jnp.einsum("kn,fnj->fkj", table, data, preferred_element_type=jnp.float32)


def right_product(data, table):
    return jnp.einsum("fkn,nj->fkj", data, table, preferred_element_type=jnp.float32)


def transform(table_re, table_im, data_re, data_im):
    mid_re = (left_product(table_re, data_re) - left_product(table_im, data_im)).astype(
        jnp.bfloat16
    )
    mid_im = (left_product(table_re, data_im) + left_product(table_im, data_re)).astype(
        jnp.bfloat16
    )
    out_re = right_product(mid_re, table_re) - right_product(mid_im, table_im)
    out_im = right_product(mid_re, table_im) + right_product(mid_im, table_re)
    return (out_re, out_im)


def fold_rims(interior, arrived, margin):
    columns = interior.shape[2]
    left_part = interior[:, :, :margin] + arrived[:, :, :margin]
    middle = interior[:, :, margin : columns - margin]
    right_part = interior[:, :, columns - margin :] + arrived[:, :, arrived.shape[2] - margin :]
    return jnp.concatenate([left_part, middle, right_part], axis=2)


def edge_cells(accumulated, margin):
    width = accumulated.shape[2]
    return jnp.concatenate(
        [accumulated[:, :, :margin], accumulated[:, :, width - margin :]], axis=2
    )


def place_frames(stacked, offsets, columns, margin):
    frame_count, channels, length = (stacked.shape[0], stacked.shape[1], stacked.shape[2])
    accumulated = jnp.zeros((channels, length, columns + 2 * margin), jnp.float32)
    for frame in range(frame_count):
        current = lax.dynamic_slice_in_dim(accumulated, offsets[frame] + margin, length, 2)
        accumulated = lax.dynamic_update_slice_in_dim(
            accumulated, current + stacked[frame], offsets[frame] + margin, 2
        )
    return accumulated


def per_device(maps, measured, offsets, probe, spectrum, wave_index, edge_band, band_coef):
    materials, length, columns = maps.shape
    frame_count = measured.shape[0]
    band_count = band_coef.shape[1]
    margin = length // 2
    extended = padded(maps, (("tile", 2),), margin)
    windows = jnp.stack(
        [
            lax.dynamic_slice_in_dim(extended, offsets[frame] + margin, length, 2)
            for frame in range(frame_count)
        ]
    )
    onehot = (edge_band[:, :, None] == jnp.arange(band_count, dtype=jnp.int32)).astype(jnp.float32)
    coefficient = jnp.einsum("smb,cbm->csm", onehot, band_coef, precision=lax.Precision.HIGHEST)

    def forward_slot(partial_value, inputs):
        wave_probe, absorb_coef, phase_coef, weight, which_wave = inputs
        absorb = jnp.einsum("m,fmrk->frk", absorb_coef, windows, precision=lax.Precision.HIGHEST)
        phase_sum = jnp.einsum("m,fmrk->frk", phase_coef, windows, precision=lax.Precision.HIGHEST)
        damping = jnp.exp(-absorb)
        obj_re = damping * jnp.cos(phase_sum)
        obj_im = damping * jnp.sin(phase_sum)
        psi_re = wave_probe[0] * obj_re - wave_probe[1] * obj_im
        psi_im = wave_probe[0] * obj_im + wave_probe[1] * obj_re
        table_re, table_im = chirp_table(which_wave, length)
        far_re, far_im = transform(
            table_re, table_im, psi_re.astype(jnp.bfloat16), psi_im.astype(jnp.bfloat16)
        )
        partial_value = partial_value + weight * (far_re * far_re + far_im * far_im)
        return (partial_value, (table_re, table_im, psi_re, psi_im, far_re, far_im))

    partial_value = jnp.zeros((frame_count, length, length), jnp.float32)
    partial_value, stored = lax.scan(
        forward_slot, partial_value, (probe, coefficient[0], coefficient[1], spectrum, wave_index)
    )
    intensity = lax.psum(partial_value, "wave")
    shortfall = jnp.sqrt(measured / jnp.maximum(intensity, floor_level)) - 1.0

    def backward_slot(totals, inputs):
        absorb_coef, phase_coef, weight, table_re, table_im, psi_re, psi_im, far_re, far_im = inputs
        factor = weight * shortfall
        back_re, back_im = transform(
            table_re,
            -table_im,
            (factor * far_re).astype(jnp.bfloat16),
            (factor * far_im).astype(jnp.bfloat16),
        )
        cross_re = psi_re * back_re + psi_im * back_im
        cross_im = psi_re * back_im - psi_im * back_re
        gradient = (
            cross_re[:, None] * (-absorb_coef)[None, :, None, None]
            + cross_im[:, None] * phase_coef[None, :, None, None]
        )
        power_sum = weight * (psi_re * psi_re + psi_im * psi_im)
        return ((totals[0] + gradient, totals[1] + power_sum), None)

    start_totals = (
        jnp.zeros((frame_count, materials, length, length), jnp.float32),
        jnp.zeros((frame_count, length, length), jnp.float32),
    )
    table_re, table_im, psi_re, psi_im, far_re, far_im = stored
    (gradient, power_sum), _ = lax.scan(
        backward_slot,
        start_totals,
        (
            coefficient[0],
            coefficient[1],
            spectrum,
            table_re,
            table_im,
            psi_re,
            psi_im,
            far_re,
            far_im,
        ),
    )
    stacked = jnp.concatenate([gradient, power_sum[:, None]], axis=1)
    accumulated = place_frames(stacked, offsets, columns, margin)
    arrived = padded(edge_cells(accumulated, margin), (("tile", 2),), margin)
    summed = lax.psum(
        fold_rims(accumulated[:, :, margin : margin + columns], arrived, margin), "wave"
    )
    return maps + relax * summed[:materials] / (summed[materials] + 1.0)


def solution(mesh):
    in_specs = (
        P(None, None, "tile"),
        P("tile", None, None),
        P("tile"),
        P("wave", None, None, None),
        P("wave"),
        P("wave"),
        P("wave", None),
        P(),
    )
    out_specs = P(None, None, "tile")
    return jax.shard_map(
        per_device, mesh=mesh, in_specs=in_specs, out_specs=out_specs, check_vma=False
    )
```

profile of v0, /device:TPU:0, one launch (start us, length us, event | category | flops | bytes accessed | tf_op | source)
XLA Modules:
  0.0 355.2 jit_solution(11261539689890777825)
XLA Ops:
  6.5 1.2 fusion.115
  7.7 2.4 collective-permute-start
  10.1 1.3 collective-permute-start.1
  11.4 1.4 fusion.117
  17.3 1.2 pad_maximum_fusion
  18.9 154.0 %while.38 = (s32[]{:T(128)}, f32[2,128,128]{2,1,0:T(8,128)S(1)}, bf16[12,128,128]{2,1,0:T(8,128)(2,1)S(1)}, bf16[12,128,128]{2,1,0:T(8,128)(2,1)S(1)}, f32[12,2,...) while((s32[]{:T(128)}, f32[2,128,128]{2,1,0:T(8,128)S(1)}, ...), condition=%wide.region_1.2_spmd.clone, body=%wide.region_0.1_spmd.clone.sunk | while | flops 71778440 | bytes 5973319 | solution.py:118
  18.9 1.3 fusion.204
  20.2 1.3 fusion.205
  22.7 1.2 bitcast_dynamic-update-slice_fusion.7
  31.7 1.3 fusion.204
  33.0 1.3 fusion.205
  35.5 1.2 bitcast_dynamic-update-slice_fusion.7
  44.5 1.3 fusion.204
  45.9 1.3 fusion.205
  48.3 1.2 bitcast_dynamic-update-slice_fusion.7
  57.3 1.3 fusion.204
  58.7 1.3 fusion.205
  61.2 1.2 bitcast_dynamic-update-slice_fusion.7
  70.2 1.3 fusion.204
  71.5 1.3 fusion.205
  74.0 1.2 bitcast_dynamic-update-slice_fusion.7
  83.0 1.3 fusion.204
  84.4 1.3 fusion.205
  86.8 1.2 bitcast_dynamic-update-slice_fusion.7
  95.8 1.3 fusion.204
  97.2 1.3 fusion.205
  99.7 1.3 bitcast_dynamic-update-slice_fusion.7
  108.7 1.3 fusion.204
  110.1 1.3 fusion.205
  112.5 1.2 bitcast_dynamic-update-slice_fusion.7
  121.5 1.3 fusion.204
  122.9 1.3 fusion.205
  125.3 1.2 bitcast_dynamic-update-slice_fusion.7
  134.3 1.3 fusion.204
  135.7 1.3 fusion.205
  138.2 1.2 bitcast_dynamic-update-slice_fusion.7
  147.2 1.3 fusion.204
  148.6 1.3 fusion.205
  151.0 1.2 bitcast_dynamic-update-slice_fusion.7
  160.0 1.3 fusion.204
  161.4 1.3 fusion.205
  163.9 1.2 bitcast_dynamic-update-slice_fusion.7
  173.6 39.1 %all-reduce.3.cloned.1.call-done = f32[2,128,128]{2,1,0:T(8,128)} async-done(((f32[2,128,128]{2,1,0:T(8,128)}), f32[2,128,128]{2,1,0:T(8,128)}) %all-reduce.3.cloned.1.call-update) | async-done | bytes 131088 | tf_op jit(solution)/shard_map/psum | solution.py:121
  213.7 70.5 %while.39 = (s32[]{:T(128)}, f32[2,4,128,128]{3,2,1,0:T(8,128)S(1)}, f32[2,128,128]{2,1,0:T(8,128)S(1)}, f32[12,2,128,128]{2,3,1,0:T(8,128)}, f32[12]{0:T(128)S(...) while((s32[]{:T(128)}, ...), condition=%wide.region_4.5_spmd.clone, body=%wide.region_3.4_spmd.clone.sunk | while | flops 68583424 | bytes 5898552 | solution.py:147
  214.3 1.6 fusion.229
  220.2 1.6 fusion.229
  226.1 1.6 fusion.229
  232.0 1.6 fusion.229
  237.8 1.6 fusion.229
  243.7 1.6 fusion.229
  249.6 1.6 fusion.229
  255.5 1.6 fusion.229
  261.4 1.6 fusion.229
  267.2 1.6 fusion.229
  273.1 1.6 fusion.229
  279.0 1.6 fusion.229
  284.4 3.1 dynamic_update_slice.44
  287.6 4.5 %dynamic_update_slice.45 = f32[5,128,256]{2,1,0:T(8,128)S(1)} dynamic-update-slice(f32[5,128,256]{2,1,0:T(8,128)S(1)} %dynamic_update_slice.44, f32[5,128,128]{2,1,0:T(8,128)S(1)} %fusion.110, s32[]{:T(128)} %constant.93.clone.1, s32[]{:T(128)} %constant.93.clone.1, s32[]{:T(128)S(6)} %select_n.10) | dynamic-update-slice | bytes 655364 | tf_op jit(solution)/shard_map/dynamic_update_slice | solution.py:80
  292.3 1.3 collective-permute-start.2
  293.6 1.2 collective-permute-done.2
  295.0 1.4 collective-permute-start.3
  296.5 6.6 %collective-permute-done.3 = f32[5,128,64]{2,1,0:T(8,128)S(1)} collective-permute-done((f32[5,128,64]{2,1,0:T(8,128)S(1)}, f32[5,128,64]{2,1,0:T(8,128)S(1)}, u32[]{:S(2)}, u32[]{:S(2)}) %collective-permute-start.3) | collective-permute-done | bytes 163872 | tf_op jit(solution)/shard_map/ppermute | solution.py:23
  304.0 41.8 %all-reduce.5.cloned.1.call-done = f32[5,128,128]{2,1,0:T(8,128)} async-done(((f32[5,128,128]{2,1,0:T(8,128)}), f32[5,128,128]{2,1,0:T(8,128)}) %all-reduce.5.cloned.1.call-update) | async-done | bytes 327696 | tf_op jit(solution)/shard_map/psum | solution.py:165
  346.7 1.7 fusion.112
  (425 shorter events, 155.8 us)
Async XLA Ops:
  6.5 206.2 %all-reduce.3.cloned.1.call-start = ((), (), s32[]{:S(2)}) async-start(), calls=%async_computation | async-start | bytes 262144 | tf_op jit(solution)/shard_map/psum | solution.py:121
  7.7 9.6 %collective-permute-start = (f32[4,128,64]{2,1,0:T(8,128)S(1)}, f32[4,128,64]{2,1,0:T(8,128)S(1)}, u32[]{:S(2)}, u32[]{:S(2)}) collective-permute-start(f32[4,128,64]{2,1,0:T(8,128)S(1)} %get-tuple-element.457), channel_id=1, source_target_pairs={{0,4},{4,8},{8,12},{12,16},{16,20},{20,24},{24,28},{1,5},{5,9},{9,... | collective-permute-start | bytes 393224 | tf_op jit(solution)/shard_map/ppermute | solution.py:20
  10.1 7.3 %collective-permute-start.1 = (f32[4,128,64]{2,1,0:T(8,128)S(1)}, f32[4,128,64]{2,1,0:T(8,128)S(1)}, u32[]{:S(2)}, u32[]{:S(2)}) collective-permute-start(f32[4,128,64]{2,1,0:T(8,128)S(1)} %get-tuple-element.458), channel_id=1, source_target_pairs={{4,0},{8,4},{12,8},{16,12},{20,16},{24,20},{28,24},{5,1},{9,5},{13... | collective-permute-start | bytes 393224 | tf_op jit(solution)/shard_map/ppermute | solution.py:23
  17.3 1.5 copy-start.3
  17.3 1.5 copy-start.4
  18.9 193.9 %copy-start.2 = (f32[2,128,128]{2,1,0:T(8,128)S(1)}, f32[2,128,128]{2,1,0:T(8,128)}, u32[]{:S(2)}) copy-start(f32[2,128,128]{2,1,0:T(8,128)} %param.13) | copy-start | bytes 393220
  172.9 0.7 copy-start
  173.6 172.3 %all-reduce.5.cloned.1.call-start = ((), (), s32[]{:S(2)}) async-start(), calls=%async_computation.1 | async-start | bytes 655360 | tf_op jit(solution)/shard_map/psum | solution.py:165
  292.3 2.5 collective-permute-start.2
  295.0 51.7 %copy-start.1 = (f32[4,128,128]{2,1,0:T(8,128)S(1)}, f32[4,128,128]{2,1,0:T(8,128)}, u32[]{:S(2)}) copy-start(f32[4,128,128]{2,1,0:T(8,128)} %param.12) | copy-start | bytes 786436
  295.0 8.1 %collective-permute-start.3 = (f32[5,128,64]{2,1,0:T(8,128)S(1)}, f32[5,128,64]{2,1,0:T(8,128)S(1)}, u32[]{:S(2)}, u32[]{:S(2)}) collective-permute-start(f32[5,128,64]{2,1,0:T(8,128)S(1)} %get-tuple-element.454), channel_id=1, source_target_pairs={{4,0},{8,4},{12,8},{16,12},{20,16},{24,20},{28,24},{5,1},{9,5},{13... | collective-permute-start | bytes 491528 | tf_op jit(solution)/shard_map/ppermute | solution.py:23
Sparse Core Ops, SparseCore 0:
  173.7 39.0 all-reduce.2
  304.2 41.6 all-reduce.4
where the time goes:
time: 357 us; the launch traced here: 355 us
  matrix products  114 us (32%)
  waiting for transfers between devices  88.8 us (25%)
  local copies, waits for them, and re-layouts  72.2 us (20%)
  other arithmetic  46.8 us (13%)
  between operations  16.3 us (5%)
  loops' own time  10.2 us (3%)
  starting transfers between devices  6.44 us (2%)
    dot_general x96, matrix products, right_product(): jnp.einsum('fkn,nj->fkj', data, table, preferred_element_type=jnp.float32)  53.6 us
    psum x1, waiting for transfers between devices, per_device(): lax.psum(fold_rims(accumulated[:, :, margin:margin + columns], arrived, m...  41.8 us
    psum x1, waiting for transfers between devices, per_device(): intensity = lax.psum(partial_value, 'wave')  39.1 us
    dynamic_slice x72, local copies, waits for them, and re-layouts, per_device(): lax.scan(forward_slot, partial_value, (probe, coefficient[0], coefficient...  36.9 us
    dot_general x96, matrix products, left_product(): jnp.einsum('kn,fnj->fkj', table, data, preferred_element_type=jnp.float32)  29.9 us
    convert_element_type x12, other arithmetic, backward_slot(): (factor * far_im).astype(jnp.bfloat16)  19.7 us
    dynamic_update_slice x24, other arithmetic, per_device(): lax.scan(forward_slot, partial_value, (probe, coefficient[0], coefficient...  19 us
    dot_general x12, matrix products, forward_slot(): jnp.einsum('m,fmrk->frk', absorb_coef, windows, precision=lax.Precision.H...  15 us
  transfers between devices with their start and end apart: 6, of which 4 were waited for; matrix products, arithmetic and copies ran while one was open for 1% of the time, Pallas kernels for 0%

commit v1 on v0

v1 whole, which is shorter than its diff:
```python
import math

import jax
import jax.numpy as jnp
import numpy as np
from jax import lax
from jax.experimental import pallas as pl
from jax.experimental.pallas import tpu as pltpu
from jax.sharding import PartitionSpec as P

WAVES = 48

relax = 4.0
floor_level = 1.0

VM = pl.BlockSpec(memory_space=pltpu.VMEM)
SM = pl.BlockSpec(memory_space=pltpu.SMEM)
f32 = jnp.float32
bf16 = jnp.bfloat16


def fit(parity, degree):
    nodes = 0.5 * np.cos(np.pi * (np.arange(400) + 0.5) / 800)
    turns = 2 * np.pi * nodes
    value = np.sin(turns) if parity else np.cos(turns)
    powers = np.stack([nodes ** (parity + 2 * i) for i in range(degree)], axis=1)
    return [float(c) for c in np.linalg.lstsq(powers, value, rcond=None)[0]]


SIN = fit(1, 6)
COS = fit(0, 7)


def horner(square, coefs):
    total = coefs[-1]
    for c in coefs[-2::-1]:
        total = total * square + c
    return total


def cos_sin(turns):
    r = turns - jnp.round(turns)
    square = r * r
    return horner(square, COS), horner(square, SIN) * r


def lanes(rows, length):
    return lax.broadcasted_iota(jnp.int32, (rows, length), 1)


def halves_packed(top, bottom, upper):
    length = top.shape[-1]
    half = length // 2
    low = lanes(top.shape[0], length) < half
    if upper:
        return jnp.where(low, pltpu.roll(top, half, 1), bottom)
    return jnp.where(low, top, pltpu.roll(bottom, half, 1))


def block(table_ref, s, kind):
    re, im, neg = table_ref[s, 0], table_ref[s, 1], table_ref[s, 2]
    top, bottom = ((re, neg), (im, re)) if kind == "L" else ((re, im), (neg, re))
    return jnp.concatenate(
        [jnp.concatenate(top, axis=1), jnp.concatenate(bottom, axis=1)], axis=0
    )


def transform(left, right, re, im):
    length = re.shape[0]
    stacked = jnp.concatenate([re.astype(bf16), im.astype(bf16)], axis=0)
    mid = jnp.dot(left, stacked, preferred_element_type=f32).astype(bf16)
    beside = jnp.concatenate([mid[:length], mid[length:]], axis=1)
    return jnp.dot(beside, right, preferred_element_type=f32)


def pack_kernel(offsets, maps, measured, out):
    materials, length, _ = maps.shape
    half = length // 2
    for m in range(materials):
        out[m * half : (m + 1) * half] = halves_packed(maps[m, :half], maps[m, half:], False)
    left = jnp.where(offsets[0] < offsets[1], 0, 1)
    out[materials * half :] = measured[left]


def first_kernel(tiles, spectrum, wave_index, edge_band, band_coef, maps, probe, table, power):
    materials, length, _ = maps.shape
    half = length // 2
    slots = probe.shape[0]
    tile = lax.axis_index("tile")
    group = 8
    centred_lane = (lanes(group, length) - half).astype(f32)
    row = lax.broadcasted_iota(jnp.int32, (group, length), 0)
    fine = row.astype(f32) * centred_lane / length
    normaliser = 1.0 / math.sqrt(length)
    coarse_rows = length // group

    def tables(s, carry):
        which = jnp.full((group, length), wave_index[s], jnp.int32).astype(f32)
        sampling = 0.6 + 0.4 * which / (WAVES - 1)
        fine_cos, fine_sin = cos_sin(sampling * fine)
        fine_cos, fine_sin = fine_cos * normaliser, fine_sin * normaliser
        for base in range(0, coarse_rows, group):
            step = ((row + base) * group - half).astype(f32) * centred_lane / length
            cos, sin = cos_sin(sampling * step)
            for i in range(0, group, 2):
                parts = []
                for j in (i, i + 1):
                    c = jnp.broadcast_to(cos[j : j + 1], (group, length))
                    n = jnp.broadcast_to(sin[j : j + 1], (group, length))
                    parts.append((c * fine_cos - n * fine_sin, n * fine_cos + c * fine_sin))
                at = pl.ds((base + i) * group, 2 * group)
                re = jnp.concatenate([parts[0][0], parts[1][0]], axis=0).astype(bf16)
                positive = jnp.concatenate([parts[0][1], parts[1][1]], axis=0)
                table[s, 0, at, :] = re
                table[s, 1, at, :] = (-positive).astype(bf16)
                table[s, 2, at, :] = positive.astype(bf16)
        return carry

    lax.fori_loop(0, slots, tables, 0)

    chunk = 32
    low = lanes(chunk, length) < half
    frames = jnp.where(
        low,
        jnp.where(tile == tiles - 1, 1.0, 2.0),
        jnp.where(tile == 0, 1.0, 2.0),
    )
    for start in range(0, length, chunk):
        at = slice(start, start + chunk)
        own = [pltpu.roll(maps[m, at], half, 1) for m in range(materials)]

        def add(s, total):
            absorb = None
            for m in range(materials):
                coef = band_coef[0, edge_band[s, m], m] * (-2.0 * math.log2(math.e))
                absorb = coef * own[m] if absorb is None else absorb + coef * own[m]
            re, im = probe[s, 0, at], probe[s, 1, at]
            return total + (spectrum[s] * jnp.exp2(absorb)) * (re * re + im * im)

        total = lax.fori_loop(0, slots, add, jnp.zeros((chunk, length), f32))
        power[at] = frames * total


def piece(array, q, count, half_rows):
    groups = count // 2
    rows = 2 * half_rows
    start = pl.multiple_of(lax.rem(q, groups) * rows, half_rows)
    top = array[pl.ds(start, half_rows), :]
    bottom = array[pl.ds(start + half_rows, half_rows), :]
    return jnp.where(
        q < groups, halves_packed(top, bottom, False), halves_packed(top, bottom, True)
    )


def forward_kernel(
    tiles, count, spectrum, edge_band, band_coef, maps, halo, probe, table, power,
    psi, far, far_edge, keep, edge_keep, *messages_and_scratch,
):
    messages = messages_and_scratch[: count - 1]
    window, total, total_edge = messages_and_scratch[count - 1 :]
    materials, length, _ = maps.shape
    half = length // 2
    slots = probe.shape[0]
    edge = lax.axis_index("tile") == tiles - 1
    me = lax.axis_index("wave")
    low = lanes(half, length) < half
    for m in range(materials):
        packed = halo[m * half : (m + 1) * half]
        window[m, :half] = jnp.where(
            low, pltpu.roll(maps[m, :half], half, 1), pltpu.roll(packed, half, 1)
        )
        window[m, half:] = jnp.where(low, pltpu.roll(maps[m, half:], half, 1), packed)
    total[...] = jnp.zeros_like(total)
    chunk = 32

    def exit_wave(s):
        for start in range(0, length, chunk):
            at = slice(start, start + chunk)
            absorb, phase = None, None
            for m in range(materials):
                band = edge_band[s, m]
                a = band_coef[0, band, m] * (-math.log2(math.e))
                b = band_coef[1, band, m] * (0.5 / math.pi)
                w = window[m, at]
                absorb = a * w if absorb is None else absorb + a * w
                phase = b * w if phase is None else phase + b * w
            damping = jnp.exp2(absorb)
            cos, sin = cos_sin(phase)
            cos, sin = damping * cos, damping * sin
            re, im = probe[s, 0, at], probe[s, 1, at]
            psi[s, 0, at] = re * cos - im * sin
            psi[s, 1, at] = re * sin + im * cos

    def add_intensity(s, got, total):
        re, im = got[:, :length], got[:, length:]
        total[...] += spectrum[s] * (re * re + im * im)

    @pl.when(jnp.logical_not(edge))
    def _():
        def step(s, carry):
            exit_wave(s)
            got = transform(block(table, s, "L"), block(table, s, "R"), psi[s, 0], psi[s, 1])
            far[s] = got
            add_intensity(s, got, total)
            return carry

        lax.fori_loop(0, slots, step, 0)

    @pl.when(edge)
    def _():
        total_edge[...] = jnp.zeros_like(total_edge)
        low = lanes(length, length) < half

        def step(s, carry):
            exit_wave(s)
            left, right = block(table, s, "L"), block(table, s, "R")
            re, im, bare_re, bare_im = psi[s, 0], psi[s, 1], probe[s, 0], probe[s, 1]
            got = transform(left, right, jnp.where(low, re, bare_re), jnp.where(low, im, bare_im))
            far[s] = got
            add_intensity(s, got, total)
            got = transform(left, right, jnp.where(low, bare_re, re), jnp.where(low, bare_im, im))
            far_edge[s] = got
            add_intensity(s, got, total_edge)
            return carry

        lax.fori_loop(0, slots, step, 0)
        edge_keep[...] = total_edge[...]

    half_rows = length // count
    for k, message in enumerate((keep, *messages)):
        message[:length] = total[...]
        message[length:] = piece(power, lax.rem(me + k, count), count, half_rows)


def backward_kernel(
    tiles, count, offsets, spectrum, edge_band, band_coef, measured, halo, table, psi, far, far_edge,
    *rest,
):
    shares, rest = rest[:count], rest[count:]
    edges, rest = rest[:count], rest[count:]
    sends, rest = rest[:count], rest[count:]
    power, shortfall, shortfall_edge, gradient, back = rest
    materials = edge_band.shape[1]
    length = measured.shape[1]
    half = length // 2
    slots = psi.shape[0]
    edge = lax.axis_index("tile") == tiles - 1
    me = lax.axis_index("wave")
    half_rows = length // count
    intensity = shares[0][:length]
    powers = shares[0][length:]
    for share in shares[1:]:
        intensity = intensity + share[:length]
        powers = powers + share[length:]
    power[...] = relax / (powers + 1.0)
    mine = jnp.sqrt(measured[jnp.where(offsets[0] < offsets[1], 1, 0)])
    theirs = jnp.sqrt(halo[materials * half :])
    inverse = lax.rsqrt(jnp.maximum(intensity, floor_level))
    gradient[...] = jnp.zeros_like(gradient)

    def delta(s, far, shortfall):
        factor = spectrum[s] * shortfall[...]
        return factor * far[s, :, :length], factor * far[s, :, length:]

    chunk = 32

    def collect(s):
        for start in range(0, length, chunk):
            at = slice(start, start + chunk)
            re, im = psi[s, 0, at], psi[s, 1, at]
            back_re, back_im = back[at, :length], back[at, length:]
            cross_re = re * back_re + im * back_im
            cross_im = re * back_im - im * back_re
            for m in range(materials):
                band = edge_band[s, m]
                gradient[m, at] += band_coef[1, band, m] * cross_im - band_coef[0, band, m] * cross_re

    @pl.when(jnp.logical_not(edge))
    def _():
        shortfall[...] = (mine + theirs) * inverse - 2.0

        def step(s, carry):
            back[...] = transform(block(table, s, "R"), block(table, s, "L"), *delta(s, far, shortfall))
            collect(s)
            return carry

        lax.fori_loop(0, slots, step, 0)

    @pl.when(edge)
    def _():
        shortfall[...] = mine * inverse - 1.0
        intensity = edges[0][...]
        for share in edges[1:]:
            intensity = intensity + share[...]
        shortfall_edge[...] = theirs * lax.rsqrt(jnp.maximum(intensity, floor_level)) - 1.0
        low = (lax.broadcasted_iota(jnp.int32, (length, 2 * length), 1) & (length - 1)) < half

        def step(s, carry):
            left, right = block(table, s, "R"), block(table, s, "L")
            one = transform(left, right, *delta(s, far, shortfall))
            two = transform(left, right, *delta(s, far_edge, shortfall_edge))
            back[...] = jnp.where(low, one, two)
            collect(s)
            return carry

        lax.fori_loop(0, slots, step, 0)

    for k, send in enumerate(sends):
        for m in range(materials):
            send[m] = piece(gradient.at[m], lax.rem(me + k, count), count, half_rows)


def update_kernel(count, maps, power, *refs):
    own, arrived, out = refs[0], refs[1:-1], refs[-1]
    materials, length, _ = maps.shape
    half = length // 2
    me = lax.axis_index("wave")
    half_rows = length // count
    for m in range(materials):
        total = jnp.where(me < count // 2, own[m], arrived[0][m])
        for other in arrived[1:]:
            total = total + other[m]
        here = piece(maps.at[m], lax.rem(me + count // 2, count), count, half_rows)
        out[m] = here + power[...] * total


def join_kernel(count, *refs):
    shares, out = refs[:count], refs[count]
    materials, length, _ = out.shape
    half = length // 2
    me = lax.axis_index("wave")
    half_rows = length // count
    groups = count // 2
    low = lanes(half_rows, length) < half
    for position in range(count):

        @pl.when(me == position)
        def _():
            held = lambda q: shares[(q - position) % count]
            for g in range(groups):
                right, left = held(g), held(g + groups)
                start = g * 2 * half_rows
                for m in range(materials):
                    r, l = right[m], left[m]
                    out[m, start : start + half_rows] = jnp.where(low, l, pltpu.roll(r, half, 1))
                    out[m, start + half_rows : start + 2 * half_rows] = jnp.where(
                        low, pltpu.roll(l, half, 1), r
                    )


def params(mib=40):
    return pltpu.CompilerParams(vmem_limit_bytes=mib * 2**20)


def per_device(tiles, count, maps, measured, offsets, probe, spectrum, wave_index, edge_band, band_coef):
    materials, length, columns = maps.shape
    slots = probe.shape[0]
    half = length // 2
    shape = jax.ShapeDtypeStruct
    half_rows = length // count

    packed = pl.pallas_call(
        pack_kernel,
        out_shape=shape((materials * half + length, length), f32),
        in_specs=[SM, VM, VM],
        out_specs=VM,
        compiler_params=params(),
        name="pack",
    )(offsets, maps, measured)
    halo = lax.ppermute(packed, "tile", [(i, (i - 1) % tiles) for i in range(tiles)])

    table, power = pl.pallas_call(
        lambda *refs: first_kernel(tiles, *refs),
        out_shape=(shape((slots, 3, length, length), bf16), shape((length, length), f32)),
        in_specs=[SM] * 4 + [VM] * 2,
        out_specs=(VM, VM),
        compiler_params=params(),
        cost_estimate=pl.CostEstimate(flops=10**9, bytes_accessed=2**22, transcendentals=0),
        name="tables",
    )(spectrum, wave_index, edge_band, band_coef, maps, probe)

    share = shape((length + half_rows, length), f32)
    psi, far, far_edge, keep, edge_keep, *messages = pl.pallas_call(
        lambda *refs: forward_kernel(tiles, count, *refs),
        out_shape=(
            shape((slots, 2, length, length), f32),
            shape((slots, length, 2 * length), f32),
            shape((slots, length, 2 * length), f32),
            share,
            shape((length, length), f32),
        )
        + (share,) * (count - 1),
        in_specs=[SM] * 3 + [VM] * 5,
        out_specs=(VM,) * (4 + count),
        scratch_shapes=[
            pltpu.VMEM((materials, length, length), f32),
            pltpu.VMEM((length, length), f32),
            pltpu.VMEM((length, length), f32),
        ],
        compiler_params=params(),
        name="forward",
    )(spectrum, edge_band, band_coef, maps, halo, probe, table, power)

    both = ("tile", "wave")
    shares, edges = [keep], [edge_keep]
    for k in range(1, count):
        ring = [(w, (w + k) % count) for w in range(count)]
        shares.append(lax.ppermute(messages[k - 1], "wave", ring))
        last = (tiles - 1) * count
        edges.append(lax.ppermute(edge_keep, both, [(last + a, last + b) for a, b in ring]))

    *sends, scale = pl.pallas_call(
        lambda *refs: backward_kernel(tiles, count, *refs),
        out_shape=(shape((materials, half_rows, length), f32),) * count
        + (shape((half_rows, length), f32),),
        in_specs=[SM] * 4 + [VM] * (6 + 2 * count),
        out_specs=(VM,) * (count + 1),
        scratch_shapes=[
            pltpu.VMEM((length, length), f32),
            pltpu.VMEM((length, length), f32),
            pltpu.VMEM((materials, length, length), f32),
            pltpu.VMEM((length, 2 * length), f32),
        ],
        compiler_params=params(),
        name="backward",
    )(offsets, spectrum, edge_band, band_coef, measured, halo, table, psi, far, far_edge, *shares, *edges)

    def owner(t, q):
        return (t + (q >= count // 2)) % tiles * count + q

    arrived = []
    for k in range(count):
        pairs = [
            (t * count + w, owner(t, (w + k) % count)) for t in range(tiles) for w in range(count)
        ]
        arrived.append(lax.ppermute(sends[k], both, [p for p in pairs if p[0] != p[1]]))

    new = pl.pallas_call(
        lambda *refs: update_kernel(count, *refs),
        out_shape=shape((materials, half_rows, length), f32),
        in_specs=[VM] * (3 + count),
        out_specs=VM,
        compiler_params=params(),
        name="update",
    )(maps, scale, sends[0], *arrived)

    parts = [new]
    for k in range(1, count):
        parts.append(lax.ppermute(new, "wave", [((w + k) % count, w) for w in range(count)]))
    return pl.pallas_call(
        lambda *refs: join_kernel(count, *refs),
        out_shape=shape((materials, length, length), f32),
        in_specs=[VM] * count,
        out_specs=VM,
        compiler_params=params(),
        name="join",
    )(*parts)


def solution(mesh):
    in_specs = (
        P(None, None, "tile"),
        P("tile", None, None),
        P("tile"),
        P("wave", None, None, None),
        P("wave"),
        P("wave"),
        P("wave", None),
        P(),
    )
    out_specs = P(None, None, "tile")
    tiles, count = mesh.shape["tile"], mesh.shape["wave"]
    return jax.shard_map(
        lambda *args: per_device(tiles, count, *args),
        mesh=mesh,
        in_specs=in_specs,
        out_specs=out_specs,
        check_vma=False,
    )
```

time: 357 us -> 64.3 us (0.18)
  matrix products: 114 us -> 0 us
  waiting for transfers between devices: 88.8 us -> 9.44 us
  local copies, waits for them, and re-layouts: 72.2 us -> 7.65 us
  other arithmetic: 46.8 us -> 0 us
  starting transfers between devices: 6.44 us -> 31 us
  between operations: 16.3 us -> 0.15 us
  Pallas kernels: 0 us -> 15.7 us
  loops' own time: 10.2 us -> 0 us
    dot_general x217 -> x0, matrix products: 114 us -> none  [the longest x96 53.6 us: right_product(): jnp.einsum('fkn,nj->fkj', data, table, preferred_element_type=jnp.float32)]
    psum x2 -> x0, waiting for transfers between devices: 80.9 us -> none  [the longest x1 41.8 us: per_device(): lax.psum(fold_rims(accumulated[:, :, margin:margin + columns], arrived, m...]
    dynamic_slice x72 -> x0, local copies, waits for them, and re-layouts: 36.9 us -> none  [per_device(): lax.scan(forward_slot, partial_value, (probe, coefficient[0], coefficient...]
    ppermute x4 -> x14, starting transfers between devices: 6.4 us -> 31 us  [the longest x3 15.7 us: per_device(): lax.ppermute(new, 'wave', [((w + k) % count, w) for w in range(count)])]
    convert_element_type x12 -> x0, other arithmetic: 19.7 us -> none  [backward_slot(): (factor * far_im).astype(jnp.bfloat16)]
    dynamic_update_slice x24 -> x0, other arithmetic: 19 us -> none  [per_device(): lax.scan(forward_slot, partial_value, (probe, coefficient[0], coefficient...]
    pallas_call x0 -> x6, Pallas kernels: none -> 15.7 us  [the longest x1 6.13 us: per_device(): pl.pallas_call(lambda *refs: forward_kernel(tiles, count, *refs), out_sha...]
    dynamic_update_slice x14 -> x0, local copies, waits for them, and re-layouts: 15.6 us -> none  [the longest x12 8 us: per_device(): lax.scan(forward_slot, partial_value, (probe, coefficient[0], coefficient...]
  transfers between devices with their start and end apart: 6 -> 14, of which waited for: 4 -> 7; matrix products, arithmetic and copies ran while one was open for 1% -> 2% of each run, Pallas kernels for 0% -> 4%
where the time goes in v1:
time: 64.3 us; the launch traced here: 63.9 us
  starting transfers between devices  31 us (48%)
  Pallas kernels  15.7 us (24%)
  waiting for transfers between devices  9.44 us (15%)
  local copies, waits for them, and re-layouts  7.65 us (12%)
    ppermute x3, starting transfers between devices, per_device(): lax.ppermute(new, 'wave', [((w + k) % count, w) for w in range(count)])  15.7 us
    unnamed x22, local copies, waits for them, and re-layouts  7.65 us
    pallas_call x1, Pallas kernels, per_device(): pl.pallas_call(lambda *refs: forward_kernel(tiles, count, *refs), out_sha...  6.13 us
    ppermute x3, starting transfers between devices, per_device(): shares.append(lax.ppermute(messages[k - 1], 'wave', ring))  5.56 us
    pallas_call x1, Pallas kernels, per_device(): pl.pallas_call(lambda *refs: backward_kernel(tiles, count, *refs), out_sh...  5.19 us
    ppermute x4, waiting for transfers between devices, per_device(): lax.ppermute(sends[k], both, [p for p in pairs if p[0] != p[1]])  4.79 us
    ppermute x4, starting transfers between devices, per_device(): lax.ppermute(sends[k], both, [p for p in pairs if p[0] != p[1]])  4.39 us
    ppermute x1, starting transfers between devices, per_device(): lax.ppermute(packed, 'tile', [(i, (i - 1) % tiles) for i in range(tiles)])  3.39 us
  transfers between devices with their start and end apart: 14, of which 7 were waited for; matrix products, arithmetic and copies ran while one was open for 2% of the time, Pallas kernels for 4%

profile of v1, /device:TPU:0, one launch (start us, length us, event | category | flops | bytes accessed | tf_op | source)
XLA Modules:
  0.0 63.9 jit_solution(12208337446685479408)
XLA Ops:
  0.0 0.0 copy-start
  0.0 0.9 %copy-done = f32[4,128,128]{2,1,0:T(8,128)S(1)} copy-done((f32[4,128,128]{2,1,0:T(8,128)S(1)}, f32[4,128,128]{2,1,0:T(8,128)}, u32[]{:S(2)}) %copy-start) | copy-done | bytes 262168
  1.0 0.0 copy-start.4
  1.0 0.9 %copy-done.4 = f32[2,128,128]{2,1,0:T(8,128)S(1)} copy-done((f32[2,128,128]{2,1,0:T(8,128)S(1)}, f32[2,128,128]{2,1,0:T(8,128)}, u32[]{:S(2)}) %copy-start.4) | copy-done | bytes 131096
  1.9 0.0 copy-start.6
  1.9 0.7 %copy-done.6 = s32[2]{0:T(128)S(1)} copy-done((s32[2]{0:T(128)S(1)}, s32[2]{0:T(128)}, u32[]{:S(2)}) %copy-start.6) | copy-done | bytes 32
  2.5 0.6 pack.1
  3.2 3.4 %collective-permute-start = (f32[384,128]{1,0:T(8,128)S(1)}, f32[384,128]{1,0:T(8,128)S(1)}, u32[]{:S(2)}, u32[]{:S(2)}) collective-permute-start(f32[384,128]{1,0:T(8,128)S(1)} %pack.1), channel_id=1, source_target_pairs={{0,28},{4,0},{8,4},{12,8},{16,12},{20,16},{24,20},{28,24},{1,29},{... | collective-permute-start | bytes 589832 | tf_op jit(solution)/shard_map/ppermute | solution.py:370
  6.5 0.7 %copy.14.refs_3_.refs_2_ = f32[2,3,4]{2,1,0:T(4,128)S(1)} copy(f32[2,3,4]{2,0,1:T(2,128)} %param.15) | data formatting | bytes 192 | tf_op args[7]
  7.2 0.8 %copy.13.refs_2_.refs_1_ = s32[12,4]{1,0:T(8,128)S(1)} copy(s32[12,4]{0,1:T(4,128)} %param.14) | data formatting | bytes 384 | tf_op args[6]
  8.0 0.0 copy-start.1
  8.0 0.9 %copy-done.1 = f32[4,128,128]{2,1,0:T(8,128)S(1)} copy-done((f32[4,128,128]{2,1,0:T(8,128)S(1)}, f32[4,128,128]{2,1,0:T(8,128)}, u32[]{:S(2)}) %copy-start.1) | copy-done | bytes 262168
  8.9 0.0 copy-start.3
  8.9 1.4 %copy-done.3 = f32[12,2,128,128]{3,2,1,0:T(8,128)S(1)} copy-done((f32[12,2,128,128]{3,2,1,0:T(8,128)S(1)}, f32[12,2,128,128]{3,2,1,0:T(8,128)}, u32[]{:S(2)}) %copy-start.3) | copy-done | bytes 1572888
  10.4 0.0 copy-start.8
  10.4 0.7 %copy-done.8 = f32[12]{0:T(128)S(1)} copy-done((f32[12]{0:T(128)S(1)}, f32[12]{0:T(128)}, u32[]{:S(2)}) %copy-start.8) | copy-done | bytes 72
  11.0 0.0 copy-start.9
  11.0 0.7 %copy-done.9 = s32[12]{0:T(128)S(1)} copy-done((s32[12]{0:T(128)S(1)}, s32[12]{0:T(128)}, u32[]{:S(2)}) %copy-start.9) | copy-done | bytes 72
  11.7 2.8 %tables.1 = (bf16[12,3,128,128]{3,2,1,0:T(8,128)(2,1)S(1)}, f32[128,128]{1,0:T(8,128)S(1)}) custom-call(f32[12]{0:T(128)S(1)} %copy-done.8, s32[12]{0:T(128)S(1)} %copy-done.9, s32[12,4]{1,0:T(8,128)S(1)} %copy.13.refs_2_.refs_1_, f32[2,3,4]{2,1,0:T(4,128)S(1)} %copy.14.refs_3_.refs_2_, f32[4,128,128]{2,1,0:T(8,128)S(1)} %copy-done.1, ...), custom_call_target="tpu_custom_call" | custom-call | flops 1000000000 | bytes 4194304 | tf_op jit(solution)/shard_map/tables/pallas_call | solution.py:372
  14.4 0.0 collective-permute-done.refs_4_.refs_5_
  14.5 0.0 copy-start.5
  14.5 0.0 copy-start.7
  14.5 6.1 %forward.1 = (f32[12,2,128,128]{3,2,1,0:T(8,128)S(1)}, f32[12,128,256]{2,1,0:T(8,128)S(1)}, f32[12,128,256]{2,1,0:T(8,128)S(1)}, f32[160,128]{1,0:T(8,128)S(1)},...) custom-call(f32[12]{0:T(128)S(1)} %copy-done.8, ...), custom_call_target="tpu_custom_call" | custom-call | tf_op jit(solution)/shard_map/forward/pallas_call | solution.py:383
  20.6 0.7 %collective-permute-start.6 = (f32[128,128]{1,0:T(8,128)S(1)}, f32[128,128]{1,0:T(8,128)S(1)}, u32[]{:S(2)}, u32[]{:S(2)}) collective-permute-start(f32[128,128]{1,0:T(8,128)S(1)} %get-tuple-element.29.refs_14_), channel_id=1, source_target_pairs={{28,31},{29,28},{30,29},{31,30}} | collective-permute-start | bytes 196616 | tf_op jit(solution)/shard_map/ppermute | solution.py:410
  21.3 1.6 %collective-permute-start.1 = (f32[160,128]{1,0:T(8,128)S(1)}, f32[160,128]{1,0:T(8,128)S(1)}, u32[]{:S(2)}, u32[]{:S(2)}) collective-permute-start(f32[160,128]{1,0:T(8,128)S(1)} %get-tuple-element.26), channel_id=1, source_target_pairs={{0,1},{1,2},{2,3},{3,0},{4,5},{5,6},{6,7},{7,4},{8,9},{9,10},{10,1... | collective-permute-start | bytes 245768 | tf_op jit(solution)/shard_map/ppermute | solution.py:408
  22.9 2.6 %collective-permute-start.2 = (f32[160,128]{1,0:T(8,128)S(1)}, f32[160,128]{1,0:T(8,128)S(1)}, u32[]{:S(2)}, u32[]{:S(2)}) collective-permute-start(f32[160,128]{1,0:T(8,128)S(1)} %get-tuple-element.27), channel_id=1, source_target_pairs={{0,2},{1,3},{2,0},{3,1},{4,6},{5,7},{6,4},{7,5},{8,10},{9,11},{10,... | collective-permute-start | bytes 245768 | tf_op jit(solution)/shard_map/ppermute | solution.py:408
  25.5 1.3 %collective-permute-start.3 = (f32[160,128]{1,0:T(8,128)S(1)}, f32[160,128]{1,0:T(8,128)S(1)}, u32[]{:S(2)}, u32[]{:S(2)}) collective-permute-start(f32[160,128]{1,0:T(8,128)S(1)} %get-tuple-element.28), channel_id=1, source_target_pairs={{0,3},{1,0},{2,1},{3,2},{4,7},{5,4},{6,5},{7,6},{8,11},{9,8},{10,9... | collective-permute-start | bytes 245768 | tf_op jit(solution)/shard_map/ppermute | solution.py:408
  26.9 0.7 %collective-permute-start.5 = (f32[128,128]{1,0:T(8,128)S(1)}, f32[128,128]{1,0:T(8,128)S(1)}, u32[]{:S(2)}, u32[]{:S(2)}) collective-permute-start(f32[128,128]{1,0:T(8,128)S(1)} %get-tuple-element.29.refs_14_), channel_id=1, source_target_pairs={{28,30},{29,31},{30,28},{31,29}} | collective-permute-start | bytes 196616 | tf_op jit(solution)/shard_map/ppermute | solution.py:410
  27.5 0.0 collective-permute-done.6.refs_17_
  27.5 0.7 %collective-permute-start.4 = (f32[128,128]{1,0:T(8,128)S(1)}, f32[128,128]{1,0:T(8,128)S(1)}, u32[]{:S(2)}, u32[]{:S(2)}) collective-permute-start(f32[128,128]{1,0:T(8,128)S(1)} %get-tuple-element.29.refs_14_), channel_id=1, source_target_pairs={{28,29},{29,30},{30,31},{31,28}} | collective-permute-start | bytes 196616 | tf_op jit(solution)/shard_map/ppermute | solution.py:410
  28.2 0.0 collective-permute-done.5.refs_16_
  28.2 0.0 collective-permute-done.4.refs_15_
  28.2 0.2 collective-permute-done.1.refs_11_
  28.4 2.2 %collective-permute-done.2.refs_12_ = f32[160,128]{1,0:T(8,128)S(1)} collective-permute-done((f32[160,128]{1,0:T(8,128)S(1)}, f32[160,128]{1,0:T(8,128)S(1)}, u32[]{:S(2)}, u32[]{:S(2)}) %collective-permute-start.2) | collective-permute-done | bytes 81952 | tf_op jit(solution)/shard_map/ppermute | solution.py:408
  30.6 0.0 collective-permute-done.3.refs_13_
  30.6 0.0 copy-done.5
  30.6 0.0 copy-done.7
  30.6 0.0 copy-start.2
  30.6 5.2 %backward.1 = (f32[4,32,128]{2,1,0:T(8,128)S(1)}, f32[4,32,128]{2,1,0:T(8,128)S(1)}, f32[4,32,128]{2,1,0:T(8,128)S(1)}, f32[4,32,128]{2,1,0:T(8,128)S(1)}, f32[32,128]{1,0:T(8,128)S(1)}) custom-call(s32[2]{0:T(128)S(1)} %copy-done.7, f32[12]{0:T(128)S(1)} %copy-done.8, s32[12,4]{1,0:T(8,128)S(1)} %copy.13.refs_2_.refs_1_, ...), custom_call_target="tpu_custom_call" | custom-call | tf_op jit(solution)/shard_map/backward/pallas_call | solution.py:412
  35.8 1.4 %collective-permute-start.8 = (f32[4,32,128]{2,1,0:T(8,128)S(1)}, f32[4,32,128]{2,1,0:T(8,128)S(1)}, u32[]{:S(2)}, u32[]{:S(2)}) collective-permute-start(f32[4,32,128]{2,1,0:T(8,128)S(1)} %get-tuple-element.32), channel_id=1, source_target_pairs={{0,1},{1,6},{2,7},{3,0},{4,5},{5,10},{6,11},{7,4},{8,9},{9,14},{10... | collective-permute-start | bytes 196616 | tf_op jit(solution)/shard_map/ppermute | solution.py:436
  37.3 2.3 %collective-permute-start.9 = (f32[4,32,128]{2,1,0:T(8,128)S(1)}, f32[4,32,128]{2,1,0:T(8,128)S(1)}, u32[]{:S(2)}, u32[]{:S(2)}) collective-permute-start(f32[4,32,128]{2,1,0:T(8,128)S(1)} %get-tuple-element.33), channel_id=1, source_target_pairs={{0,6},{1,7},{2,0},{3,1},{4,10},{5,11},{6,4},{7,5},{8,14},{9,15},{1... | collective-permute-start | bytes 196616 | tf_op jit(solution)/shard_map/ppermute | solution.py:436
  39.6 0.0 collective-permute-start.10
  39.6 0.7 %collective-permute-start.7 = (f32[4,32,128]{2,1,0:T(8,128)S(1)}, f32[4,32,128]{2,1,0:T(8,128)S(1)}, u32[]{:S(2)}, u32[]{:S(2)}) collective-permute-start(f32[4,32,128]{2,1,0:T(8,128)S(1)} %get-tuple-element.31.refs_2_), channel_id=1, source_target_pairs={{2,6},{3,7},{6,10},{7,11},{10,14},{11,15},{14,18},{15,19},{18,22},... | collective-permute-start | bytes 196616 | tf_op jit(solution)/shard_map/ppermute | solution.py:436
  40.2 2.2 %collective-permute-done.8.refs_4_ = f32[4,32,128]{2,1,0:T(8,128)S(1)} collective-permute-done((f32[4,32,128]{2,1,0:T(8,128)S(1)}, f32[4,32,128]{2,1,0:T(8,128)S(1)}, u32[]{:S(2)}, u32[]{:S(2)}) %collective-permute-start.8) | collective-permute-done | bytes 65568 | tf_op jit(solution)/shard_map/ppermute | solution.py:436
  42.4 2.0 %collective-permute-done.9.refs_5_ = f32[4,32,128]{2,1,0:T(8,128)S(1)} collective-permute-done((f32[4,32,128]{2,1,0:T(8,128)S(1)}, f32[4,32,128]{2,1,0:T(8,128)S(1)}, u32[]{:S(2)}, u32[]{:S(2)}) %collective-permute-start.9) | collective-permute-done | bytes 65568 | tf_op jit(solution)/shard_map/ppermute | solution.py:436
  44.4 0.6 collective-permute-done.10.refs_6_
  45.0 0.0 collective-permute-done.7.refs_3_
  45.0 0.0 copy-done.2
  45.0 0.1 update.1.refs_0_
  45.1 1.3 %collective-permute-start.13 = (f32[4,32,128]{2,1,0:T(8,128)S(1)}, f32[4,32,128]{2,1,0:T(8,128)S(1)}, u32[]{:S(2)}, u32[]{:S(2)}) collective-permute-start(f32[4,32,128]{2,1,0:T(8,128)S(1)} %update.1.refs_0_), channel_id=1, source_target_pairs={{3,0},{0,1},{1,2},{2,3},{7,4},{4,5},{5,6},{6,7},{11,8},{8,9},{9,10... | collective-permute-start | bytes 196616 | tf_op jit(solution)/shard_map/ppermute | solution.py:449
  46.5 12.4 %collective-permute-start.12 = (f32[4,32,128]{2,1,0:T(8,128)S(1)}, f32[4,32,128]{2,1,0:T(8,128)S(1)}, u32[]{:S(2)}, u32[]{:S(2)}) collective-permute-start(f32[4,32,128]{2,1,0:T(8,128)S(1)} %update.1.refs_0_), channel_id=1, source_target_pairs={{2,0},{3,1},{0,2},{1,3},{6,4},{7,5},{4,6},{5,7},{10,8},{11,9},{8,1... | collective-permute-start | bytes 196616 | tf_op jit(solution)/shard_map/ppermute | solution.py:449
  58.8 2.0 %collective-permute-start.11 = (f32[4,32,128]{2,1,0:T(8,128)S(1)}, f32[4,32,128]{2,1,0:T(8,128)S(1)}, u32[]{:S(2)}, u32[]{:S(2)}) collective-permute-start(f32[4,32,128]{2,1,0:T(8,128)S(1)} %update.1.refs_0_), channel_id=1, source_target_pairs={{1,0},{2,1},{3,2},{0,3},{5,4},{6,5},{7,6},{4,7},{9,8},{10,9},{11,1... | collective-permute-start | bytes 196616 | tf_op jit(solution)/shard_map/ppermute | solution.py:449
  60.9 0.0 collective-permute-done.13.refs_3_
  60.9 0.3 collective-permute-done.12.refs_2_
  61.2 1.9 %collective-permute-done.11.refs_1_ = f32[4,32,128]{2,1,0:T(8,128)S(1)} collective-permute-done((f32[4,32,128]{2,1,0:T(8,128)S(1)}, f32[4,32,128]{2,1,0:T(8,128)S(1)}, u32[]{:S(2)}, u32[]{:S(2)}) %collective-permute-start.11) | collective-permute-done | bytes 65568 | tf_op jit(solution)/shard_map/ppermute | solution.py:449
  63.1 0.8 %join.1 = f32[4,128,128]{2,1,0:T(8,128)} custom-call(f32[4,32,128]{2,1,0:T(8,128)S(1)} %update.1.refs_0_, f32[4,32,128]{2,1,0:T(8,128)S(1)} %collective-permute-done.11.refs_1_, f32[4,32,128]{2,1,0:T(8,128)S(1)} %collective-permute-done.12.refs_2_, f32[4,32,128]{2,1,0:T(8,128)S(1)} %collective-permute-done.13.refs_3_), custom_call_target="tpu_custom_call" | custom-call | tf_op jit(solution)/shard_map/join/pallas_call | solution.py:450
Async XLA Ops:
  0.0 0.9 %copy-start = (f32[4,128,128]{2,1,0:T(8,128)S(1)}, f32[4,128,128]{2,1,0:T(8,128)}, u32[]{:S(2)}) copy-start(f32[4,128,128]{2,1,0:T(8,128)} %refs_0_.7) | copy-start | bytes 786436
  1.0 0.9 %copy-start.4 = (f32[2,128,128]{2,1,0:T(8,128)S(1)}, f32[2,128,128]{2,1,0:T(8,128)}, u32[]{:S(2)}) copy-start(f32[2,128,128]{2,1,0:T(8,128)} %refs_4_.3) | copy-start | bytes 393220
  1.9 0.7 %copy-start.6 = (s32[2]{0:T(128)S(1)}, s32[2]{0:T(128)}, u32[]{:S(2)}) copy-start(s32[2]{0:T(128)} %refs_0_.6) | copy-start | bytes 28
  3.2 11.3 %collective-permute-start = (f32[384,128]{1,0:T(8,128)S(1)}, f32[384,128]{1,0:T(8,128)S(1)}, u32[]{:S(2)}, u32[]{:S(2)}) collective-permute-start(f32[384,128]{1,0:T(8,128)S(1)} %pack.1), channel_id=1, source_target_pairs={{0,28},{4,0},{8,4},{12,8},{16,12},{20,16},{24,20},{28,24},{1,29},{... | collective-permute-start | bytes 589832 | tf_op jit(solution)/shard_map/ppermute | solution.py:370
  8.0 0.9 %copy-start.1 = (f32[4,128,128]{2,1,0:T(8,128)S(1)}, f32[4,128,128]{2,1,0:T(8,128)}, u32[]{:S(2)}) copy-start(f32[4,128,128]{2,1,0:T(8,128)} %refs_0_.7) | copy-start | bytes 786436
  8.9 1.4 %copy-start.3 = (f32[12,2,128,128]{3,2,1,0:T(8,128)S(1)}, f32[12,2,128,128]{3,2,1,0:T(8,128)}, u32[]{:S(2)}) copy-start(f32[12,2,128,128]{3,2,1,0:T(8,128)} %refs_5_.3) | copy-start | bytes 4718596
  10.4 0.7 %copy-start.8 = (f32[12]{0:T(128)S(1)}, f32[12]{0:T(128)}, u32[]{:S(2)}) copy-start(f32[12]{0:T(128)} %refs_1_.4) | copy-start | bytes 148
  11.0 0.7 %copy-start.9 = (s32[12]{0:T(128)S(1)}, s32[12]{0:T(128)}, u32[]{:S(2)}) copy-start(s32[12]{0:T(128)} %refs_1_.3) | copy-start | bytes 148
  14.5 16.2 %copy-start.5 = (f32[2,128,128]{2,1,0:T(8,128)S(1)}, f32[2,128,128]{2,1,0:T(8,128)}, u32[]{:S(2)}) copy-start(f32[2,128,128]{2,1,0:T(8,128)} %refs_4_.3) | copy-start | bytes 393220
  14.5 16.2 %copy-start.7 = (s32[2]{0:T(128)S(1)}, s32[2]{0:T(128)}, u32[]{:S(2)}) copy-start(s32[2]{0:T(128)} %refs_0_.6) | copy-start | bytes 28
  20.6 6.9 %collective-permute-start.6 = (f32[128,128]{1,0:T(8,128)S(1)}, f32[128,128]{1,0:T(8,128)S(1)}, u32[]{:S(2)}, u32[]{:S(2)}) collective-permute-start(f32[128,128]{1,0:T(8,128)S(1)} %get-tuple-element.29.refs_14_), channel_id=1, source_target_pairs={{28,31},{29,28},{30,29},{31,30}} | collective-permute-start | bytes 196616 | tf_op jit(solution)/shard_map/ppermute | solution.py:410
  21.3 7.1 %collective-permute-start.1 = (f32[160,128]{1,0:T(8,128)S(1)}, f32[160,128]{1,0:T(8,128)S(1)}, u32[]{:S(2)}, u32[]{:S(2)}) collective-permute-start(f32[160,128]{1,0:T(8,128)S(1)} %get-tuple-element.26), channel_id=1, source_target_pairs={{0,1},{1,2},{2,3},{3,0},{4,5},{5,6},{6,7},{7,4},{8,9},{9,10},{10,1... | collective-permute-start | bytes 245768 | tf_op jit(solution)/shard_map/ppermute | solution.py:408
  22.9 7.7 %collective-permute-start.2 = (f32[160,128]{1,0:T(8,128)S(1)}, f32[160,128]{1,0:T(8,128)S(1)}, u32[]{:S(2)}, u32[]{:S(2)}) collective-permute-start(f32[160,128]{1,0:T(8,128)S(1)} %get-tuple-element.27), channel_id=1, source_target_pairs={{0,2},{1,3},{2,0},{3,1},{4,6},{5,7},{6,4},{7,5},{8,10},{9,11},{10,... | collective-permute-start | bytes 245768 | tf_op jit(solution)/shard_map/ppermute | solution.py:408
  25.5 5.1 %collective-permute-start.3 = (f32[160,128]{1,0:T(8,128)S(1)}, f32[160,128]{1,0:T(8,128)S(1)}, u32[]{:S(2)}, u32[]{:S(2)}) collective-permute-start(f32[160,128]{1,0:T(8,128)S(1)} %get-tuple-element.28), channel_id=1, source_target_pairs={{0,3},{1,0},{2,1},{3,2},{4,7},{5,4},{6,5},{7,6},{8,11},{9,8},{10,9... | collective-permute-start | bytes 245768 | tf_op jit(solution)/shard_map/ppermute | solution.py:408
  26.9 1.3 %collective-permute-start.5 = (f32[128,128]{1,0:T(8,128)S(1)}, f32[128,128]{1,0:T(8,128)S(1)}, u32[]{:S(2)}, u32[]{:S(2)}) collective-permute-start(f32[128,128]{1,0:T(8,128)S(1)} %get-tuple-element.29.refs_14_), channel_id=1, source_target_pairs={{28,30},{29,31},{30,28},{31,29}} | collective-permute-start | bytes 196616 | tf_op jit(solution)/shard_map/ppermute | solution.py:410
  27.5 0.7 %collective-permute-start.4 = (f32[128,128]{1,0:T(8,128)S(1)}, f32[128,128]{1,0:T(8,128)S(1)}, u32[]{:S(2)}, u32[]{:S(2)}) collective-permute-start(f32[128,128]{1,0:T(8,128)S(1)} %get-tuple-element.29.refs_14_), channel_id=1, source_target_pairs={{28,29},{29,30},{30,31},{31,28}} | collective-permute-start | bytes 196616 | tf_op jit(solution)/shard_map/ppermute | solution.py:410
  30.6 14.4 %copy-start.2 = (f32[4,128,128]{2,1,0:T(8,128)S(1)}, f32[4,128,128]{2,1,0:T(8,128)}, u32[]{:S(2)}) copy-start(f32[4,128,128]{2,1,0:T(8,128)} %refs_0_.7) | copy-start | bytes 786436
  35.8 6.6 %collective-permute-start.8 = (f32[4,32,128]{2,1,0:T(8,128)S(1)}, f32[4,32,128]{2,1,0:T(8,128)S(1)}, u32[]{:S(2)}, u32[]{:S(2)}) collective-permute-start(f32[4,32,128]{2,1,0:T(8,128)S(1)} %get-tuple-element.32), channel_id=1, source_target_pairs={{0,1},{1,6},{2,7},{3,0},{4,5},{5,10},{6,11},{7,4},{8,9},{9,14},{10... | collective-permute-start | bytes 196616 | tf_op jit(solution)/shard_map/ppermute | solution.py:436
  37.3 7.2 %collective-permute-start.9 = (f32[4,32,128]{2,1,0:T(8,128)S(1)}, f32[4,32,128]{2,1,0:T(8,128)S(1)}, u32[]{:S(2)}, u32[]{:S(2)}) collective-permute-start(f32[4,32,128]{2,1,0:T(8,128)S(1)} %get-tuple-element.33), channel_id=1, source_target_pairs={{0,6},{1,7},{2,0},{3,1},{4,10},{5,11},{6,4},{7,5},{8,14},{9,15},{1... | collective-permute-start | bytes 196616 | tf_op jit(solution)/shard_map/ppermute | solution.py:436
  39.6 5.5 %collective-permute-start.10 = (f32[4,32,128]{2,1,0:T(8,128)S(1)}, f32[4,32,128]{2,1,0:T(8,128)S(1)}, u32[]{:S(2)}, u32[]{:S(2)}) collective-permute-start(f32[4,32,128]{2,1,0:T(8,128)S(1)} %get-tuple-element.34), channel_id=1, source_target_pairs={{0,7},{1,0},{2,1},{3,6},{4,11},{5,4},{6,5},{7,10},{8,15},{9,8},{10... | collective-permute-start | bytes 196616 | tf_op jit(solution)/shard_map/ppermute | solution.py:436
  39.6 5.5 %collective-permute-start.7 = (f32[4,32,128]{2,1,0:T(8,128)S(1)}, f32[4,32,128]{2,1,0:T(8,128)S(1)}, u32[]{:S(2)}, u32[]{:S(2)}) collective-permute-start(f32[4,32,128]{2,1,0:T(8,128)S(1)} %get-tuple-element.31.refs_2_), channel_id=1, source_target_pairs={{2,6},{3,7},{6,10},{7,11},{10,14},{11,15},{14,18},{15,19},{18,22},... | collective-permute-start | bytes 196616 | tf_op jit(solution)/shard_map/ppermute | solution.py:436
  45.1 15.7 %collective-permute-start.13 = (f32[4,32,128]{2,1,0:T(8,128)S(1)}, f32[4,32,128]{2,1,0:T(8,128)S(1)}, u32[]{:S(2)}, u32[]{:S(2)}) collective-permute-start(f32[4,32,128]{2,1,0:T(8,128)S(1)} %update.1.refs_0_), channel_id=1, source_target_pairs={{3,0},{0,1},{1,2},{2,3},{7,4},{4,5},{5,6},{6,7},{11,8},{8,9},{9,10... | collective-permute-start | bytes 196616 | tf_op jit(solution)/shard_map/ppermute | solution.py:449
  46.5 14.8 %collective-permute-start.12 = (f32[4,32,128]{2,1,0:T(8,128)S(1)}, f32[4,32,128]{2,1,0:T(8,128)S(1)}, u32[]{:S(2)}, u32[]{:S(2)}) collective-permute-start(f32[4,32,128]{2,1,0:T(8,128)S(1)} %update.1.refs_0_), channel_id=1, source_target_pairs={{2,0},{3,1},{0,2},{1,3},{6,4},{7,5},{4,6},{5,7},{10,8},{11,9},{8,1... | collective-permute-start | bytes 196616 | tf_op jit(solution)/shard_map/ppermute | solution.py:449
  58.8 4.3 %collective-permute-start.11 = (f32[4,32,128]{2,1,0:T(8,128)S(1)}, f32[4,32,128]{2,1,0:T(8,128)S(1)}, u32[]{:S(2)}, u32[]{:S(2)}) collective-permute-start(f32[4,32,128]{2,1,0:T(8,128)S(1)} %update.1.refs_0_), channel_id=1, source_target_pairs={{1,0},{2,1},{3,2},{0,3},{5,4},{6,5},{7,6},{4,7},{9,8},{10,9},{11,1... | collective-permute-start | bytes 196616 | tf_op jit(solution)/shard_map/ppermute | solution.py:449

commit v2 on v1

v2 whole, which is shorter than its diff:
```python
import math

import jax
import jax.numpy as jnp
import numpy as np
from jax import lax
from jax.experimental import pallas as pl
from jax.experimental.pallas import tpu as pltpu
from jax.sharding import PartitionSpec as P

WAVES = 48

relax = 4.0
floor_level = 1.0

UNROLL = 4
EDGE_UNROLL = 2

VM = pl.BlockSpec(memory_space=pltpu.VMEM)
ANY = pl.BlockSpec(memory_space=pltpu.HBM)
f32 = jnp.float32
bf16 = jnp.bfloat16


def fit(parity, degree):
    nodes = 0.5 * np.cos(np.pi * (np.arange(400) + 0.5) / 800)
    turns = 2 * np.pi * nodes
    value = np.sin(turns) if parity else np.cos(turns)
    powers = np.stack([nodes ** (parity + 2 * i) for i in range(degree)], axis=1)
    return [float(c) for c in np.linalg.lstsq(powers, value, rcond=None)[0]]


SIN = fit(1, 6)
COS = fit(0, 7)


def horner(square, coefs):
    total = coefs[-1]
    for c in coefs[-2::-1]:
        total = total * square + c
    return total


def cos_sin(turns):
    r = turns - jnp.round(turns)
    square = r * r
    return horner(square, COS), horner(square, SIN) * r


def lanes(rows, length):
    return lax.broadcasted_iota(jnp.int32, (rows, length), 1)


def halves_packed(top, bottom, upper):
    length = top.shape[-1]
    half = length // 2
    low = lanes(top.shape[0], length) < half
    if upper:
        return jnp.where(low, pltpu.roll(top, half, 1), bottom)
    return jnp.where(low, top, pltpu.roll(bottom, half, 1))


def block(table_ref, s, kind):
    re, im, neg = table_ref[s, 0], table_ref[s, 1], table_ref[s, 2]
    top, bottom = ((re, neg), (im, re)) if kind == "L" else ((re, im), (neg, re))
    return jnp.concatenate(
        [jnp.concatenate(top, axis=1), jnp.concatenate(bottom, axis=1)], axis=0
    )


def pack_kernel(offsets_any, maps_any, measured_any, out, right_root, offsets, maps, measured, sems):
    copies = [
        pltpu.make_async_copy(source, target, sems.at[i])
        for i, (source, target) in enumerate(
            ((offsets_any, offsets), (maps_any, maps), (measured_any, measured))
        )
    ]
    for copy in copies:
        copy.start()
    materials, length, _ = maps.shape
    half = length // 2
    copies[1].wait()
    for m in range(materials):
        out[m * half : (m + 1) * half] = halves_packed(maps[m, :half], maps[m, half:], False)
    copies[0].wait()
    copies[2].wait()
    left_first = offsets[0] < offsets[1]
    first, second = jnp.sqrt(measured[0]), jnp.sqrt(measured[1])
    out[materials * half :] = jnp.where(left_first, first, second)
    right_root[...] = jnp.where(left_first, second, first)


def piece(array, q, count, half_rows):
    groups = count // 2
    rows = 2 * half_rows
    start = pl.multiple_of(lax.rem(q, groups) * rows, half_rows)
    top = array[pl.ds(start, half_rows), :]
    bottom = array[pl.ds(start + half_rows, half_rows), :]
    return jnp.where(
        q < groups, halves_packed(top, bottom, False), halves_packed(top, bottom, True)
    )


def first_kernel(
    tiles, count, spectrum_any, wave_any, edge_any, band_any, maps_any, probe_any,
    table, coef, probe, own, here, power,
    spectrum, wave_index, edge_band, band_coef, maps, sems,
):
    copies = [
        pltpu.make_async_copy(source, target, sems.at[i])
        for i, (source, target) in enumerate(
            (
                (wave_any, wave_index),
                (edge_any, edge_band),
                (band_any, band_coef),
                (spectrum_any, spectrum),
                (maps_any, maps),
                (probe_any, probe),
            )
        )
    ]
    for copy in copies:
        copy.start()
    materials, length, _ = maps.shape
    half = length // 2
    slots = probe.shape[0]
    tile = lax.axis_index("tile")
    me = lax.axis_index("wave")
    group = 8
    centred_lane = (lanes(group, length) - half).astype(f32)
    row = lax.broadcasted_iota(jnp.int32, (group, length), 0)
    fine = row.astype(f32) * centred_lane / length
    normaliser = 1.0 / math.sqrt(length)
    coarse_rows = length // group
    copies[0].wait()

    def tables(s, carry):
        which = jnp.full((group, length), wave_index[s], jnp.int32).astype(f32)
        sampling = 0.6 + 0.4 * which / (WAVES - 1)
        fine_cos, fine_sin = cos_sin(sampling * fine)
        fine_cos, fine_sin = fine_cos * normaliser, fine_sin * normaliser
        for base in range(0, coarse_rows, group):
            step = ((row + base) * group - half).astype(f32) * centred_lane / length
            cos, sin = cos_sin(sampling * step)
            for i in range(0, group, 2):
                parts = []
                for j in (i, i + 1):
                    c = jnp.broadcast_to(cos[j : j + 1], (group, length))
                    n = jnp.broadcast_to(sin[j : j + 1], (group, length))
                    parts.append((c * fine_cos - n * fine_sin, n * fine_cos + c * fine_sin))
                at = pl.ds((base + i) * group, 2 * group)
                re = jnp.concatenate([parts[0][0], parts[1][0]], axis=0).astype(bf16)
                positive = jnp.concatenate([parts[0][1], parts[1][1]], axis=0)
                table[s, 0, at, :] = re
                table[s, 1, at, :] = (-positive).astype(bf16)
                table[s, 2, at, :] = positive.astype(bf16)
        return carry

    lax.fori_loop(0, slots, tables, 0, unroll=2)

    for copy in copies[1:]:
        copy.wait()
    for s in range(slots):
        for m in range(materials):
            band = edge_band[m, s]
            a, b = band_coef[band, 0, m], band_coef[band, 1, m]
            coef[s, m, :] = jnp.full((length,), a * (-math.log2(math.e)), f32)
            coef[s, materials + m, :] = jnp.full((length,), b * (0.5 / math.pi), f32)
            coef[s, 2 * materials + m, :] = jnp.full((length,), a, f32)
            coef[s, 3 * materials + m, :] = jnp.full((length,), b, f32)
        coef[s, 4 * materials, :] = jnp.full((length,), spectrum[s], f32)
    for m in range(materials):
        own[m] = pltpu.roll(maps[m], half, 1)
    chunk = 32
    low = lanes(chunk, length) < half
    frames = jnp.where(
        low,
        jnp.where(tile == tiles - 1, 1.0, 2.0),
        jnp.where(tile == 0, 1.0, 2.0),
    )
    for start in range(0, length, chunk):
        at = slice(start, start + chunk)
        window = [own[m, at] for m in range(materials)]

        def add(s, total):
            absorb = None
            for m in range(materials):
                term = coef[s, m : m + 1] * window[m]
                absorb = term if absorb is None else absorb + term
            re, im = probe[s, 0, at], probe[s, 1, at]
            weight = coef[s, 4 * materials : 4 * materials + 1]
            return total + (weight * jnp.exp2(absorb + absorb)) * (re * re + im * im)

        total = lax.fori_loop(0, slots, add, jnp.zeros((chunk, length), f32), unroll=4)
        power[at] = frames * total
    half_rows = length // count
    for m in range(materials):
        here[m] = piece(own.at[m], me, count, half_rows)


CHUNK = 32


def transform(left, right, fields):
    length = fields[0][0].shape[0]
    stacked = jnp.concatenate(
        [jnp.concatenate([re.astype(bf16), im.astype(bf16)], axis=0) for re, im in fields], axis=1
    )
    mid = jnp.dot(left, stacked, preferred_element_type=f32).astype(bf16)
    beside = jnp.concatenate(
        [
            jnp.concatenate(
                [mid[:length, i * length : (i + 1) * length], mid[length:, i * length : (i + 1) * length]], axis=1
            )
            for i in range(len(fields))
        ],
        axis=0,
    )
    return jnp.dot(beside, right, preferred_element_type=f32)


def forward_kernel(
    tiles, count, own, halo, probe, table, coef, power,
    psi, far, *messages_and_scratch,
):
    messages = messages_and_scratch[:count]
    window, total = messages_and_scratch[count:]
    materials, length, _ = own.shape
    half = length // 2
    slots = probe.shape[0]
    edge = lax.axis_index("tile") == tiles - 1
    me = lax.axis_index("wave")
    low = lanes(half, length) < half
    for m in range(materials):
        packed = halo[m * half : (m + 1) * half]
        window[m, :half] = jnp.where(low, own[m, :half], pltpu.roll(packed, half, 1))
        window[m, half:] = jnp.where(low, own[m, half:], packed)
    total[...] = jnp.zeros_like(total)

    def exit_wave(s):
        for start in range(0, length, CHUNK):
            at = slice(start, start + CHUNK)
            absorb, phase = None, None
            for m in range(materials):
                w = window[m, at]
                a = coef[s, m : m + 1] * w
                b = coef[s, materials + m : materials + m + 1] * w
                absorb = a if absorb is None else absorb + a
                phase = b if phase is None else phase + b
            damping = jnp.exp2(absorb)
            cos, sin = cos_sin(phase)
            cos, sin = damping * cos, damping * sin
            re, im = probe[s, 0, at], probe[s, 1, at]
            psi[s, 0, at] = re * cos - im * sin
            psi[s, 1, at] = re * sin + im * cos

    def add_intensity(s, got, at):
        re, im = got[:, :length], got[:, length:]
        total[at : at + length] += coef[s, 4 * materials : 4 * materials + 1] * (re * re + im * im)

    @pl.when(jnp.logical_not(edge))
    def _():
        def step(s, carry):
            exit_wave(s)
            got = transform(block(table, s, "L"), block(table, s, "R"), [(psi[s, 0], psi[s, 1])])
            far[s, :length] = got
            add_intensity(s, got, 0)
            return carry

        lax.fori_loop(0, slots, step, 0, unroll=UNROLL)

    @pl.when(edge)
    def _():
        low = lanes(length, length) < half

        def step(s, carry):
            exit_wave(s)
            re, im, bare_re, bare_im = psi[s, 0], psi[s, 1], probe[s, 0], probe[s, 1]
            got = transform(
                block(table, s, "L"),
                block(table, s, "R"),
                [
                    (jnp.where(low, re, bare_re), jnp.where(low, im, bare_im)),
                    (jnp.where(low, bare_re, re), jnp.where(low, bare_im, im)),
                ],
            )
            far[s] = got
            add_intensity(s, got[:length], 0)
            add_intensity(s, got[length:], length)
            return carry

        lax.fori_loop(0, slots, step, 0, unroll=EDGE_UNROLL)

    half_rows = length // count
    for k, message in enumerate(messages):
        message[: 2 * length] = total[...]
        message[2 * length :] = piece(power, jnp.bitwise_xor(me, k), count, half_rows)


def backward_kernel(tiles, count, right_root, halo, table, coef, psi, far, *rest):
    shares, rest = rest[:count], rest[count:]
    sends, rest = rest[:count], rest[count:]
    scale, shortfall, gradient, back = rest
    length = right_root.shape[0]
    materials = gradient.shape[0]
    half = length // 2
    slots = psi.shape[0]
    edge = lax.axis_index("tile") == tiles - 1
    me = lax.axis_index("wave")
    half_rows = length // count
    powers = shares[0][2 * length :]
    for share in shares[1:]:
        powers = powers + share[2 * length :]
    scale[...] = relax / (powers + 1.0)
    gradient[...] = jnp.zeros_like(gradient)

    def inverse(at):
        intensity = shares[0][at : at + length]
        for share in shares[1:]:
            intensity = intensity + share[at : at + length]
        return lax.rsqrt(jnp.maximum(intensity, floor_level))

    left_root = halo.at[materials * half :]

    def delta(s, at):
        factor = coef[s, 4 * materials : 4 * materials + 1] * shortfall[at : at + length]
        return factor * far[s, at : at + length, :length], factor * far[s, at : at + length, length:]

    def collect(s):
        for start in range(0, length, CHUNK):
            at = slice(start, start + CHUNK)
            re, im = psi[s, 0, at], psi[s, 1, at]
            back_re, back_im = back[at, :length], back[at, length:]
            cross_re = re * back_re + im * back_im
            cross_im = re * back_im - im * back_re
            for m in range(materials):
                a = coef[s, 2 * materials + m : 2 * materials + m + 1]
                b = coef[s, 3 * materials + m : 3 * materials + m + 1]
                gradient[m, at] += b * cross_im - a * cross_re

    @pl.when(jnp.logical_not(edge))
    def _():
        shortfall[:length] = (right_root[...] + left_root[...]) * inverse(0) - 2.0

        def step(s, carry):
            back[...] = transform(block(table, s, "R"), block(table, s, "L"), [delta(s, 0)])
            collect(s)
            return carry

        lax.fori_loop(0, slots, step, 0, unroll=UNROLL)

    @pl.when(edge)
    def _():
        shortfall[:length] = right_root[...] * inverse(0) - 1.0
        shortfall[length:] = left_root[...] * inverse(length) - 1.0
        low = (lax.broadcasted_iota(jnp.int32, (length, 2 * length), 1) & (length - 1)) < half

        def step(s, carry):
            both = transform(
                block(table, s, "R"), block(table, s, "L"), [delta(s, 0), delta(s, length)]
            )
            back[...] = jnp.where(low, both[:length], both[length:])
            collect(s)
            return carry

        lax.fori_loop(0, slots, step, 0, unroll=EDGE_UNROLL)

    for k, send in enumerate(sends):
        for m in range(materials):
            send[m] = piece(gradient.at[m], jnp.bitwise_xor(me, k), count, half_rows)


def update_kernel(count, here, scale, *refs):
    own, arrived, out = refs[0], refs[1:-1], refs[-1]
    me = lax.axis_index("wave")
    for m in range(here.shape[0]):
        total = jnp.where(me < count // 2, own[m], arrived[0][m])
        for other in arrived[1:]:
            total = total + other[m]
        out[m] = here[m] + scale[...] * total


def join_kernel(count, *refs):
    shares, out = refs[:count], refs[count]
    materials, length, _ = out.shape
    half = length // 2
    me = lax.axis_index("wave")
    half_rows = length // count
    groups = count // 2
    low = lanes(half_rows, length) < half
    for position in range(count):

        @pl.when(me == position)
        def _():
            held = lambda q: shares[q ^ position]
            for g in range(groups):
                right, left = held(g), held(g + groups)
                start = g * 2 * half_rows
                for m in range(materials):
                    r, l = right[m], left[m]
                    out[m, start : start + half_rows] = jnp.where(low, l, pltpu.roll(r, half, 1))
                    out[m, start + half_rows : start + 2 * half_rows] = jnp.where(
                        low, pltpu.roll(l, half, 1), r
                    )


def in_hbm(array):
    return pltpu.with_memory_space_constraint(array, pltpu.HBM)


def params(mib=40):
    return pltpu.CompilerParams(vmem_limit_bytes=mib * 2**20)


def per_device(tiles, count, maps, measured, offsets, probe, spectrum, wave_index, edge_band, band_coef):
    materials, length, columns = maps.shape
    slots = probe.shape[0]
    half = length // 2
    shape = jax.ShapeDtypeStruct
    half_rows = length // count
    square = shape((length, length), f32)
    share = shape((materials, half_rows, length), f32)

    packed, right_root = pl.pallas_call(
        pack_kernel,
        out_shape=(shape((materials * half + length, length), f32), square),
        in_specs=[ANY] * 3,
        out_specs=(VM, VM),
        scratch_shapes=[
            pltpu.SMEM(offsets.shape, jnp.int32),
            pltpu.VMEM(maps.shape, f32),
            pltpu.VMEM(measured.shape, f32),
            pltpu.SemaphoreType.DMA((3,)),
        ],
        compiler_params=params(),
        name="pack",
    )(*map(in_hbm, (offsets, maps, measured)))
    halo = lax.ppermute(packed, "tile", [(i, (i - 1) % tiles) for i in range(tiles)])

    band_first = jnp.transpose(band_coef, (1, 0, 2))
    table, coef, near_probe, own, here, power = pl.pallas_call(
        lambda *refs: first_kernel(tiles, count, *refs),
        out_shape=(
            shape((slots, 3, length, length), bf16),
            shape((slots, 6 * materials, length), f32),
            shape(probe.shape, f32),
            shape(maps.shape, f32),
            share,
            square,
        ),
        in_specs=[ANY] * 6,
        out_specs=(VM,) * 6,
        scratch_shapes=[
            pltpu.SMEM(spectrum.shape, f32),
            pltpu.SMEM(wave_index.shape, jnp.int32),
            pltpu.SMEM(edge_band.shape[::-1], jnp.int32),
            pltpu.SMEM(band_first.shape, f32),
            pltpu.VMEM(maps.shape, f32),
            pltpu.SemaphoreType.DMA((6,)),
        ],
        compiler_params=params(),
        cost_estimate=pl.CostEstimate(flops=10**9, bytes_accessed=2**22, transcendentals=0),
        name="tables",
    )(*map(in_hbm, (spectrum, wave_index, edge_band.T, band_first, maps, probe)))

    message = shape((2 * length + half_rows, length), f32)
    psi, far, *messages = pl.pallas_call(
        lambda *refs: forward_kernel(tiles, count, *refs),
        out_shape=(
            shape((slots, 2, length, length), f32),
            shape((slots, 2 * length, 2 * length), f32),
        )
        + (message,) * count,
        in_specs=[VM] * 6,
        out_specs=(VM,) * (2 + count),
        scratch_shapes=[
            pltpu.VMEM((materials, length, length), f32),
            pltpu.VMEM((2 * length, length), f32),
        ],
        compiler_params=params(),
        name="forward",
    )(own, halo, near_probe, table, coef, power)

    shares = [messages[0]]
    for k in range(1, count):
        shares.append(lax.ppermute(messages[k], "wave", [(w, w ^ k) for w in range(count)]))

    *sends, scale = pl.pallas_call(
        lambda *refs: backward_kernel(tiles, count, *refs),
        out_shape=(share,) * count + (shape((half_rows, length), f32),),
        in_specs=[VM] * (6 + count),
        out_specs=(VM,) * (count + 1),
        scratch_shapes=[
            pltpu.VMEM((2 * length, length), f32),
            pltpu.VMEM((materials, length, length), f32),
            pltpu.VMEM((length, 2 * length), f32),
        ],
        compiler_params=params(),
        name="backward",
    )(right_root, halo, table, coef, psi, far, *shares)

    def owner(t, q):
        return (t + (q >= count // 2)) % tiles * count + q

    arrived = []
    for k in range(count):
        pairs = [(t * count + w, owner(t, w ^ k)) for t in range(tiles) for w in range(count)]
        arrived.append(lax.ppermute(sends[k], ("tile", "wave"), [p for p in pairs if p[0] != p[1]]))

    new = pl.pallas_call(
        lambda *refs: update_kernel(count, *refs),
        out_shape=share,
        in_specs=[VM] * (3 + count),
        out_specs=VM,
        compiler_params=params(),
        name="update",
    )(here, scale, sends[0], *arrived)

    parts = [new]
    for k in range(1, count):
        parts.append(lax.ppermute(new, "wave", [(w, w ^ k) for w in range(count)]))
    return pl.pallas_call(
        lambda *refs: join_kernel(count, *refs),
        out_shape=shape((materials, length, length), f32),
        in_specs=[VM] * count,
        out_specs=VM,
        compiler_params=params(),
        name="join",
    )(*parts)


def solution(mesh):
    in_specs = (
        P(None, None, "tile"),
        P("tile", None, None),
        P("tile"),
        P("wave", None, None, None),
        P("wave"),
        P("wave"),
        P("wave", None),
        P(),
    )
    out_specs = P(None, None, "tile")
    tiles, count = mesh.shape["tile"], mesh.shape["wave"]
    return jax.shard_map(
        lambda *args: per_device(tiles, count, *args),
        mesh=mesh,
        in_specs=in_specs,
        out_specs=out_specs,
        check_vma=False,
    )
```

time: 64.3 us -> 49.9 us (0.78)
  starting transfers between devices: 31 us -> 16.8 us
  waiting for transfers between devices: 9.44 us -> 22.3 us
  local copies, waits for them, and re-layouts: 7.65 us -> 0 us
  Pallas kernels: 15.7 us -> 10.6 us
    ppermute x13 -> x10, starting transfers between devices: 27.6 us -> 13.4 us  [the longest x4 4.49 us: per_device(): lax.ppermute(sends[k], ('tile', 'wave'), [p for p in pairs if p[0] != p[1]])]
    ppermute x13 -> x10, waiting for transfers between devices: 9.43 us -> 21.4 us  [the longest x3 11.2 us: per_device(): lax.ppermute(messages[k], 'wave', [(w, w ^ k) for w in range(count)])]
    unnamed x22 -> x0, local copies, waits for them, and re-layouts: 7.65 us -> none
    pallas_call x1, Pallas kernels: 6.13 us -> 3.34 us  [per_device(): pl.pallas_call(lambda *refs: forward_kernel(tiles, count, *refs), out_sha...]
    pallas_call x1, Pallas kernels: 5.19 us -> 2.99 us  [per_device(): pl.pallas_call(lambda *refs: backward_kernel(tiles, count, *refs), out_sh...]
    ppermute x1, waiting for transfers between devices: 0.01 us -> 0.94 us  [per_device(): lax.ppermute(packed, 'tile', [(i, (i - 1) % tiles) for i in range(tiles)])]
  transfers between devices with their start and end apart: 14 -> 11, of which waited for: 7 -> 7; matrix products, arithmetic and copies ran while one was open for 2% -> 0% of each run, Pallas kernels for 4% -> 5%
where the time goes in v2:
time: 49.9 us; the launch traced here: 49.7 us
  waiting for transfers between devices  22.3 us (45%)
  starting transfers between devices  16.8 us (34%)
  Pallas kernels  10.6 us (21%)
    ppermute x3, waiting for transfers between devices, per_device(): lax.ppermute(messages[k], 'wave', [(w, w ^ k) for w in range(count)])  11.2 us
    ppermute x4, waiting for transfers between devices, per_device(): lax.ppermute(sends[k], ('tile', 'wave'), [p for p in pairs if p[0] != p[1]])  6.03 us
    ppermute x4, starting transfers between devices, per_device(): lax.ppermute(sends[k], ('tile', 'wave'), [p for p in pairs if p[0] != p[1]])  4.49 us
    ppermute x3, starting transfers between devices, per_device(): parts.append(lax.ppermute(new, 'wave', [(w, w ^ k) for w in range(count)]))  4.45 us
    ppermute x3, starting transfers between devices, per_device(): lax.ppermute(messages[k], 'wave', [(w, w ^ k) for w in range(count)])  4.45 us
    ppermute x3, waiting for transfers between devices, per_device(): parts.append(lax.ppermute(new, 'wave', [(w, w ^ k) for w in range(count)]))  4.14 us
    ppermute x1, starting transfers between devices, per_device(): lax.ppermute(packed, 'tile', [(i, (i - 1) % tiles) for i in range(tiles)])  3.39 us
    pallas_call x1, Pallas kernels, per_device(): pl.pallas_call(lambda *refs: forward_kernel(tiles, count, *refs), out_sha...  3.34 us
  transfers between devices with their start and end apart: 11, of which 7 were waited for; matrix products, arithmetic and copies ran while one was open for 0% of the time, Pallas kernels for 5%

profile of v2, /device:TPU:0, one launch (start us, length us, event | category | flops | bytes accessed | tf_op | source)
XLA Modules:
  0.0 49.7 jit_solution(16023781669045920602)
XLA Ops:
  0.0 1.1 %pack.1 = (f32[384,128]{1,0:T(8,128)S(1)}, f32[128,128]{1,0:T(8,128)S(1)}) custom-call(s32[2]{0:T(128)} %offsets_any.1, f32[4,128,128]{2,1,0:T(8,128)} %maps_any.1, f32[2,128,128]{2,1,0:T(8,128)} %measured_any.1), custom_call_target="tpu_custom_call" | custom-call | tf_op jit(solution)/shard_map/pack/pallas_call | solution.py:424
  1.1 3.4 %collective-permute-start = (f32[384,128]{1,0:T(8,128)S(1)}, f32[384,128]{1,0:T(8,128)S(1)}, u32[]{:S(2)}, u32[]{:S(2)}) collective-permute-start(f32[384,128]{1,0:T(8,128)S(1)} %get-tuple-element.26), channel_id=1, source_target_pairs={{0,28},{4,0},{8,4},{12,8},{16,12},{20,16},{24,20},{28,24},{1,29},{... | collective-permute-start | bytes 589832 | tf_op jit(solution)/shard_map/ppermute | solution.py:438
  4.5 2.2 %tables.1 = (bf16[12,3,128,128]{3,2,1,0:T(8,128)(2,1)S(1)}, f32[12,24,128]{2,1,0:T(8,128)S(1)}, f32[12,2,128,128]{3,2,1,0:T(8,128)S(1)}, f32[4,128,128]{2,1,0:T(...) custom-call(f32[12]{0:T(128)} %refs_0_.1, s32[12]{0:T(128)} %refs_1_.1, s32[4,12]{1,0:T(4,128)} %bitcast.3, ...), custom_call_target="tpu_custom_call" | custom-call | flops 1000000000 | bytes 4194304 | tf_op jit(solution)/shard_map/tables/pallas_call | solution.py:441
  6.8 0.9 %collective-permute-done.refs_1_ = f32[384,128]{1,0:T(8,128)S(1)} collective-permute-done((f32[384,128]{1,0:T(8,128)S(1)}, f32[384,128]{1,0:T(8,128)S(1)}, u32[]{:S(2)}, u32[]{:S(2)}) %collective-permute-start) | collective-permute-done | bytes 196640 | tf_op jit(solution)/shard_map/ppermute | solution.py:438
  7.7 3.3 %forward.1 = (f32[12,2,128,128]{3,2,1,0:T(8,128)S(1)}, f32[12,256,256]{2,1,0:T(8,128)S(1)}, f32[288,128]{1,0:T(8,128)S(1)}, f32[288,128]{1,0:T(8,128)S(1)}, f32[...) custom-call(f32[4,128,128]{2,1,0:T(8,128)S(1)} %get-tuple-element.29.refs_0_, f32[384,128]{1,0:T(8,128)S(1)} %collective-permute-done.refs_1_, ...), custom_call_target="tpu_custom_call" | custom-call | tf_op jit(solution)/shard_map/forward/pallas_call | solution.py:467
  11.1 1.6 %collective-permute-start.1 = (f32[288,128]{1,0:T(8,128)S(1)}, f32[288,128]{1,0:T(8,128)S(1)}, u32[]{:S(2)}, u32[]{:S(2)}) collective-permute-start(f32[288,128]{1,0:T(8,128)S(1)} %get-tuple-element.35), channel_id=1, source_target_pairs={{0,1},{1,0},{2,3},{3,2},{4,5},{5,4},{6,7},{7,6},{8,9},{9,8},{10,11... | collective-permute-start | bytes 442376 | tf_op jit(solution)/shard_map/ppermute | solution.py:486
  12.7 2.6 %collective-permute-start.2 = (f32[288,128]{1,0:T(8,128)S(1)}, f32[288,128]{1,0:T(8,128)S(1)}, u32[]{:S(2)}, u32[]{:S(2)}) collective-permute-start(f32[288,128]{1,0:T(8,128)S(1)} %get-tuple-element.36), channel_id=1, source_target_pairs={{0,2},{1,3},{2,0},{3,1},{4,6},{5,7},{6,4},{7,5},{8,10},{9,11},{10,... | collective-permute-start | bytes 442376 | tf_op jit(solution)/shard_map/ppermute | solution.py:486
  15.3 0.2 collective-permute-start.3
  15.5 3.4 %collective-permute-done.1.refs_7_ = f32[288,128]{1,0:T(8,128)S(1)} collective-permute-done((f32[288,128]{1,0:T(8,128)S(1)}, f32[288,128]{1,0:T(8,128)S(1)}, u32[]{:S(2)}, u32[]{:S(2)}) %collective-permute-start.1) | collective-permute-done | bytes 147488 | tf_op jit(solution)/shard_map/ppermute | solution.py:486
  18.9 7.8 %collective-permute-done.2.refs_8_ = f32[288,128]{1,0:T(8,128)S(1)} collective-permute-done((f32[288,128]{1,0:T(8,128)S(1)}, f32[288,128]{1,0:T(8,128)S(1)}, u32[]{:S(2)}, u32[]{:S(2)}) %collective-permute-start.2) | collective-permute-done | bytes 147488 | tf_op jit(solution)/shard_map/ppermute | solution.py:486
  26.7 0.0 collective-permute-done.3.refs_9_
  26.7 3.0 %backward.1 = (f32[4,32,128]{2,1,0:T(8,128)S(1)}, f32[4,32,128]{2,1,0:T(8,128)S(1)}, f32[4,32,128]{2,1,0:T(8,128)S(1)}, f32[4,32,128]{2,1,0:T(8,128)S(1)}, f32[32,128]{1,0:T(8,128)S(1)}) custom-call(f32[128,128]{1,0:T(8,128)S(1)} %get-tuple-element.25.refs_0_, f32[384,128]{1,0:T(8,128)S(1)} %collective-permute-done.refs_1_, ...), custom_call_target="tpu_custom_call" | custom-call | tf_op jit(solution)/shard_map/backward/pallas_call | solution.py:488
  29.7 2.4 %collective-permute-start.5 = (f32[4,32,128]{2,1,0:T(8,128)S(1)}, f32[4,32,128]{2,1,0:T(8,128)S(1)}, u32[]{:S(2)}, u32[]{:S(2)}) collective-permute-start(f32[4,32,128]{2,1,0:T(8,128)S(1)} %get-tuple-element.40), channel_id=1, source_target_pairs={{0,1},{1,0},{2,7},{3,6},{4,5},{5,4},{6,11},{7,10},{8,9},{9,8},{10,... | collective-permute-start | bytes 196616 | tf_op jit(solution)/shard_map/ppermute | solution.py:508
  32.1 0.0 collective-permute-start.6
  32.1 1.4 %collective-permute-start.7 = (f32[4,32,128]{2,1,0:T(8,128)S(1)}, f32[4,32,128]{2,1,0:T(8,128)S(1)}, u32[]{:S(2)}, u32[]{:S(2)}) collective-permute-start(f32[4,32,128]{2,1,0:T(8,128)S(1)} %get-tuple-element.42), channel_id=1, source_target_pairs={{0,7},{1,6},{2,1},{3,0},{4,11},{5,10},{6,5},{7,4},{8,15},{9,14},{1... | collective-permute-start | bytes 196616 | tf_op jit(solution)/shard_map/ppermute | solution.py:508
  33.5 0.7 %collective-permute-start.4 = (f32[4,32,128]{2,1,0:T(8,128)S(1)}, f32[4,32,128]{2,1,0:T(8,128)S(1)}, u32[]{:S(2)}, u32[]{:S(2)}) collective-permute-start(f32[4,32,128]{2,1,0:T(8,128)S(1)} %get-tuple-element.39.refs_2_), channel_id=1, source_target_pairs={{2,6},{3,7},{6,10},{7,11},{10,14},{11,15},{14,18},{15,19},{18,22},... | collective-permute-start | bytes 196616 | tf_op jit(solution)/shard_map/ppermute | solution.py:508
  34.2 0.8 %collective-permute-done.5.refs_4_ = f32[4,32,128]{2,1,0:T(8,128)S(1)} collective-permute-done((f32[4,32,128]{2,1,0:T(8,128)S(1)}, f32[4,32,128]{2,1,0:T(8,128)S(1)}, u32[]{:S(2)}, u32[]{:S(2)}) %collective-permute-start.5) | collective-permute-done | bytes 65568 | tf_op jit(solution)/shard_map/ppermute | solution.py:508
  35.0 5.2 %collective-permute-done.6.refs_5_ = f32[4,32,128]{2,1,0:T(8,128)S(1)} collective-permute-done((f32[4,32,128]{2,1,0:T(8,128)S(1)}, f32[4,32,128]{2,1,0:T(8,128)S(1)}, u32[]{:S(2)}, u32[]{:S(2)}) %collective-permute-start.6) | collective-permute-done | bytes 65568 | tf_op jit(solution)/shard_map/ppermute | solution.py:508
  40.2 0.0 collective-permute-done.7.refs_6_
  40.2 0.0 collective-permute-done.4.refs_3_
  40.3 2.6 %collective-permute-start.10 = (f32[4,32,128]{2,1,0:T(8,128)S(1)}, f32[4,32,128]{2,1,0:T(8,128)S(1)}, u32[]{:S(2)}, u32[]{:S(2)}) collective-permute-start(f32[4,32,128]{2,1,0:T(8,128)S(1)} %update.1.refs_0_), channel_id=1, source_target_pairs={{0,3},{1,2},{2,1},{3,0},{4,7},{5,6},{6,5},{7,4},{8,11},{9,10},{10,... | collective-permute-start | bytes 196616 | tf_op jit(solution)/shard_map/ppermute | solution.py:521
  42.9 0.2 collective-permute-start.9
  43.1 1.6 %collective-permute-start.8 = (f32[4,32,128]{2,1,0:T(8,128)S(1)}, f32[4,32,128]{2,1,0:T(8,128)S(1)}, u32[]{:S(2)}, u32[]{:S(2)}) collective-permute-start(f32[4,32,128]{2,1,0:T(8,128)S(1)} %update.1.refs_0_), channel_id=1, source_target_pairs={{0,1},{1,0},{2,3},{3,2},{4,5},{5,4},{6,7},{7,6},{8,9},{9,8},{10,11... | collective-permute-start | bytes 196616 | tf_op jit(solution)/shard_map/ppermute | solution.py:521
  44.7 2.4 %collective-permute-done.10.refs_3_ = f32[4,32,128]{2,1,0:T(8,128)S(1)} collective-permute-done((f32[4,32,128]{2,1,0:T(8,128)S(1)}, f32[4,32,128]{2,1,0:T(8,128)S(1)}, u32[]{:S(2)}, u32[]{:S(2)}) %collective-permute-start.10) | collective-permute-done | bytes 65568 | tf_op jit(solution)/shard_map/ppermute | solution.py:521
  47.1 1.7 %collective-permute-done.9.refs_2_ = f32[4,32,128]{2,1,0:T(8,128)S(1)} collective-permute-done((f32[4,32,128]{2,1,0:T(8,128)S(1)}, f32[4,32,128]{2,1,0:T(8,128)S(1)}, u32[]{:S(2)}, u32[]{:S(2)}) %collective-permute-start.9) | collective-permute-done | bytes 65568 | tf_op jit(solution)/shard_map/ppermute | solution.py:521
  48.8 0.0 collective-permute-done.8.refs_1_
  48.9 0.8 %join.1 = f32[4,128,128]{2,1,0:T(8,128)} custom-call(f32[4,32,128]{2,1,0:T(8,128)S(1)} %update.1.refs_0_, f32[4,32,128]{2,1,0:T(8,128)S(1)} %collective-permute-done.8.refs_1_, f32[4,32,128]{2,1,0:T(8,128)S(1)} %collective-permute-done.9.refs_2_, f32[4,32,128]{2,1,0:T(8,128)S(1)} %collective-permute-done.10.refs_3_), custom_call_target="tpu_custom_call" | custom-call | tf_op jit(solution)/shard_map/join/pallas_call | solution.py:522
  (1 shorter events, 0.0 us)
Async XLA Ops:
  1.1 6.6 %collective-permute-start = (f32[384,128]{1,0:T(8,128)S(1)}, f32[384,128]{1,0:T(8,128)S(1)}, u32[]{:S(2)}, u32[]{:S(2)}) collective-permute-start(f32[384,128]{1,0:T(8,128)S(1)} %get-tuple-element.26), channel_id=1, source_target_pairs={{0,28},{4,0},{8,4},{12,8},{16,12},{20,16},{24,20},{28,24},{1,29},{... | collective-permute-start | bytes 589832 | tf_op jit(solution)/shard_map/ppermute | solution.py:438
  11.1 7.8 %collective-permute-start.1 = (f32[288,128]{1,0:T(8,128)S(1)}, f32[288,128]{1,0:T(8,128)S(1)}, u32[]{:S(2)}, u32[]{:S(2)}) collective-permute-start(f32[288,128]{1,0:T(8,128)S(1)} %get-tuple-element.35), channel_id=1, source_target_pairs={{0,1},{1,0},{2,3},{3,2},{4,5},{5,4},{6,7},{7,6},{8,9},{9,8},{10,11... | collective-permute-start | bytes 442376 | tf_op jit(solution)/shard_map/ppermute | solution.py:486
  12.7 14.0 %collective-permute-start.2 = (f32[288,128]{1,0:T(8,128)S(1)}, f32[288,128]{1,0:T(8,128)S(1)}, u32[]{:S(2)}, u32[]{:S(2)}) collective-permute-start(f32[288,128]{1,0:T(8,128)S(1)} %get-tuple-element.36), channel_id=1, source_target_pairs={{0,2},{1,3},{2,0},{3,1},{4,6},{5,7},{6,4},{7,5},{8,10},{9,11},{10,... | collective-permute-start | bytes 442376 | tf_op jit(solution)/shard_map/ppermute | solution.py:486
  15.3 11.4 %collective-permute-start.3 = (f32[288,128]{1,0:T(8,128)S(1)}, f32[288,128]{1,0:T(8,128)S(1)}, u32[]{:S(2)}, u32[]{:S(2)}) collective-permute-start(f32[288,128]{1,0:T(8,128)S(1)} %get-tuple-element.37), channel_id=1, source_target_pairs={{0,3},{1,2},{2,1},{3,0},{4,7},{5,6},{6,5},{7,4},{8,11},{9,10},{10,... | collective-permute-start | bytes 442376 | tf_op jit(solution)/shard_map/ppermute | solution.py:486
  29.7 5.3 %collective-permute-start.5 = (f32[4,32,128]{2,1,0:T(8,128)S(1)}, f32[4,32,128]{2,1,0:T(8,128)S(1)}, u32[]{:S(2)}, u32[]{:S(2)}) collective-permute-start(f32[4,32,128]{2,1,0:T(8,128)S(1)} %get-tuple-element.40), channel_id=1, source_target_pairs={{0,1},{1,0},{2,7},{3,6},{4,5},{5,4},{6,11},{7,10},{8,9},{9,8},{10,... | collective-permute-start | bytes 196616 | tf_op jit(solution)/shard_map/ppermute | solution.py:508
  32.1 8.1 %collective-permute-start.6 = (f32[4,32,128]{2,1,0:T(8,128)S(1)}, f32[4,32,128]{2,1,0:T(8,128)S(1)}, u32[]{:S(2)}, u32[]{:S(2)}) collective-permute-start(f32[4,32,128]{2,1,0:T(8,128)S(1)} %get-tuple-element.41), channel_id=1, source_target_pairs={{0,6},{1,7},{2,0},{3,1},{4,10},{5,11},{6,4},{7,5},{8,14},{9,15},{1... | collective-permute-start | bytes 196616 | tf_op jit(solution)/shard_map/ppermute | solution.py:508
  32.1 8.1 %collective-permute-start.7 = (f32[4,32,128]{2,1,0:T(8,128)S(1)}, f32[4,32,128]{2,1,0:T(8,128)S(1)}, u32[]{:S(2)}, u32[]{:S(2)}) collective-permute-start(f32[4,32,128]{2,1,0:T(8,128)S(1)} %get-tuple-element.42), channel_id=1, source_target_pairs={{0,7},{1,6},{2,1},{3,0},{4,11},{5,10},{6,5},{7,4},{8,15},{9,14},{1... | collective-permute-start | bytes 196616 | tf_op jit(solution)/shard_map/ppermute | solution.py:508
  33.5 6.7 %collective-permute-start.4 = (f32[4,32,128]{2,1,0:T(8,128)S(1)}, f32[4,32,128]{2,1,0:T(8,128)S(1)}, u32[]{:S(2)}, u32[]{:S(2)}) collective-permute-start(f32[4,32,128]{2,1,0:T(8,128)S(1)} %get-tuple-element.39.refs_2_), channel_id=1, source_target_pairs={{2,6},{3,7},{6,10},{7,11},{10,14},{11,15},{14,18},{15,19},{18,22},... | collective-permute-start | bytes 196616 | tf_op jit(solution)/shard_map/ppermute | solution.py:508
  40.3 6.9 %collective-permute-start.10 = (f32[4,32,128]{2,1,0:T(8,128)S(1)}, f32[4,32,128]{2,1,0:T(8,128)S(1)}, u32[]{:S(2)}, u32[]{:S(2)}) collective-permute-start(f32[4,32,128]{2,1,0:T(8,128)S(1)} %update.1.refs_0_), channel_id=1, source_target_pairs={{0,3},{1,2},{2,1},{3,0},{4,7},{5,6},{6,5},{7,4},{8,11},{9,10},{10,... | collective-permute-start | bytes 196616 | tf_op jit(solution)/shard_map/ppermute | solution.py:521
  42.9 6.0 %collective-permute-start.9 = (f32[4,32,128]{2,1,0:T(8,128)S(1)}, f32[4,32,128]{2,1,0:T(8,128)S(1)}, u32[]{:S(2)}, u32[]{:S(2)}) collective-permute-start(f32[4,32,128]{2,1,0:T(8,128)S(1)} %update.1.refs_0_), channel_id=1, source_target_pairs={{0,2},{1,3},{2,0},{3,1},{4,6},{5,7},{6,4},{7,5},{8,10},{9,11},{10,... | collective-permute-start | bytes 196616 | tf_op jit(solution)/shard_map/ppermute | solution.py:521
  43.1 5.8 %collective-permute-start.8 = (f32[4,32,128]{2,1,0:T(8,128)S(1)}, f32[4,32,128]{2,1,0:T(8,128)S(1)}, u32[]{:S(2)}, u32[]{:S(2)}) collective-permute-start(f32[4,32,128]{2,1,0:T(8,128)S(1)} %update.1.refs_0_), channel_id=1, source_target_pairs={{0,1},{1,0},{2,3},{3,2},{4,5},{5,4},{6,7},{7,6},{8,9},{9,8},{10,11... | collective-permute-start | bytes 196616 | tf_op jit(solution)/shard_map/ppermute | solution.py:521

commit v3 on v2

--- a/solution.py
+++ b/solution.py
@@ -13,8 +13,9 @@
 relax = 4.0
 floor_level = 1.0
 
-UNROLL = 4
-EDGE_UNROLL = 2
+UNROLL = 12
+EDGE_UNROLL = 4
+CHUNK = 32
 
 VM = pl.BlockSpec(memory_space=pltpu.VMEM)
 ANY = pl.BlockSpec(memory_space=pltpu.HBM)
@@ -66,28 +67,6 @@
     return jnp.concatenate(
         [jnp.concatenate(top, axis=1), jnp.concatenate(bottom, axis=1)], axis=0
     )
-
-
-def pack_kernel(offsets_any, maps_any, measured_any, out, right_root, offsets, maps, measured, sems):
-    copies = [
-        pltpu.make_async_copy(source, target, sems.at[i])
-        for i, (source, target) in enumerate(
-            ((offsets_any, offsets), (maps_any, maps), (measured_any, measured))
-        )
-    ]
-    for copy in copies:
-        copy.start()
-    materials, length, _ = maps.shape
-    half = length // 2
-    copies[1].wait()
-    for m in range(materials):
-        out[m * half : (m + 1) * half] = halves_packed(maps[m, :half], maps[m, half:], False)
-    copies[0].wait()
-    copies[2].wait()
-    left_first = offsets[0] < offsets[1]
-    first, second = jnp.sqrt(measured[0]), jnp.sqrt(measured[1])
-    out[materials * half :] = jnp.where(left_first, first, second)
-    right_root[...] = jnp.where(left_first, second, first)
 
 
 def piece(array, q, count, half_rows):
@@ -102,9 +81,9 @@
 
 
 def first_kernel(
-    tiles, count, spectrum_any, wave_any, edge_any, band_any, maps_any, probe_any,
-    table, coef, probe, own, here, power,
-    spectrum, wave_index, edge_band, band_coef, maps, sems,
+    spectrum_any, wave_any, edge_any, band_any, maps_any, probe_any,
+    table, coef, probe, near, own, far_edge, total_edge,
+    spectrum, wave_index, edge_band, band_coef, maps, packed, sems,
 ):
     copies = [
         pltpu.make_async_copy(source, target, sems.at[i])
@@ -124,8 +103,6 @@
     materials, length, _ = maps.shape
     half = length // 2
     slots = probe.shape[0]
-    tile = lax.axis_index("tile")
-    me = lax.axis_index("wave")
     group = 8
     centred_lane = (lanes(group, length) - half).astype(f32)
     row = lax.broadcasted_iota(jnp.int32, (group, length), 0)
@@ -171,15 +148,61 @@
         coef[s, 4 * materials, :] = jnp.full((length,), spectrum[s], f32)
     for m in range(materials):
         own[m] = pltpu.roll(maps[m], half, 1)
-    chunk = 32
-    low = lanes(chunk, length) < half
+        packed[m] = halves_packed(own[m, :half], own[m, half:], False)
+
+    def near_object(s, carry):
+        for start in range(0, half, CHUNK):
+            parts = object_of(coef, s, [packed[m, start : start + CHUNK] for m in range(materials)])
+            for i, part in enumerate(parts):
+                near[s, i, start : start + CHUNK] = part
+                near[s, i, half + start : half + start + CHUNK] = pltpu.roll(part, half, 1)
+        return carry
+
+    lax.fori_loop(0, slots, near_object, 0, unroll=2)
+
+    @pl.when(lax.axis_index("tile") == lax.axis_size("tile") - 1)
+    def _():
+        total_edge[...] = jnp.zeros_like(total_edge)
+        low = lanes(length, length) < half
+
+        def step(s, carry):
+            re, im, cos, sin = probe[s, 0], probe[s, 1], near[s, 0], near[s, 1]
+            field = [
+                (jnp.where(low, re * cos - im * sin, re), jnp.where(low, re * sin + im * cos, im))
+            ]
+            got = transform(block(table, s, "L"), block(table, s, "R"), field)
+            far_edge[s] = got
+            re, im = got[:, :length], got[:, length:]
+            total_edge[...] += coef[s, 4 * materials : 4 * materials + 1] * (re * re + im * im)
+            return carry
+
+        lax.fori_loop(0, slots, step, 0, unroll=EDGE_UNROLL)
+
+
+def power_kernel(
+    count, offsets_any, measured_any, coef, probe, own,
+    here, power, left_root, right_root,
+    offsets, measured, sems,
+):
+    copies = [
+        pltpu.make_async_copy(source, target, sems.at[i])
+        for i, (source, target) in enumerate(((offsets_any, offsets), (measured_any, measured)))
+    ]
+    for copy in copies:
+        copy.start()
+    materials, length, _ = own.shape
+    half = length // 2
+    slots = probe.shape[0]
+    tile, tiles = lax.axis_index("tile"), lax.axis_size("tile")
+    me = lax.axis_index("wave")
+    low = lanes(CHUNK, length) < half
     frames = jnp.where(
         low,
         jnp.where(tile == tiles - 1, 1.0, 2.0),
         jnp.where(tile == 0, 1.0, 2.0),
     )
-    for start in range(0, length, chunk):
-        at = slice(start, start + chunk)
+    for start in range(0, length, CHUNK):
+        at = slice(start, start + CHUNK)
         window = [own[m, at] for m in range(materials)]
 
         def add(s, total):
@@ -191,14 +214,30 @@
             weight = coef[s, 4 * materials : 4 * materials + 1]
             return total + (weight * jnp.exp2(absorb + absorb)) * (re * re + im * im)
 
-        total = lax.fori_loop(0, slots, add, jnp.zeros((chunk, length), f32), unroll=4)
+        total = lax.fori_loop(0, slots, add, jnp.zeros((CHUNK, length), f32), unroll=4)
         power[at] = frames * total
     half_rows = length // count
     for m in range(materials):
         here[m] = piece(own.at[m], me, count, half_rows)
-
-
-CHUNK = 32
+    for copy in copies:
+        copy.wait()
+    left_first = offsets[0] < offsets[1]
+    first, second = jnp.sqrt(measured[0]), jnp.sqrt(measured[1])
+    left_root[...] = jnp.where(left_first, first, second)
+    right_root[...] = jnp.where(left_first, second, first)
+
+
+def object_of(coef, s, window):
+    materials = len(window)
+    absorb, phase = None, None
+    for m, w in enumerate(window):
+        a = coef[s, m : m + 1] * w
+        b = coef[s, materials + m : materials + m + 1] * w
+        absorb = a if absorb is None else absorb + a
+        phase = b if phase is None else phase + b
+    damping = jnp.exp2(absorb)
+    cos, sin = cos_sin(phase)
+    return damping * cos, damping * sin
 
 
 def transform(left, right, fields):
@@ -219,86 +258,59 @@
     return jnp.dot(beside, right, preferred_element_type=f32)
 
 
-def forward_kernel(
-    tiles, count, own, halo, probe, table, coef, power,
-    psi, far, *messages_and_scratch,
-):
-    messages = messages_and_scratch[:count]
-    window, total = messages_and_scratch[count:]
-    materials, length, _ = own.shape
+def forward_kernel(count, near, halo, probe, table, coef, power, psi, far, *rest):
+    messages, (beyond, total) = rest[:count], rest[count:]
+    materials, length, _ = halo.shape
     half = length // 2
     slots = probe.shape[0]
-    edge = lax.axis_index("tile") == tiles - 1
     me = lax.axis_index("wave")
-    low = lanes(half, length) < half
     for m in range(materials):
-        packed = halo[m * half : (m + 1) * half]
-        window[m, :half] = jnp.where(low, own[m, :half], pltpu.roll(packed, half, 1))
-        window[m, half:] = jnp.where(low, own[m, half:], packed)
+        beyond[m] = halves_packed(halo[m, :half], halo[m, half:], False)
     total[...] = jnp.zeros_like(total)
+    low = lanes(CHUNK, length) < half
 
     def exit_wave(s):
-        for start in range(0, length, CHUNK):
-            at = slice(start, start + CHUNK)
-            absorb, phase = None, None
-            for m in range(materials):
-                w = window[m, at]
-                a = coef[s, m : m + 1] * w
-                b = coef[s, materials + m : materials + m + 1] * w
-                absorb = a if absorb is None else absorb + a
-                phase = b if phase is None else phase + b
-            damping = jnp.exp2(absorb)
-            cos, sin = cos_sin(phase)
-            cos, sin = damping * cos, damping * sin
-            re, im = probe[s, 0, at], probe[s, 1, at]
-            psi[s, 0, at] = re * cos - im * sin
-            psi[s, 1, at] = re * sin + im * cos
-
-    def add_intensity(s, got, at):
+        for start in range(0, half, CHUNK):
+            parts = object_of(coef, s, [beyond[m, start : start + CHUNK] for m in range(materials)])
+            upper, lower = slice(start, start + CHUNK), slice(half + start, half + start + CHUNK)
+            for at, turned in ((upper, True), (lower, False)):
+                cos, sin = [
+                    jnp.where(low, near[s, i, at], pltpu.roll(part, half, 1) if turned else part)
+                    for i, part in enumerate(parts)
+                ]
+                re, im = probe[s, 0, at], probe[s, 1, at]
+                psi[s, 0, at] = re * cos - im * sin
+                psi[s, 1, at] = re * sin + im * cos
+
+    def step(s, joined):
+        exit_wave(s)
+        re, im = psi[s, 0], psi[s, 1]
+        if joined:
+            low = lanes(length, length) < half
+            re, im = jnp.where(low, probe[s, 0], re), jnp.where(low, probe[s, 1], im)
+        got = transform(block(table, s, "L"), block(table, s, "R"), [(re, im)])
+        far[s] = got
         re, im = got[:, :length], got[:, length:]
-        total[at : at + length] += coef[s, 4 * materials : 4 * materials + 1] * (re * re + im * im)
-
-    @pl.when(jnp.logical_not(edge))
-    def _():
-        def step(s, carry):
-            exit_wave(s)
-            got = transform(block(table, s, "L"), block(table, s, "R"), [(psi[s, 0], psi[s, 1])])
-            far[s, :length] = got
-            add_intensity(s, got, 0)
-            return carry
-
-        lax.fori_loop(0, slots, step, 0, unroll=UNROLL)
-
-    @pl.when(edge)
-    def _():
-        low = lanes(length, length) < half
-
-        def step(s, carry):
-            exit_wave(s)
-            re, im, bare_re, bare_im = psi[s, 0], psi[s, 1], probe[s, 0], probe[s, 1]
-            got = transform(
-                block(table, s, "L"),
-                block(table, s, "R"),
-                [
-                    (jnp.where(low, re, bare_re), jnp.where(low, im, bare_im)),
-                    (jnp.where(low, bare_re, re), jnp.where(low, bare_im, im)),
-                ],
+        total[...] += coef[s, 4 * materials : 4 * materials + 1] * (re * re + im * im)
+
+    edge = lax.axis_index("tile") == lax.axis_size("tile") - 1
+    for joined in (False, True):
+
+        @pl.when(edge == joined)
+        def _():
+            lax.fori_loop(
+                0, slots, lambda s, c: (step(s, joined), c)[1], 0, unroll=EDGE_UNROLL if joined else UNROLL
             )
-            far[s] = got
-            add_intensity(s, got[:length], 0)
-            add_intensity(s, got[length:], length)
-            return carry
-
-        lax.fori_loop(0, slots, step, 0, unroll=EDGE_UNROLL)
 
     half_rows = length // count
     for k, message in enumerate(messages):
-        message[: 2 * length] = total[...]
-        message[2 * length :] = piece(power, jnp.bitwise_xor(me, k), count, half_rows)
-
-
-def backward_kernel(tiles, count, right_root, halo, table, coef, psi, far, *rest):
+        message[:length] = total[...]
+        message[length:] = piece(power, jnp.bitwise_xor(me, k), count, half_rows)
+
+
+def backward_kernel(tiles, count, right_root, left_root, table, coef, psi, far, far_edge, *rest):
     shares, rest = rest[:count], rest[count:]
+    edges, rest = rest[:count], rest[count:]
     sends, rest = rest[:count], rest[count:]
     scale, shortfall, gradient, back = rest
     length = right_root.shape[0]
@@ -308,23 +320,21 @@
     edge = lax.axis_index("tile") == tiles - 1
     me = lax.axis_index("wave")
     half_rows = length // count
-    powers = shares[0][2 * length :]
+    powers = shares[0][length:]
     for share in shares[1:]:
-        powers = powers + share[2 * length :]
+        powers = powers + share[length:]
     scale[...] = relax / (powers + 1.0)
     gradient[...] = jnp.zeros_like(gradient)
 
-    def inverse(at):
-        intensity = shares[0][at : at + length]
+    def inverse(shares):
+        intensity = shares[0][:length]
         for share in shares[1:]:
-            intensity = intensity + share[at : at + length]
+            intensity = intensity + share[:length]
         return lax.rsqrt(jnp.maximum(intensity, floor_level))
 
-    left_root = halo.at[materials * half :]
-
-    def delta(s, at):
+    def delta(s, far, at):
         factor = coef[s, 4 * materials : 4 * materials + 1] * shortfall[at : at + length]
-        return factor * far[s, at : at + length, :length], factor * far[s, at : at + length, length:]
+        return factor * far[s, :, :length], factor * far[s, :, length:]
 
     def collect(s):
         for start in range(0, length, CHUNK):
@@ -340,10 +350,10 @@
 
     @pl.when(jnp.logical_not(edge))
     def _():
-        shortfall[:length] = (right_root[...] + left_root[...]) * inverse(0) - 2.0
+        shortfall[:length] = (right_root[...] + left_root[...]) * inverse(shares) - 2.0
 
         def step(s, carry):
-            back[...] = transform(block(table, s, "R"), block(table, s, "L"), [delta(s, 0)])
+            back[...] = transform(block(table, s, "R"), block(table, s, "L"), [delta(s, far, 0)])
             collect(s)
             return carry
 
@@ -351,15 +361,15 @@
 
     @pl.when(edge)
     def _():
-        shortfall[:length] = right_root[...] * inverse(0) - 1.0
-        shortfall[length:] = left_root[...] * inverse(length) - 1.0
+        shortfall[:length] = left_root[...] * inverse(shares) - 1.0
+        shortfall[length:] = right_root[...] * inverse(edges) - 1.0
         low = (lax.broadcasted_iota(jnp.int32, (length, 2 * length), 1) & (length - 1)) < half
 
         def step(s, carry):
             both = transform(
-                block(table, s, "R"), block(table, s, "L"), [delta(s, 0), delta(s, length)]
+                block(table, s, "R"), block(table, s, "L"), [delta(s, far, 0), delta(s, far_edge, length)]
             )
-            back[...] = jnp.where(low, both[:length], both[length:])
+            back[...] = jnp.where(low, both[length:], both[:length])
             collect(s)
             return carry
 
@@ -421,66 +431,69 @@
     square = shape((length, length), f32)
     share = shape((materials, half_rows, length), f32)
 
-    packed, right_root = pl.pallas_call(
-        pack_kernel,
-        out_shape=(shape((materials * half + length, length), f32), square),
-        in_specs=[ANY] * 3,
-        out_specs=(VM, VM),
-        scratch_shapes=[
-            pltpu.SMEM(offsets.shape, jnp.int32),
-            pltpu.VMEM(maps.shape, f32),
-            pltpu.VMEM(measured.shape, f32),
-            pltpu.SemaphoreType.DMA((3,)),
-        ],
-        compiler_params=params(),
-        name="pack",
-    )(*map(in_hbm, (offsets, maps, measured)))
-    halo = lax.ppermute(packed, "tile", [(i, (i - 1) % tiles) for i in range(tiles)])
+    ring = [(i, (i - 1) % tiles) for i in range(tiles)]
+    halo = lax.ppermute(maps, "tile", ring)
 
     band_first = jnp.transpose(band_coef, (1, 0, 2))
-    table, coef, near_probe, own, here, power = pl.pallas_call(
-        lambda *refs: first_kernel(tiles, count, *refs),
+    field = shape((slots, length, 2 * length), f32)
+    table, coef, near_probe, near, own, far_edge, total_edge = pl.pallas_call(
+        first_kernel,
         out_shape=(
             shape((slots, 3, length, length), bf16),
             shape((slots, 6 * materials, length), f32),
             shape(probe.shape, f32),
+            shape(probe.shape, f32),
             shape(maps.shape, f32),
-            share,
+            field,
             square,
         ),
         in_specs=[ANY] * 6,
-        out_specs=(VM,) * 6,
+        out_specs=(VM,) * 7,
         scratch_shapes=[
             pltpu.SMEM(spectrum.shape, f32),
             pltpu.SMEM(wave_index.shape, jnp.int32),
             pltpu.SMEM(edge_band.shape[::-1], jnp.int32),
             pltpu.SMEM(band_first.shape, f32),
             pltpu.VMEM(maps.shape, f32),
+            pltpu.VMEM((materials, half, length), f32),
             pltpu.SemaphoreType.DMA((6,)),
         ],
         compiler_params=params(),
         cost_estimate=pl.CostEstimate(flops=10**9, bytes_accessed=2**22, transcendentals=0),
         name="tables",
     )(*map(in_hbm, (spectrum, wave_index, edge_band.T, band_first, maps, probe)))
-
-    message = shape((2 * length + half_rows, length), f32)
+    edges = [total_edge]
+    last = (tiles - 1) * count
+    for k in range(1, count):
+        pairs = [(last + w, last + (w ^ k)) for w in range(count)]
+        edges.append(lax.ppermute(total_edge, ("tile", "wave"), pairs))
+    here, power, left, right_root = pl.pallas_call(
+        lambda *refs: power_kernel(count, *refs),
+        out_shape=(share, square, square, square),
+        in_specs=[ANY] * 2 + [VM] * 3,
+        out_specs=(VM,) * 4,
+        scratch_shapes=[
+            pltpu.SMEM(offsets.shape, jnp.int32),
+            pltpu.VMEM(measured.shape, f32),
+            pltpu.SemaphoreType.DMA((2,)),
+        ],
+        compiler_params=params(),
+        name="power",
+    )(*map(in_hbm, (offsets, measured)), coef, near_probe, own)
+    left_root = lax.ppermute(left, "tile", ring)
+    message = shape((length + half_rows, length), f32)
     psi, far, *messages = pl.pallas_call(
-        lambda *refs: forward_kernel(tiles, count, *refs),
-        out_shape=(
-            shape((slots, 2, length, length), f32),
-            shape((slots, 2 * length, 2 * length), f32),
-        )
-        + (message,) * count,
+        lambda *refs: forward_kernel(count, *refs),
+        out_shape=(shape(probe.shape, f32), field) + (message,) * count,
         in_specs=[VM] * 6,
         out_specs=(VM,) * (2 + count),
         scratch_shapes=[
-            pltpu.VMEM((materials, length, length), f32),
-            pltpu.VMEM((2 * length, length), f32),
+            pltpu.VMEM((materials, half, length), f32),
+            pltpu.VMEM((length, length), f32),
         ],
         compiler_params=params(),
         name="forward",
-    )(own, halo, near_probe, table, coef, power)
-
+    )(near, halo, near_probe, table, coef, power)
     shares = [messages[0]]
     for k in range(1, count):
         shares.append(lax.ppermute(messages[k], "wave", [(w, w ^ k) for w in range(count)]))
@@ -488,7 +501,7 @@
     *sends, scale = pl.pallas_call(
         lambda *refs: backward_kernel(tiles, count, *refs),
         out_shape=(share,) * count + (shape((half_rows, length), f32),),
-        in_specs=[VM] * (6 + count),
+        in_specs=[VM] * (7 + 2 * count),
         out_specs=(VM,) * (count + 1),
         scratch_shapes=[
             pltpu.VMEM((2 * length, length), f32),
@@ -497,7 +510,7 @@
         ],
         compiler_params=params(),
         name="backward",
-    )(right_root, halo, table, coef, psi, far, *shares)
+    )(right_root, left_root, table, coef, psi, far, far_edge, *shares, *edges)
 
     def owner(t, q):
         return (t + (q >= count // 2)) % tiles * count + q

time: 49.9 us -> 46.9 us (0.940)
  waiting for transfers between devices: 22.3 us -> 14.7 us
  starting transfers between devices: 16.8 us -> 21.9 us
  Pallas kernels: 10.6 us -> 9.99 us
    ppermute x3, waiting for transfers between devices: 11.2 us -> 4.64 us  [per_device(): lax.ppermute(messages[k], 'wave', [(w, w ^ k) for w in range(count)])]
    ppermute x1 -> x5, starting transfers between devices: 3.39 us -> 8.74 us  [the longest x1 3.43 us: per_device(): left_root = lax.ppermute(left, 'tile', ring)]
    ppermute x4, starting transfers between devices: 4.49 us -> 2.21 us  [per_device(): lax.ppermute(sends[k], ('tile', 'wave'), [p for p in pairs if p[0] != p[1]])]
    ppermute x3, starting transfers between devices: 4.45 us -> 6.5 us  [per_device(): parts.append(lax.ppermute(new, 'wave', [(w, w ^ k) for w in range(count)]))]
    ppermute x1 -> x5, waiting for transfers between devices: 0.94 us -> 0.01 us  [the longest x3 0.01 us: per_device(): edges.append(lax.ppermute(total_edge, ('tile', 'wave'), pairs))]
  transfers between devices with their start and end apart: 11 -> 15, of which waited for: 7 -> 7; matrix products, arithmetic and copies ran while one was open for 0% -> 0% of each run, Pallas kernels for 5% -> 14%
where the time goes in v3:
time: 46.9 us; the launch traced here: 46.7 us
  starting transfers between devices  21.9 us (47%)
  waiting for transfers between devices  14.7 us (31%)
  Pallas kernels  9.99 us (21%)
    ppermute x3, starting transfers between devices, per_device(): parts.append(lax.ppermute(new, 'wave', [(w, w ^ k) for w in range(count)]))  6.5 us
    ppermute x4, waiting for transfers between devices, per_device(): lax.ppermute(sends[k], ('tile', 'wave'), [p for p in pairs if p[0] != p[1]])  5.99 us
    ppermute x3, waiting for transfers between devices, per_device(): lax.ppermute(messages[k], 'wave', [(w, w ^ k) for w in range(count)])  4.64 us
    ppermute x3, starting transfers between devices, per_device(): lax.ppermute(messages[k], 'wave', [(w, w ^ k) for w in range(count)])  4.45 us
    ppermute x3, waiting for transfers between devices, per_device(): parts.append(lax.ppermute(new, 'wave', [(w, w ^ k) for w in range(count)]))  4.05 us
    ppermute x1, starting transfers between devices, per_device(): left_root = lax.ppermute(left, 'tile', ring)  3.43 us
    ppermute x1, starting transfers between devices, per_device(): halo = lax.ppermute(maps, 'tile', ring)  3.33 us
    pallas_call x1, Pallas kernels, per_device(): pl.pallas_call(first_kernel, out_shape=(shape((slots, 3, length, length),...  2.76 us
  transfers between devices with their start and end apart: 15, of which 7 were waited for; matrix products, arithmetic and copies ran while one was open for 0% of the time, Pallas kernels for 14%

profile of v3, /device:TPU:0, one launch (start us, length us, event | category | flops | bytes accessed | tf_op | source)
XLA Modules:
  0.0 46.7 jit_solution(5749950618642827219)
XLA Ops:
  0.0 3.3 %collective-permute-start.1 = (f32[4,128,128]{2,1,0:T(8,128)}, f32[4,128,128]{2,1,0:T(8,128)S(1)}, u32[]{:S(2)}, u32[]{:S(2)}) collective-permute-start(f32[4,128,128]{2,1,0:T(8,128)} %maps_any.1), channel_id=1, source_target_pairs={{0,28},{4,0},{8,4},{12,8},{16,12},{20,16},{24,20},{28,24},{1,29},{... | collective-permute-start | bytes 786440 | tf_op jit(solution)/shard_map/ppermute | solution.py:435
  3.3 2.8 %tables.1 = (bf16[12,3,128,128]{3,2,1,0:T(8,128)(2,1)S(1)}, f32[12,24,128]{2,1,0:T(8,128)S(1)}, f32[12,2,128,128]{3,2,1,0:T(8,128)S(1)}, f32[12,2,128,128]{3,2,1...) custom-call(f32[12]{0:T(128)} %spectrum_any.1, s32[12]{0:T(128)} %wave_any.1, ...), custom_call_target="tpu_custom_call" | custom-call | flops 1000000000 | bytes 4194304 | tf_op jit(solution)/shard_map/tables/pallas_call | solution.py:439
  6.1 1.0 %power.1 = (f32[4,32,128]{2,1,0:T(8,128)S(1)}, f32[128,128]{1,0:T(8,128)S(1)}, f32[128,128]{1,0:T(8,128)S(1)}, f32[128,128]{1,0:T(8,128)S(1)}) custom-call(s32[2]{0:T(128)} %refs_0_.1, f32[2,128,128]{2,1,0:T(8,128)} %refs_1_.1, f32[12,24,128]{2,1,0:T(8,128)S(1)} %get-tuple-element.27.refs_2_.refs_4_.refs_3_, ...), custom_call_target="tpu_custom_call" | custom-call | tf_op jit(solution)/shard_map/power/pallas_call | solution.py:470
  7.1 3.4 %collective-permute-start = (f32[128,128]{1,0:T(8,128)S(1)}, f32[128,128]{1,0:T(8,128)S(1)}, u32[]{:S(2)}, u32[]{:S(2)}) collective-permute-start(f32[128,128]{1,0:T(8,128)S(1)} %get-tuple-element.32), channel_id=1, source_target_pairs={{0,28},{4,0},{8,4},{12,8},{16,12},{20,16},{24,20},{28,24},{1,29},{... | collective-permute-start | bytes 196616 | tf_op jit(solution)/shard_map/ppermute | solution.py:483
  10.5 0.7 %collective-permute-start.7 = (f32[128,128]{1,0:T(8,128)S(1)}, f32[128,128]{1,0:T(8,128)S(1)}, u32[]{:S(2)}, u32[]{:S(2)}) collective-permute-start(f32[128,128]{1,0:T(8,128)S(1)} %get-tuple-element.43.refs_11_), channel_id=1, source_target_pairs={{28,31},{29,30},{30,29},{31,28}} | collective-permute-start | bytes 196616 | tf_op jit(solution)/shard_map/ppermute | solution.py:469
  11.2 0.0 collective-permute-done.1.refs_1_
  11.2 2.7 %forward.1 = (f32[12,2,128,128]{3,2,1,0:T(8,128)S(1)}, f32[12,128,256]{2,1,0:T(8,128)S(1)}, f32[160,128]{1,0:T(8,128)S(1)}, f32[160,128]{1,0:T(8,128)S(1)}, f32[...) custom-call(f32[12,2,128,128]{3,2,1,0:T(8,128)S(1)} %get-tuple-element.34.refs_0_, ...), custom_call_target="tpu_custom_call" | custom-call | tf_op jit(solution)/shard_map/forward/pallas_call | solution.py:485
  13.9 1.6 %collective-permute-start.2 = (f32[160,128]{1,0:T(8,128)S(1)}, f32[160,128]{1,0:T(8,128)S(1)}, u32[]{:S(2)}, u32[]{:S(2)}) collective-permute-start(f32[160,128]{1,0:T(8,128)S(1)} %get-tuple-element.40), channel_id=1, source_target_pairs={{0,1},{1,0},{2,3},{3,2},{4,5},{5,4},{6,7},{7,6},{8,9},{9,8},{10,11... | collective-permute-start | bytes 245768 | tf_op jit(solution)/shard_map/ppermute | solution.py:499
  15.6 2.6 %collective-permute-start.3 = (f32[160,128]{1,0:T(8,128)S(1)}, f32[160,128]{1,0:T(8,128)S(1)}, u32[]{:S(2)}, u32[]{:S(2)}) collective-permute-start(f32[160,128]{1,0:T(8,128)S(1)} %get-tuple-element.41), channel_id=1, source_target_pairs={{0,2},{1,3},{2,0},{3,1},{4,6},{5,7},{6,4},{7,5},{8,10},{9,11},{10,... | collective-permute-start | bytes 245768 | tf_op jit(solution)/shard_map/ppermute | solution.py:499
  18.1 0.2 collective-permute-start.4
  18.4 0.0 collective-permute-done.refs_1_
  18.4 0.7 %collective-permute-start.6 = (f32[128,128]{1,0:T(8,128)S(1)}, f32[128,128]{1,0:T(8,128)S(1)}, u32[]{:S(2)}, u32[]{:S(2)}) collective-permute-start(f32[128,128]{1,0:T(8,128)S(1)} %get-tuple-element.43.refs_11_), channel_id=1, source_target_pairs={{28,30},{29,31},{30,28},{31,29}} | collective-permute-start | bytes 196616 | tf_op jit(solution)/shard_map/ppermute | solution.py:469
  19.0 0.0 collective-permute-done.7.refs_14_
  19.0 0.7 %collective-permute-start.5 = (f32[128,128]{1,0:T(8,128)S(1)}, f32[128,128]{1,0:T(8,128)S(1)}, u32[]{:S(2)}, u32[]{:S(2)}) collective-permute-start(f32[128,128]{1,0:T(8,128)S(1)} %get-tuple-element.43.refs_11_), channel_id=1, source_target_pairs={{28,29},{29,28},{30,31},{31,30}} | collective-permute-start | bytes 196616 | tf_op jit(solution)/shard_map/ppermute | solution.py:469
  19.7 0.0 collective-permute-done.6.refs_13_
  19.7 0.0 collective-permute-done.5.refs_12_
  19.7 0.0 collective-permute-done.2.refs_8_
  19.7 2.3 %collective-permute-done.3.refs_9_ = f32[160,128]{1,0:T(8,128)S(1)} collective-permute-done((f32[160,128]{1,0:T(8,128)S(1)}, f32[160,128]{1,0:T(8,128)S(1)}, u32[]{:S(2)}, u32[]{:S(2)}) %collective-permute-start.3) | collective-permute-done | bytes 81952 | tf_op jit(solution)/shard_map/ppermute | solution.py:499
  22.0 2.4 %collective-permute-done.4.refs_10_ = f32[160,128]{1,0:T(8,128)S(1)} collective-permute-done((f32[160,128]{1,0:T(8,128)S(1)}, f32[160,128]{1,0:T(8,128)S(1)}, u32[]{:S(2)}, u32[]{:S(2)}) %collective-permute-start.4) | collective-permute-done | bytes 81952 | tf_op jit(solution)/shard_map/ppermute | solution.py:499
  24.4 2.7 %backward.1 = (f32[4,32,128]{2,1,0:T(8,128)S(1)}, f32[4,32,128]{2,1,0:T(8,128)S(1)}, f32[4,32,128]{2,1,0:T(8,128)S(1)}, f32[4,32,128]{2,1,0:T(8,128)S(1)}, f32[32,128]{1,0:T(8,128)S(1)}) custom-call(f32[128,128]{1,0:T(8,128)S(1)} %get-tuple-element.31.refs_0_, f32[128,128]{1,0:T(8,128)S(1)} %collective-permute-done.refs_1_, ...), custom_call_target="tpu_custom_call" | custom-call | tf_op jit(solution)/shard_map/backward/pallas_call | solution.py:501
  27.1 0.0 collective-permute-start.9
  27.1 0.1 collective-permute-start.10
  27.2 1.4 %collective-permute-start.11 = (f32[4,32,128]{2,1,0:T(8,128)S(1)}, f32[4,32,128]{2,1,0:T(8,128)S(1)}, u32[]{:S(2)}, u32[]{:S(2)}) collective-permute-start(f32[4,32,128]{2,1,0:T(8,128)S(1)} %get-tuple-element.48), channel_id=1, source_target_pairs={{0,7},{1,6},{2,1},{3,0},{4,11},{5,10},{6,5},{7,4},{8,15},{9,14},{1... | collective-permute-start | bytes 196616 | tf_op jit(solution)/shard_map/ppermute | solution.py:521
  28.6 0.7 %collective-permute-start.8 = (f32[4,32,128]{2,1,0:T(8,128)S(1)}, f32[4,32,128]{2,1,0:T(8,128)S(1)}, u32[]{:S(2)}, u32[]{:S(2)}) collective-permute-start(f32[4,32,128]{2,1,0:T(8,128)S(1)} %get-tuple-element.45.refs_2_), channel_id=1, source_target_pairs={{2,6},{3,7},{6,10},{7,11},{10,14},{11,15},{14,18},{15,19},{18,22},... | collective-permute-start | bytes 196616 | tf_op jit(solution)/shard_map/ppermute | solution.py:521
  29.3 2.1 %collective-permute-done.9.refs_4_ = f32[4,32,128]{2,1,0:T(8,128)S(1)} collective-permute-done((f32[4,32,128]{2,1,0:T(8,128)S(1)}, f32[4,32,128]{2,1,0:T(8,128)S(1)}, u32[]{:S(2)}, u32[]{:S(2)}) %collective-permute-start.9) | collective-permute-done | bytes 65568 | tf_op jit(solution)/shard_map/ppermute | solution.py:521
  31.4 3.9 %collective-permute-done.10.refs_5_ = f32[4,32,128]{2,1,0:T(8,128)S(1)} collective-permute-done((f32[4,32,128]{2,1,0:T(8,128)S(1)}, f32[4,32,128]{2,1,0:T(8,128)S(1)}, u32[]{:S(2)}, u32[]{:S(2)}) %collective-permute-start.10) | collective-permute-done | bytes 65568 | tf_op jit(solution)/shard_map/ppermute | solution.py:521
  35.3 0.0 collective-permute-done.11.refs_6_
  35.3 0.0 collective-permute-done.8.refs_3_
  35.3 4.7 %collective-permute-start.14 = (f32[4,32,128]{2,1,0:T(8,128)S(1)}, f32[4,32,128]{2,1,0:T(8,128)S(1)}, u32[]{:S(2)}, u32[]{:S(2)}) collective-permute-start(f32[4,32,128]{2,1,0:T(8,128)S(1)} %update.1.refs_0_), channel_id=1, source_target_pairs={{0,3},{1,2},{2,1},{3,0},{4,7},{5,6},{6,5},{7,4},{8,11},{9,10},{10,... | collective-permute-start | bytes 196616 | tf_op jit(solution)/shard_map/ppermute | solution.py:534
  40.0 1.3 %collective-permute-start.13 = (f32[4,32,128]{2,1,0:T(8,128)S(1)}, f32[4,32,128]{2,1,0:T(8,128)S(1)}, u32[]{:S(2)}, u32[]{:S(2)}) collective-permute-start(f32[4,32,128]{2,1,0:T(8,128)S(1)} %update.1.refs_0_), channel_id=1, source_target_pairs={{0,2},{1,3},{2,0},{3,1},{4,6},{5,7},{6,4},{7,5},{8,10},{9,11},{10,... | collective-permute-start | bytes 196616 | tf_op jit(solution)/shard_map/ppermute | solution.py:534
  41.3 0.5 %collective-permute-start.12 = (f32[4,32,128]{2,1,0:T(8,128)S(1)}, f32[4,32,128]{2,1,0:T(8,128)S(1)}, u32[]{:S(2)}, u32[]{:S(2)}) collective-permute-start(f32[4,32,128]{2,1,0:T(8,128)S(1)} %update.1.refs_0_), channel_id=1, source_target_pairs={{0,1},{1,0},{2,3},{3,2},{4,5},{5,4},{6,7},{7,6},{8,9},{9,8},{10,11... | collective-permute-start | bytes 196616 | tf_op jit(solution)/shard_map/ppermute | solution.py:534
  41.8 1.0 %collective-permute-done.14.refs_3_ = f32[4,32,128]{2,1,0:T(8,128)S(1)} collective-permute-done((f32[4,32,128]{2,1,0:T(8,128)S(1)}, f32[4,32,128]{2,1,0:T(8,128)S(1)}, u32[]{:S(2)}, u32[]{:S(2)}) %collective-permute-start.14) | collective-permute-done | bytes 65568 | tf_op jit(solution)/shard_map/ppermute | solution.py:534
  42.9 2.3 %collective-permute-done.13.refs_2_ = f32[4,32,128]{2,1,0:T(8,128)S(1)} collective-permute-done((f32[4,32,128]{2,1,0:T(8,128)S(1)}, f32[4,32,128]{2,1,0:T(8,128)S(1)}, u32[]{:S(2)}, u32[]{:S(2)}) %collective-permute-start.13) | collective-permute-done | bytes 65568 | tf_op jit(solution)/shard_map/ppermute | solution.py:534
  45.2 0.7 %collective-permute-done.12.refs_1_ = f32[4,32,128]{2,1,0:T(8,128)S(1)} collective-permute-done((f32[4,32,128]{2,1,0:T(8,128)S(1)}, f32[4,32,128]{2,1,0:T(8,128)S(1)}, u32[]{:S(2)}, u32[]{:S(2)}) %collective-permute-start.12) | collective-permute-done | bytes 65568 | tf_op jit(solution)/shard_map/ppermute | solution.py:534
  45.9 0.8 %join.1 = f32[4,128,128]{2,1,0:T(8,128)} custom-call(f32[4,32,128]{2,1,0:T(8,128)S(1)} %update.1.refs_0_, f32[4,32,128]{2,1,0:T(8,128)S(1)} %collective-permute-done.12.refs_1_, f32[4,32,128]{2,1,0:T(8,128)S(1)} %collective-permute-done.13.refs_2_, f32[4,32,128]{2,1,0:T(8,128)S(1)} %collective-permute-done.14.refs_3_), custom_call_target="tpu_custom_call" | custom-call | tf_op jit(solution)/shard_map/join/pallas_call | solution.py:535
  (1 shorter events, 0.0 us)
Async XLA Ops:
  0.0 11.2 %collective-permute-start.1 = (f32[4,128,128]{2,1,0:T(8,128)}, f32[4,128,128]{2,1,0:T(8,128)S(1)}, u32[]{:S(2)}, u32[]{:S(2)}) collective-permute-start(f32[4,128,128]{2,1,0:T(8,128)} %maps_any.1), channel_id=1, source_target_pairs={{0,28},{4,0},{8,4},{12,8},{16,12},{20,16},{24,20},{28,24},{1,29},{... | collective-permute-start | bytes 786440 | tf_op jit(solution)/shard_map/ppermute | solution.py:435
  7.1 11.3 %collective-permute-start = (f32[128,128]{1,0:T(8,128)S(1)}, f32[128,128]{1,0:T(8,128)S(1)}, u32[]{:S(2)}, u32[]{:S(2)}) collective-permute-start(f32[128,128]{1,0:T(8,128)S(1)} %get-tuple-element.32), channel_id=1, source_target_pairs={{0,28},{4,0},{8,4},{12,8},{16,12},{20,16},{24,20},{28,24},{1,29},{... | collective-permute-start | bytes 196616 | tf_op jit(solution)/shard_map/ppermute | solution.py:483
  10.5 8.5 %collective-permute-start.7 = (f32[128,128]{1,0:T(8,128)S(1)}, f32[128,128]{1,0:T(8,128)S(1)}, u32[]{:S(2)}, u32[]{:S(2)}) collective-permute-start(f32[128,128]{1,0:T(8,128)S(1)} %get-tuple-element.43.refs_11_), channel_id=1, source_target_pairs={{28,31},{29,30},{30,29},{31,28}} | collective-permute-start | bytes 196616 | tf_op jit(solution)/shard_map/ppermute | solution.py:469
  13.9 5.8 %collective-permute-start.2 = (f32[160,128]{1,0:T(8,128)S(1)}, f32[160,128]{1,0:T(8,128)S(1)}, u32[]{:S(2)}, u32[]{:S(2)}) collective-permute-start(f32[160,128]{1,0:T(8,128)S(1)} %get-tuple-element.40), channel_id=1, source_target_pairs={{0,1},{1,0},{2,3},{3,2},{4,5},{5,4},{6,7},{7,6},{8,9},{9,8},{10,11... | collective-permute-start | bytes 245768 | tf_op jit(solution)/shard_map/ppermute | solution.py:499
  15.6 6.4 %collective-permute-start.3 = (f32[160,128]{1,0:T(8,128)S(1)}, f32[160,128]{1,0:T(8,128)S(1)}, u32[]{:S(2)}, u32[]{:S(2)}) collective-permute-start(f32[160,128]{1,0:T(8,128)S(1)} %get-tuple-element.41), channel_id=1, source_target_pairs={{0,2},{1,3},{2,0},{3,1},{4,6},{5,7},{6,4},{7,5},{8,10},{9,11},{10,... | collective-permute-start | bytes 245768 | tf_op jit(solution)/shard_map/ppermute | solution.py:499
  18.1 6.2 %collective-permute-start.4 = (f32[160,128]{1,0:T(8,128)S(1)}, f32[160,128]{1,0:T(8,128)S(1)}, u32[]{:S(2)}, u32[]{:S(2)}) collective-permute-start(f32[160,128]{1,0:T(8,128)S(1)} %get-tuple-element.42), channel_id=1, source_target_pairs={{0,3},{1,2},{2,1},{3,0},{4,7},{5,6},{6,5},{7,4},{8,11},{9,10},{10,... | collective-permute-start | bytes 245768 | tf_op jit(solution)/shard_map/ppermute | solution.py:499
  18.4 1.3 %collective-permute-start.6 = (f32[128,128]{1,0:T(8,128)S(1)}, f32[128,128]{1,0:T(8,128)S(1)}, u32[]{:S(2)}, u32[]{:S(2)}) collective-permute-start(f32[128,128]{1,0:T(8,128)S(1)} %get-tuple-element.43.refs_11_), channel_id=1, source_target_pairs={{28,30},{29,31},{30,28},{31,29}} | collective-permute-start | bytes 196616 | tf_op jit(solution)/shard_map/ppermute | solution.py:469
  19.0 0.7 %collective-permute-start.5 = (f32[128,128]{1,0:T(8,128)S(1)}, f32[128,128]{1,0:T(8,128)S(1)}, u32[]{:S(2)}, u32[]{:S(2)}) collective-permute-start(f32[128,128]{1,0:T(8,128)S(1)} %get-tuple-element.43.refs_11_), channel_id=1, source_target_pairs={{28,29},{29,28},{30,31},{31,30}} | collective-permute-start | bytes 196616 | tf_op jit(solution)/shard_map/ppermute | solution.py:469
  27.1 4.3 %collective-permute-start.9 = (f32[4,32,128]{2,1,0:T(8,128)S(1)}, f32[4,32,128]{2,1,0:T(8,128)S(1)}, u32[]{:S(2)}, u32[]{:S(2)}) collective-permute-start(f32[4,32,128]{2,1,0:T(8,128)S(1)} %get-tuple-element.46), channel_id=1, source_target_pairs={{0,1},{1,0},{2,7},{3,6},{4,5},{5,4},{6,11},{7,10},{8,9},{9,8},{10,... | collective-permute-start | bytes 196616 | tf_op jit(solution)/shard_map/ppermute | solution.py:521
  27.1 8.2 %collective-permute-start.10 = (f32[4,32,128]{2,1,0:T(8,128)S(1)}, f32[4,32,128]{2,1,0:T(8,128)S(1)}, u32[]{:S(2)}, u32[]{:S(2)}) collective-permute-start(f32[4,32,128]{2,1,0:T(8,128)S(1)} %get-tuple-element.47), channel_id=1, source_target_pairs={{0,6},{1,7},{2,0},{3,1},{4,10},{5,11},{6,4},{7,5},{8,14},{9,15},{1... | collective-permute-start | bytes 196616 | tf_op jit(solution)/shard_map/ppermute | solution.py:521
  27.2 8.1 %collective-permute-start.11 = (f32[4,32,128]{2,1,0:T(8,128)S(1)}, f32[4,32,128]{2,1,0:T(8,128)S(1)}, u32[]{:S(2)}, u32[]{:S(2)}) collective-permute-start(f32[4,32,128]{2,1,0:T(8,128)S(1)} %get-tuple-element.48), channel_id=1, source_target_pairs={{0,7},{1,6},{2,1},{3,0},{4,11},{5,10},{6,5},{7,4},{8,15},{9,14},{1... | collective-permute-start | bytes 196616 | tf_op jit(solution)/shard_map/ppermute | solution.py:521
  28.6 6.7 %collective-permute-start.8 = (f32[4,32,128]{2,1,0:T(8,128)S(1)}, f32[4,32,128]{2,1,0:T(8,128)S(1)}, u32[]{:S(2)}, u32[]{:S(2)}) collective-permute-start(f32[4,32,128]{2,1,0:T(8,128)S(1)} %get-tuple-element.45.refs_2_), channel_id=1, source_target_pairs={{2,6},{3,7},{6,10},{7,11},{10,14},{11,15},{14,18},{15,19},{18,22},... | collective-permute-start | bytes 196616 | tf_op jit(solution)/shard_map/ppermute | solution.py:521
  35.3 7.5 %collective-permute-start.14 = (f32[4,32,128]{2,1,0:T(8,128)S(1)}, f32[4,32,128]{2,1,0:T(8,128)S(1)}, u32[]{:S(2)}, u32[]{:S(2)}) collective-permute-start(f32[4,32,128]{2,1,0:T(8,128)S(1)} %update.1.refs_0_), channel_id=1, source_target_pairs={{0,3},{1,2},{2,1},{3,0},{4,7},{5,6},{6,5},{7,4},{8,11},{9,10},{10,... | collective-permute-start | bytes 196616 | tf_op jit(solution)/shard_map/ppermute | solution.py:534
  40.0 5.2 %collective-permute-start.13 = (f32[4,32,128]{2,1,0:T(8,128)S(1)}, f32[4,32,128]{2,1,0:T(8,128)S(1)}, u32[]{:S(2)}, u32[]{:S(2)}) collective-permute-start(f32[4,32,128]{2,1,0:T(8,128)S(1)} %update.1.refs_0_), channel_id=1, source_target_pairs={{0,2},{1,3},{2,0},{3,1},{4,6},{5,7},{6,4},{7,5},{8,10},{9,11},{10,... | collective-permute-start | bytes 196616 | tf_op jit(solution)/shard_map/ppermute | solution.py:534
  41.3 4.5 %collective-permute-start.12 = (f32[4,32,128]{2,1,0:T(8,128)S(1)}, f32[4,32,128]{2,1,0:T(8,128)S(1)}, u32[]{:S(2)}, u32[]{:S(2)}) collective-permute-start(f32[4,32,128]{2,1,0:T(8,128)S(1)} %update.1.refs_0_), channel_id=1, source_target_pairs={{0,1},{1,0},{2,3},{3,2},{4,5},{5,4},{6,7},{7,6},{8,9},{9,8},{10,11... | collective-permute-start | bytes 196616 | tf_op jit(solution)/shard_map/ppermute | solution.py:534

commit v4 on v3

--- a/solution.py
+++ b/solution.py
@@ -14,7 +14,7 @@
 floor_level = 1.0
 
 UNROLL = 12
-EDGE_UNROLL = 4
+EDGE_UNROLL = 12
 CHUNK = 32
 
 VM = pl.BlockSpec(memory_space=pltpu.VMEM)
@@ -255,7 +255,9 @@
         ],
         axis=0,
     )
-    return jnp.dot(beside, right, preferred_element_type=f32)
+    if len(fields) == 1:
+        beside = jnp.concatenate([beside, beside], axis=0)
+    return jnp.dot(beside, right, preferred_element_type=f32)[: len(fields) * length]
 
 
 def forward_kernel(count, near, halo, probe, table, coef, power, psi, far, *rest):

time: 46.9 us -> 43.8 us (0.934)
  Pallas kernels: 9.99 us -> 7.59 us
  starting transfers between devices: 21.9 us -> 21.3 us
    ppermute x1, starting transfers between devices: 3.43 us -> 1.85 us  [per_device(): left_root = lax.ppermute(left, 'tile', ring)]
    ppermute x4, starting transfers between devices: 2.21 us -> 3.69 us  [per_device(): lax.ppermute(sends[k], ('tile', 'wave'), [p for p in pairs if p[0] != p[1]])]
    pallas_call x1, Pallas kernels: 2.67 us -> 1.41 us  [per_device(): pl.pallas_call(lambda *refs: backward_kernel(tiles, count, *refs), out_sh...]
    pallas_call x1, Pallas kernels: 2.73 us -> 1.59 us  [per_device(): pl.pallas_call(lambda *refs: forward_kernel(count, *refs), out_shape=(sha...]
    ppermute x4, waiting for transfers between devices: 5.99 us -> 5.43 us  [per_device(): lax.ppermute(sends[k], ('tile', 'wave'), [p for p in pairs if p[0] != p[1]])]
    ppermute x3, starting transfers between devices: 6.5 us -> 6.03 us  [per_device(): parts.append(lax.ppermute(new, 'wave', [(w, w ^ k) for w in range(count)]))]
  transfers between devices with their start and end apart: 15 -> 15, of which waited for: 7 -> 7; matrix products, arithmetic and copies ran while one was open for 0% -> 0% of each run, Pallas kernels for 14% -> 12%
where the time goes in v4:
time: 43.8 us; the launch traced here: 43.3 us
  starting transfers between devices  21.3 us (49%)
  waiting for transfers between devices  14.3 us (33%)
  Pallas kernels  7.59 us (17%)
    ppermute x3, starting transfers between devices, per_device(): parts.append(lax.ppermute(new, 'wave', [(w, w ^ k) for w in range(count)]))  6.03 us
    ppermute x4, waiting for transfers between devices, per_device(): lax.ppermute(sends[k], ('tile', 'wave'), [p for p in pairs if p[0] != p[1]])  5.43 us
    ppermute x3, waiting for transfers between devices, per_device(): lax.ppermute(messages[k], 'wave', [(w, w ^ k) for w in range(count)])  4.75 us
    ppermute x3, starting transfers between devices, per_device(): lax.ppermute(messages[k], 'wave', [(w, w ^ k) for w in range(count)])  4.45 us
    ppermute x3, waiting for transfers between devices, per_device(): parts.append(lax.ppermute(new, 'wave', [(w, w ^ k) for w in range(count)]))  4.12 us
    ppermute x4, starting transfers between devices, per_device(): lax.ppermute(sends[k], ('tile', 'wave'), [p for p in pairs if p[0] != p[1]])  3.69 us
    ppermute x1, starting transfers between devices, per_device(): halo = lax.ppermute(maps, 'tile', ring)  3.33 us
    pallas_call x1, Pallas kernels, per_device(): pl.pallas_call(first_kernel, out_shape=(shape((slots, 3, length, length),...  2.76 us
  transfers between devices with their start and end apart: 15, of which 7 were waited for; matrix products, arithmetic and copies ran while one was open for 0% of the time, Pallas kernels for 12%

profile of v4, /device:TPU:0, one launch (start us, length us, event | category | flops | bytes accessed | tf_op | source)
XLA Modules:
  0.0 43.3 jit_solution(2246317134722071760)
XLA Ops:
  0.0 3.3 %collective-permute-start.1 = (f32[4,128,128]{2,1,0:T(8,128)}, f32[4,128,128]{2,1,0:T(8,128)S(1)}, u32[]{:S(2)}, u32[]{:S(2)}) collective-permute-start(f32[4,128,128]{2,1,0:T(8,128)} %maps_any.1), channel_id=1, source_target_pairs={{0,28},{4,0},{8,4},{12,8},{16,12},{20,16},{24,20},{28,24},{1,29},{... | collective-permute-start | bytes 786440 | tf_op jit(solution)/shard_map/ppermute | solution.py:437
  3.3 2.8 %tables.1 = (bf16[12,3,128,128]{3,2,1,0:T(8,128)(2,1)S(1)}, f32[12,24,128]{2,1,0:T(8,128)S(1)}, f32[12,2,128,128]{3,2,1,0:T(8,128)S(1)}, f32[12,2,128,128]{3,2,1...) custom-call(f32[12]{0:T(128)} %spectrum_any.1, s32[12]{0:T(128)} %wave_any.1, ...), custom_call_target="tpu_custom_call" | custom-call | flops 1000000000 | bytes 4194304 | tf_op jit(solution)/shard_map/tables/pallas_call | solution.py:441
  6.1 1.0 %power.1 = (f32[4,32,128]{2,1,0:T(8,128)S(1)}, f32[128,128]{1,0:T(8,128)S(1)}, f32[128,128]{1,0:T(8,128)S(1)}, f32[128,128]{1,0:T(8,128)S(1)}) custom-call(s32[2]{0:T(128)} %refs_0_.1, f32[2,128,128]{2,1,0:T(8,128)} %refs_1_.1, f32[12,24,128]{2,1,0:T(8,128)S(1)} %get-tuple-element.27.refs_2_.refs_4_.refs_3_, ...), custom_call_target="tpu_custom_call" | custom-call | tf_op jit(solution)/shard_map/power/pallas_call | solution.py:472
  7.1 1.9 %collective-permute-start = (f32[128,128]{1,0:T(8,128)S(1)}, f32[128,128]{1,0:T(8,128)S(1)}, u32[]{:S(2)}, u32[]{:S(2)}) collective-permute-start(f32[128,128]{1,0:T(8,128)S(1)} %get-tuple-element.32), channel_id=1, source_target_pairs={{0,28},{4,0},{8,4},{12,8},{16,12},{20,16},{24,20},{28,24},{1,29},{... | collective-permute-start | bytes 196616 | tf_op jit(solution)/shard_map/ppermute | solution.py:485
  8.9 0.7 %collective-permute-start.7 = (f32[128,128]{1,0:T(8,128)S(1)}, f32[128,128]{1,0:T(8,128)S(1)}, u32[]{:S(2)}, u32[]{:S(2)}) collective-permute-start(f32[128,128]{1,0:T(8,128)S(1)} %get-tuple-element.43.refs_11_), channel_id=1, source_target_pairs={{28,31},{29,30},{30,29},{31,28}} | collective-permute-start | bytes 196616 | tf_op jit(solution)/shard_map/ppermute | solution.py:471
  9.6 0.0 collective-permute-done.1.refs_1_
  9.6 1.6 %forward.1 = (f32[12,2,128,128]{3,2,1,0:T(8,128)S(1)}, f32[12,128,256]{2,1,0:T(8,128)S(1)}, f32[160,128]{1,0:T(8,128)S(1)}, f32[160,128]{1,0:T(8,128)S(1)}, f32[...) custom-call(f32[12,2,128,128]{3,2,1,0:T(8,128)S(1)} %get-tuple-element.34.refs_0_, ...), custom_call_target="tpu_custom_call" | custom-call | tf_op jit(solution)/shard_map/forward/pallas_call | solution.py:487
  11.2 1.6 %collective-permute-start.2 = (f32[160,128]{1,0:T(8,128)S(1)}, f32[160,128]{1,0:T(8,128)S(1)}, u32[]{:S(2)}, u32[]{:S(2)}) collective-permute-start(f32[160,128]{1,0:T(8,128)S(1)} %get-tuple-element.40), channel_id=1, source_target_pairs={{0,1},{1,0},{2,3},{3,2},{4,5},{5,4},{6,7},{7,6},{8,9},{9,8},{10,11... | collective-permute-start | bytes 245768 | tf_op jit(solution)/shard_map/ppermute | solution.py:501
  12.8 2.6 %collective-permute-start.3 = (f32[160,128]{1,0:T(8,128)S(1)}, f32[160,128]{1,0:T(8,128)S(1)}, u32[]{:S(2)}, u32[]{:S(2)}) collective-permute-start(f32[160,128]{1,0:T(8,128)S(1)} %get-tuple-element.41), channel_id=1, source_target_pairs={{0,2},{1,3},{2,0},{3,1},{4,6},{5,7},{6,4},{7,5},{8,10},{9,11},{10,... | collective-permute-start | bytes 245768 | tf_op jit(solution)/shard_map/ppermute | solution.py:501
  15.4 0.2 collective-permute-start.4
  15.6 0.0 collective-permute-done.refs_1_
  15.7 0.7 %collective-permute-start.6 = (f32[128,128]{1,0:T(8,128)S(1)}, f32[128,128]{1,0:T(8,128)S(1)}, u32[]{:S(2)}, u32[]{:S(2)}) collective-permute-start(f32[128,128]{1,0:T(8,128)S(1)} %get-tuple-element.43.refs_11_), channel_id=1, source_target_pairs={{28,30},{29,31},{30,28},{31,29}} | collective-permute-start | bytes 196616 | tf_op jit(solution)/shard_map/ppermute | solution.py:471
  16.3 0.0 collective-permute-done.7.refs_14_
  16.3 0.7 %collective-permute-start.5 = (f32[128,128]{1,0:T(8,128)S(1)}, f32[128,128]{1,0:T(8,128)S(1)}, u32[]{:S(2)}, u32[]{:S(2)}) collective-permute-start(f32[128,128]{1,0:T(8,128)S(1)} %get-tuple-element.43.refs_11_), channel_id=1, source_target_pairs={{28,29},{29,28},{30,31},{31,30}} | collective-permute-start | bytes 196616 | tf_op jit(solution)/shard_map/ppermute | solution.py:471
  17.0 0.0 collective-permute-done.6.refs_13_
  17.0 0.0 collective-permute-done.5.refs_12_
  17.0 0.0 collective-permute-done.2.refs_8_
  17.0 3.0 %collective-permute-done.3.refs_9_ = f32[160,128]{1,0:T(8,128)S(1)} collective-permute-done((f32[160,128]{1,0:T(8,128)S(1)}, f32[160,128]{1,0:T(8,128)S(1)}, u32[]{:S(2)}, u32[]{:S(2)}) %collective-permute-start.3) | collective-permute-done | bytes 81952 | tf_op jit(solution)/shard_map/ppermute | solution.py:501
  20.0 1.7 %collective-permute-done.4.refs_10_ = f32[160,128]{1,0:T(8,128)S(1)} collective-permute-done((f32[160,128]{1,0:T(8,128)S(1)}, f32[160,128]{1,0:T(8,128)S(1)}, u32[]{:S(2)}, u32[]{:S(2)}) %collective-permute-start.4) | collective-permute-done | bytes 81952 | tf_op jit(solution)/shard_map/ppermute | solution.py:501
  21.8 1.4 %backward.1 = (f32[4,32,128]{2,1,0:T(8,128)S(1)}, f32[4,32,128]{2,1,0:T(8,128)S(1)}, f32[4,32,128]{2,1,0:T(8,128)S(1)}, f32[4,32,128]{2,1,0:T(8,128)S(1)}, f32[32,128]{1,0:T(8,128)S(1)}) custom-call(f32[128,128]{1,0:T(8,128)S(1)} %get-tuple-element.31.refs_0_, f32[128,128]{1,0:T(8,128)S(1)} %collective-permute-done.refs_1_, ...), custom_call_target="tpu_custom_call" | custom-call | tf_op jit(solution)/shard_map/backward/pallas_call | solution.py:503
  23.2 0.6 %collective-permute-start.9 = (f32[4,32,128]{2,1,0:T(8,128)S(1)}, f32[4,32,128]{2,1,0:T(8,128)S(1)}, u32[]{:S(2)}, u32[]{:S(2)}) collective-permute-start(f32[4,32,128]{2,1,0:T(8,128)S(1)} %get-tuple-element.46), channel_id=1, source_target_pairs={{0,1},{1,0},{2,7},{3,6},{4,5},{5,4},{6,11},{7,10},{8,9},{9,8},{10,... | collective-permute-start | bytes 196616 | tf_op jit(solution)/shard_map/ppermute | solution.py:523
  23.8 0.7 %collective-permute-start.10 = (f32[4,32,128]{2,1,0:T(8,128)S(1)}, f32[4,32,128]{2,1,0:T(8,128)S(1)}, u32[]{:S(2)}, u32[]{:S(2)}) collective-permute-start(f32[4,32,128]{2,1,0:T(8,128)S(1)} %get-tuple-element.47), channel_id=1, source_target_pairs={{0,6},{1,7},{2,0},{3,1},{4,10},{5,11},{6,4},{7,5},{8,14},{9,15},{1... | collective-permute-start | bytes 196616 | tf_op jit(solution)/shard_map/ppermute | solution.py:523
  24.5 1.8 %collective-permute-start.11 = (f32[4,32,128]{2,1,0:T(8,128)S(1)}, f32[4,32,128]{2,1,0:T(8,128)S(1)}, u32[]{:S(2)}, u32[]{:S(2)}) collective-permute-start(f32[4,32,128]{2,1,0:T(8,128)S(1)} %get-tuple-element.48), channel_id=1, source_target_pairs={{0,7},{1,6},{2,1},{3,0},{4,11},{5,10},{6,5},{7,4},{8,15},{9,14},{1... | collective-permute-start | bytes 196616 | tf_op jit(solution)/shard_map/ppermute | solution.py:523
  26.2 0.7 %collective-permute-start.8 = (f32[4,32,128]{2,1,0:T(8,128)S(1)}, f32[4,32,128]{2,1,0:T(8,128)S(1)}, u32[]{:S(2)}, u32[]{:S(2)}) collective-permute-start(f32[4,32,128]{2,1,0:T(8,128)S(1)} %get-tuple-element.45.refs_2_), channel_id=1, source_target_pairs={{2,6},{3,7},{6,10},{7,11},{10,14},{11,15},{14,18},{15,19},{18,22},... | collective-permute-start | bytes 196616 | tf_op jit(solution)/shard_map/ppermute | solution.py:523
  26.9 0.6 %collective-permute-done.9.refs_4_ = f32[4,32,128]{2,1,0:T(8,128)S(1)} collective-permute-done((f32[4,32,128]{2,1,0:T(8,128)S(1)}, f32[4,32,128]{2,1,0:T(8,128)S(1)}, u32[]{:S(2)}, u32[]{:S(2)}) %collective-permute-start.9) | collective-permute-done | bytes 65568 | tf_op jit(solution)/shard_map/ppermute | solution.py:523
  27.5 4.8 %collective-permute-done.10.refs_5_ = f32[4,32,128]{2,1,0:T(8,128)S(1)} collective-permute-done((f32[4,32,128]{2,1,0:T(8,128)S(1)}, f32[4,32,128]{2,1,0:T(8,128)S(1)}, u32[]{:S(2)}, u32[]{:S(2)}) %collective-permute-start.10) | collective-permute-done | bytes 65568 | tf_op jit(solution)/shard_map/ppermute | solution.py:523
  32.3 0.0 collective-permute-done.11.refs_6_
  32.3 0.0 collective-permute-done.8.refs_3_
  32.4 4.3 %collective-permute-start.14 = (f32[4,32,128]{2,1,0:T(8,128)S(1)}, f32[4,32,128]{2,1,0:T(8,128)S(1)}, u32[]{:S(2)}, u32[]{:S(2)}) collective-permute-start(f32[4,32,128]{2,1,0:T(8,128)S(1)} %update.1.refs_0_), channel_id=1, source_target_pairs={{0,3},{1,2},{2,1},{3,0},{4,7},{5,6},{6,5},{7,4},{8,11},{9,10},{10,... | collective-permute-start | bytes 196616 | tf_op jit(solution)/shard_map/ppermute | solution.py:536
  36.6 1.3 %collective-permute-start.13 = (f32[4,32,128]{2,1,0:T(8,128)S(1)}, f32[4,32,128]{2,1,0:T(8,128)S(1)}, u32[]{:S(2)}, u32[]{:S(2)}) collective-permute-start(f32[4,32,128]{2,1,0:T(8,128)S(1)} %update.1.refs_0_), channel_id=1, source_target_pairs={{0,2},{1,3},{2,0},{3,1},{4,6},{5,7},{6,4},{7,5},{8,10},{9,11},{10,... | collective-permute-start | bytes 196616 | tf_op jit(solution)/shard_map/ppermute | solution.py:536
  37.9 0.5 %collective-permute-start.12 = (f32[4,32,128]{2,1,0:T(8,128)S(1)}, f32[4,32,128]{2,1,0:T(8,128)S(1)}, u32[]{:S(2)}, u32[]{:S(2)}) collective-permute-start(f32[4,32,128]{2,1,0:T(8,128)S(1)} %update.1.refs_0_), channel_id=1, source_target_pairs={{0,1},{1,0},{2,3},{3,2},{4,5},{5,4},{6,7},{7,6},{8,9},{9,8},{10,11... | collective-permute-start | bytes 196616 | tf_op jit(solution)/shard_map/ppermute | solution.py:536
  38.4 1.2 %collective-permute-done.14.refs_3_ = f32[4,32,128]{2,1,0:T(8,128)S(1)} collective-permute-done((f32[4,32,128]{2,1,0:T(8,128)S(1)}, f32[4,32,128]{2,1,0:T(8,128)S(1)}, u32[]{:S(2)}, u32[]{:S(2)}) %collective-permute-start.14) | collective-permute-done | bytes 65568 | tf_op jit(solution)/shard_map/ppermute | solution.py:536
  39.5 2.3 %collective-permute-done.13.refs_2_ = f32[4,32,128]{2,1,0:T(8,128)S(1)} collective-permute-done((f32[4,32,128]{2,1,0:T(8,128)S(1)}, f32[4,32,128]{2,1,0:T(8,128)S(1)}, u32[]{:S(2)}, u32[]{:S(2)}) %collective-permute-start.13) | collective-permute-done | bytes 65568 | tf_op jit(solution)/shard_map/ppermute | solution.py:536
  41.8 0.7 %collective-permute-done.12.refs_1_ = f32[4,32,128]{2,1,0:T(8,128)S(1)} collective-permute-done((f32[4,32,128]{2,1,0:T(8,128)S(1)}, f32[4,32,128]{2,1,0:T(8,128)S(1)}, u32[]{:S(2)}, u32[]{:S(2)}) %collective-permute-start.12) | collective-permute-done | bytes 65568 | tf_op jit(solution)/shard_map/ppermute | solution.py:536
  42.5 0.8 %join.1 = f32[4,128,128]{2,1,0:T(8,128)} custom-call(f32[4,32,128]{2,1,0:T(8,128)S(1)} %update.1.refs_0_, f32[4,32,128]{2,1,0:T(8,128)S(1)} %collective-permute-done.12.refs_1_, f32[4,32,128]{2,1,0:T(8,128)S(1)} %collective-permute-done.13.refs_2_, f32[4,32,128]{2,1,0:T(8,128)S(1)} %collective-permute-done.14.refs_3_), custom_call_target="tpu_custom_call" | custom-call | tf_op jit(solution)/shard_map/join/pallas_call | solution.py:537
  (1 shorter events, 0.0 us)
Async XLA Ops:
  0.0 9.6 %collective-permute-start.1 = (f32[4,128,128]{2,1,0:T(8,128)}, f32[4,128,128]{2,1,0:T(8,128)S(1)}, u32[]{:S(2)}, u32[]{:S(2)}) collective-permute-start(f32[4,128,128]{2,1,0:T(8,128)} %maps_any.1), channel_id=1, source_target_pairs={{0,28},{4,0},{8,4},{12,8},{16,12},{20,16},{24,20},{28,24},{1,29},{... | collective-permute-start | bytes 786440 | tf_op jit(solution)/shard_map/ppermute | solution.py:437
  7.1 8.6 %collective-permute-start = (f32[128,128]{1,0:T(8,128)S(1)}, f32[128,128]{1,0:T(8,128)S(1)}, u32[]{:S(2)}, u32[]{:S(2)}) collective-permute-start(f32[128,128]{1,0:T(8,128)S(1)} %get-tuple-element.32), channel_id=1, source_target_pairs={{0,28},{4,0},{8,4},{12,8},{16,12},{20,16},{24,20},{28,24},{1,29},{... | collective-permute-start | bytes 196616 | tf_op jit(solution)/shard_map/ppermute | solution.py:485
  8.9 7.4 %collective-permute-start.7 = (f32[128,128]{1,0:T(8,128)S(1)}, f32[128,128]{1,0:T(8,128)S(1)}, u32[]{:S(2)}, u32[]{:S(2)}) collective-permute-start(f32[128,128]{1,0:T(8,128)S(1)} %get-tuple-element.43.refs_11_), channel_id=1, source_target_pairs={{28,31},{29,30},{30,29},{31,28}} | collective-permute-start | bytes 196616 | tf_op jit(solution)/shard_map/ppermute | solution.py:471
  11.2 5.8 %collective-permute-start.2 = (f32[160,128]{1,0:T(8,128)S(1)}, f32[160,128]{1,0:T(8,128)S(1)}, u32[]{:S(2)}, u32[]{:S(2)}) collective-permute-start(f32[160,128]{1,0:T(8,128)S(1)} %get-tuple-element.40), channel_id=1, source_target_pairs={{0,1},{1,0},{2,3},{3,2},{4,5},{5,4},{6,7},{7,6},{8,9},{9,8},{10,11... | collective-permute-start | bytes 245768 | tf_op jit(solution)/shard_map/ppermute | solution.py:501
  12.8 7.2 %collective-permute-start.3 = (f32[160,128]{1,0:T(8,128)S(1)}, f32[160,128]{1,0:T(8,128)S(1)}, u32[]{:S(2)}, u32[]{:S(2)}) collective-permute-start(f32[160,128]{1,0:T(8,128)S(1)} %get-tuple-element.41), channel_id=1, source_target_pairs={{0,2},{1,3},{2,0},{3,1},{4,6},{5,7},{6,4},{7,5},{8,10},{9,11},{10,... | collective-permute-start | bytes 245768 | tf_op jit(solution)/shard_map/ppermute | solution.py:501
  15.4 6.3 %collective-permute-start.4 = (f32[160,128]{1,0:T(8,128)S(1)}, f32[160,128]{1,0:T(8,128)S(1)}, u32[]{:S(2)}, u32[]{:S(2)}) collective-permute-start(f32[160,128]{1,0:T(8,128)S(1)} %get-tuple-element.42), channel_id=1, source_target_pairs={{0,3},{1,2},{2,1},{3,0},{4,7},{5,6},{6,5},{7,4},{8,11},{9,10},{10,... | collective-permute-start | bytes 245768 | tf_op jit(solution)/shard_map/ppermute | solution.py:501
  15.7 1.3 %collective-permute-start.6 = (f32[128,128]{1,0:T(8,128)S(1)}, f32[128,128]{1,0:T(8,128)S(1)}, u32[]{:S(2)}, u32[]{:S(2)}) collective-permute-start(f32[128,128]{1,0:T(8,128)S(1)} %get-tuple-element.43.refs_11_), channel_id=1, source_target_pairs={{28,30},{29,31},{30,28},{31,29}} | collective-permute-start | bytes 196616 | tf_op jit(solution)/shard_map/ppermute | solution.py:471
  16.3 0.7 %collective-permute-start.5 = (f32[128,128]{1,0:T(8,128)S(1)}, f32[128,128]{1,0:T(8,128)S(1)}, u32[]{:S(2)}, u32[]{:S(2)}) collective-permute-start(f32[128,128]{1,0:T(8,128)S(1)} %get-tuple-element.43.refs_11_), channel_id=1, source_target_pairs={{28,29},{29,28},{30,31},{31,30}} | collective-permute-start | bytes 196616 | tf_op jit(solution)/shard_map/ppermute | solution.py:471
  23.2 4.3 %collective-permute-start.9 = (f32[4,32,128]{2,1,0:T(8,128)S(1)}, f32[4,32,128]{2,1,0:T(8,128)S(1)}, u32[]{:S(2)}, u32[]{:S(2)}) collective-permute-start(f32[4,32,128]{2,1,0:T(8,128)S(1)} %get-tuple-element.46), channel_id=1, source_target_pairs={{0,1},{1,0},{2,7},{3,6},{4,5},{5,4},{6,11},{7,10},{8,9},{9,8},{10,... | collective-permute-start | bytes 196616 | tf_op jit(solution)/shard_map/ppermute | solution.py:523
  23.8 8.5 %collective-permute-start.10 = (f32[4,32,128]{2,1,0:T(8,128)S(1)}, f32[4,32,128]{2,1,0:T(8,128)S(1)}, u32[]{:S(2)}, u32[]{:S(2)}) collective-permute-start(f32[4,32,128]{2,1,0:T(8,128)S(1)} %get-tuple-element.47), channel_id=1, source_target_pairs={{0,6},{1,7},{2,0},{3,1},{4,10},{5,11},{6,4},{7,5},{8,14},{9,15},{1... | collective-permute-start | bytes 196616 | tf_op jit(solution)/shard_map/ppermute | solution.py:523
  24.5 7.8 %collective-permute-start.11 = (f32[4,32,128]{2,1,0:T(8,128)S(1)}, f32[4,32,128]{2,1,0:T(8,128)S(1)}, u32[]{:S(2)}, u32[]{:S(2)}) collective-permute-start(f32[4,32,128]{2,1,0:T(8,128)S(1)} %get-tuple-element.48), channel_id=1, source_target_pairs={{0,7},{1,6},{2,1},{3,0},{4,11},{5,10},{6,5},{7,4},{8,15},{9,14},{1... | collective-permute-start | bytes 196616 | tf_op jit(solution)/shard_map/ppermute | solution.py:523
  26.2 6.1 %collective-permute-start.8 = (f32[4,32,128]{2,1,0:T(8,128)S(1)}, f32[4,32,128]{2,1,0:T(8,128)S(1)}, u32[]{:S(2)}, u32[]{:S(2)}) collective-permute-start(f32[4,32,128]{2,1,0:T(8,128)S(1)} %get-tuple-element.45.refs_2_), channel_id=1, source_target_pairs={{2,6},{3,7},{6,10},{7,11},{10,14},{11,15},{14,18},{15,19},{18,22},... | collective-permute-start | bytes 196616 | tf_op jit(solution)/shard_map/ppermute | solution.py:523
  32.4 7.2 %collective-permute-start.14 = (f32[4,32,128]{2,1,0:T(8,128)S(1)}, f32[4,32,128]{2,1,0:T(8,128)S(1)}, u32[]{:S(2)}, u32[]{:S(2)}) collective-permute-start(f32[4,32,128]{2,1,0:T(8,128)S(1)} %update.1.refs_0_), channel_id=1, source_target_pairs={{0,3},{1,2},{2,1},{3,0},{4,7},{5,6},{6,5},{7,4},{8,11},{9,10},{10,... | collective-permute-start | bytes 196616 | tf_op jit(solution)/shard_map/ppermute | solution.py:536
  36.6 5.2 %collective-permute-start.13 = (f32[4,32,128]{2,1,0:T(8,128)S(1)}, f32[4,32,128]{2,1,0:T(8,128)S(1)}, u32[]{:S(2)}, u32[]{:S(2)}) collective-permute-start(f32[4,32,128]{2,1,0:T(8,128)S(1)} %update.1.refs_0_), channel_id=1, source_target_pairs={{0,2},{1,3},{2,0},{3,1},{4,6},{5,7},{6,4},{7,5},{8,10},{9,11},{10,... | collective-permute-start | bytes 196616 | tf_op jit(solution)/shard_map/ppermute | solution.py:536
  37.9 4.6 %collective-permute-start.12 = (f32[4,32,128]{2,1,0:T(8,128)S(1)}, f32[4,32,128]{2,1,0:T(8,128)S(1)}, u32[]{:S(2)}, u32[]{:S(2)}) collective-permute-start(f32[4,32,128]{2,1,0:T(8,128)S(1)} %update.1.refs_0_), channel_id=1, source_target_pairs={{0,1},{1,0},{2,3},{3,2},{4,5},{5,4},{6,7},{7,6},{8,9},{9,8},{10,11... | collective-permute-start | bytes 196616 | tf_op jit(solution)/shard_map/ppermute | solution.py:536

commit v5 on v4

--- a/solution.py
+++ b/solution.py
@@ -260,7 +260,9 @@
     return jnp.dot(beside, right, preferred_element_type=f32)[: len(fields) * length]
 
 
-def forward_kernel(count, near, halo, probe, table, coef, power, psi, far, *rest):
+def forward_kernel(
+    count, near, halo, probe, table, coef, power, total_edge, other_edge, psi, far, pair_edge, *rest
+):
     messages, (beyond, total) = rest[:count], rest[count:]
     materials, length, _ = halo.shape
     half = length // 2
@@ -296,6 +298,11 @@
         total[...] += coef[s, 4 * materials : 4 * materials + 1] * (re * re + im * im)
 
     edge = lax.axis_index("tile") == lax.axis_size("tile") - 1
+
+    @pl.when(edge)
+    def _():
+        pair_edge[...] = total_edge[...] + other_edge[...]
+
     for joined in (False, True):
 
         @pl.when(edge == joined)
@@ -312,7 +319,7 @@
 
 def backward_kernel(tiles, count, right_root, left_root, table, coef, psi, far, far_edge, *rest):
     shares, rest = rest[:count], rest[count:]
-    edges, rest = rest[:count], rest[count:]
+    edges, rest = rest[: count // 2], rest[count // 2 :]
     sends, rest = rest[:count], rest[count:]
     scale, shortfall, gradient, back = rest
     length = right_root.shape[0]
@@ -464,11 +471,13 @@
         cost_estimate=pl.CostEstimate(flops=10**9, bytes_accessed=2**22, transcendentals=0),
         name="tables",
     )(*map(in_hbm, (spectrum, wave_index, edge_band.T, band_first, maps, probe)))
-    edges = [total_edge]
+    both = ("tile", "wave")
     last = (tiles - 1) * count
-    for k in range(1, count):
-        pairs = [(last + w, last + (w ^ k)) for w in range(count)]
-        edges.append(lax.ppermute(total_edge, ("tile", "wave"), pairs))
+
+    def among_last(array, k):
+        return lax.ppermute(array, both, [(last + w, last + (w ^ k)) for w in range(count)])
+
+    other_edge = among_last(total_edge, 1)
     here, power, left, right_root = pl.pallas_call(
         lambda *refs: power_kernel(count, *refs),
         out_shape=(share, square, square, square),
@@ -484,26 +493,27 @@
     )(*map(in_hbm, (offsets, measured)), coef, near_probe, own)
     left_root = lax.ppermute(left, "tile", ring)
     message = shape((length + half_rows, length), f32)
-    psi, far, *messages = pl.pallas_call(
+    psi, far, pair_edge, *messages = pl.pallas_call(
         lambda *refs: forward_kernel(count, *refs),
-        out_shape=(shape(probe.shape, f32), field) + (message,) * count,
-        in_specs=[VM] * 6,
-        out_specs=(VM,) * (2 + count),
+        out_shape=(shape(probe.shape, f32), field, square) + (message,) * count,
+        in_specs=[VM] * 8,
+        out_specs=(VM,) * (3 + count),
         scratch_shapes=[
             pltpu.VMEM((materials, half, length), f32),
             pltpu.VMEM((length, length), f32),
         ],
         compiler_params=params(),
         name="forward",
-    )(near, halo, near_probe, table, coef, power)
+    )(near, halo, near_probe, table, coef, power, total_edge, other_edge)
     shares = [messages[0]]
     for k in range(1, count):
         shares.append(lax.ppermute(messages[k], "wave", [(w, w ^ k) for w in range(count)]))
+    edges = [pair_edge] + [among_last(pair_edge, k) for k in range(2, count, 2)]
 
     *sends, scale = pl.pallas_call(
         lambda *refs: backward_kernel(tiles, count, *refs),
         out_shape=(share,) * count + (shape((half_rows, length), f32),),
-        in_specs=[VM] * (7 + 2 * count),
+        in_specs=[VM] * (7 + count + len(edges)),
         out_specs=(VM,) * (count + 1),
         scratch_shapes=[
             pltpu.VMEM((2 * length, length), f32),
@@ -520,7 +530,7 @@
     arrived = []
     for k in range(count):
         pairs = [(t * count + w, owner(t, w ^ k)) for t in range(tiles) for w in range(count)]
-        arrived.append(lax.ppermute(sends[k], ("tile", "wave"), [p for p in pairs if p[0] != p[1]]))
+        arrived.append(lax.ppermute(sends[k], both, [p for p in pairs if p[0] != p[1]]))
 
     new = pl.pallas_call(
         lambda *refs: update_kernel(count, *refs),

time: 43.8 us -> 41.5 us (0.947)
  waiting for transfers between devices: 14.3 us -> 11.3 us
  starting transfers between devices: 21.3 us -> 22.2 us
    ppermute x3, waiting for transfers between devices: 4.75 us -> 0.01 us  [per_device(): lax.ppermute(messages[k], 'wave', [(w, w ^ k) for w in range(count)])]
    ppermute x1, starting transfers between devices: 1.85 us -> 4.44 us  [per_device(): left_root = lax.ppermute(left, 'tile', ring)]
    ppermute x1, waiting for transfers between devices: 0.01 us -> 1.25 us  [per_device(): left_root = lax.ppermute(left, 'tile', ring)]
    ppermute x3, starting transfers between devices: 6.03 us -> 4.89 us  [per_device(): parts.append(lax.ppermute(new, 'wave', [(w, w ^ k) for w in range(count)]))]
    ppermute x3, waiting for transfers between devices: 4.12 us -> 4.77 us  [per_device(): parts.append(lax.ppermute(new, 'wave', [(w, w ^ k) for w in range(count)]))]
    ppermute x7 -> x6, starting transfers between devices: 5.66 us -> 5.09 us  [the longest x4 3.77 us: per_device(): lax.ppermute(sends[k], both, [p for p in pairs if p[0] != p[1]])]
    ppermute x7 -> x6, waiting for transfers between devices: 5.44 us -> 5.25 us  [the longest x4 5.25 us: per_device(): lax.ppermute(sends[k], both, [p for p in pairs if p[0] != p[1]])]
  transfers between devices with their start and end apart: 15 -> 14, of which waited for: 7 -> 5; matrix products, arithmetic and copies ran while one was open for 0% -> 0% of each run, Pallas kernels for 12% -> 9%
where the time goes in v5:
time: 41.5 us; the launch traced here: 41.2 us
  starting transfers between devices  22.2 us (53%)
  waiting for transfers between devices  11.3 us (27%)
  Pallas kernels  7.6 us (18%)
    ppermute x4, waiting for transfers between devices, per_device(): lax.ppermute(sends[k], both, [p for p in pairs if p[0] != p[1]])  5.25 us
    ppermute x3, starting transfers between devices, per_device(): parts.append(lax.ppermute(new, 'wave', [(w, w ^ k) for w in range(count)]))  4.89 us
    ppermute x3, waiting for transfers between devices, per_device(): parts.append(lax.ppermute(new, 'wave', [(w, w ^ k) for w in range(count)]))  4.77 us
    ppermute x3, starting transfers between devices, per_device(): lax.ppermute(messages[k], 'wave', [(w, w ^ k) for w in range(count)])  4.45 us
    ppermute x1, starting transfers between devices, per_device(): left_root = lax.ppermute(left, 'tile', ring)  4.44 us
    ppermute x4, starting transfers between devices, per_device(): lax.ppermute(sends[k], both, [p for p in pairs if p[0] != p[1]])  3.77 us
    ppermute x1, starting transfers between devices, per_device(): halo = lax.ppermute(maps, 'tile', ring)  3.33 us
    pallas_call x1, Pallas kernels, per_device(): pl.pallas_call(first_kernel, out_shape=(shape((slots, 3, length, length),...  2.76 us
  transfers between devices with their start and end apart: 14, of which 5 were waited for; matrix products, arithmetic and copies ran while one was open for 0% of the time, Pallas kernels for 9%

profile of v5, /device:TPU:0, one launch (start us, length us, event | category | flops | bytes accessed | tf_op | source)
XLA Modules:
  0.0 41.2 jit_solution(17901205526289596451)
XLA Ops:
  0.0 3.3 %collective-permute-start.1 = (f32[4,128,128]{2,1,0:T(8,128)}, f32[4,128,128]{2,1,0:T(8,128)S(1)}, u32[]{:S(2)}, u32[]{:S(2)}) collective-permute-start(f32[4,128,128]{2,1,0:T(8,128)} %maps_any.1), channel_id=1, source_target_pairs={{0,28},{4,0},{8,4},{12,8},{16,12},{20,16},{24,20},{28,24},{1,29},{... | collective-permute-start | bytes 786440 | tf_op jit(solution)/shard_map/ppermute | solution.py:444
  3.3 2.8 %tables.1 = (bf16[12,3,128,128]{3,2,1,0:T(8,128)(2,1)S(1)}, f32[12,24,128]{2,1,0:T(8,128)S(1)}, f32[12,2,128,128]{3,2,1,0:T(8,128)S(1)}, f32[12,2,128,128]{3,2,1...) custom-call(f32[12]{0:T(128)} %spectrum_any.1, s32[12]{0:T(128)} %wave_any.1, ...), custom_call_target="tpu_custom_call" | custom-call | flops 1000000000 | bytes 4194304 | tf_op jit(solution)/shard_map/tables/pallas_call | solution.py:448
  6.1 0.7 %collective-permute-start.2 = (f32[128,128]{1,0:T(8,128)S(1)}, f32[128,128]{1,0:T(8,128)S(1)}, u32[]{:S(2)}, u32[]{:S(2)}) collective-permute-start(f32[128,128]{1,0:T(8,128)S(1)} %get-tuple-element.37.refs_6_), channel_id=1, source_target_pairs={{28,29},{29,28},{30,31},{31,30}} | collective-permute-start | bytes 196616 | tf_op jit(solution)/shard_map/ppermute | solution.py:478
  6.8 1.0 %power.1 = (f32[4,32,128]{2,1,0:T(8,128)S(1)}, f32[128,128]{1,0:T(8,128)S(1)}, f32[128,128]{1,0:T(8,128)S(1)}, f32[128,128]{1,0:T(8,128)S(1)}) custom-call(s32[2]{0:T(128)} %refs_0_.1, f32[2,128,128]{2,1,0:T(8,128)} %refs_1_.1, f32[12,24,128]{2,1,0:T(8,128)S(1)} %get-tuple-element.28.refs_2_.refs_4_.refs_3_, ...), custom_call_target="tpu_custom_call" | custom-call | tf_op jit(solution)/shard_map/power/pallas_call | solution.py:481
  7.7 0.0 collective-permute-done.2.refs_7_
  7.8 0.0 collective-permute-done.1.refs_1_
  7.8 1.6 %forward.1 = (f32[12,2,128,128]{3,2,1,0:T(8,128)S(1)}, f32[12,128,256]{2,1,0:T(8,128)S(1)}, f32[128,128]{1,0:T(8,128)S(1)}, f32[160,128]{1,0:T(8,128)S(1)}, f32[...) custom-call(f32[12,2,128,128]{3,2,1,0:T(8,128)S(1)} %get-tuple-element.35.refs_0_, ...), custom_call_target="tpu_custom_call" | custom-call | tf_op jit(solution)/shard_map/forward/pallas_call | solution.py:496
  9.4 1.6 %collective-permute-start.3 = (f32[160,128]{1,0:T(8,128)S(1)}, f32[160,128]{1,0:T(8,128)S(1)}, u32[]{:S(2)}, u32[]{:S(2)}) collective-permute-start(f32[160,128]{1,0:T(8,128)S(1)} %get-tuple-element.42), channel_id=1, source_target_pairs={{0,1},{1,0},{2,3},{3,2},{4,5},{5,4},{6,7},{7,6},{8,9},{9,8},{10,11... | collective-permute-start | bytes 245768 | tf_op jit(solution)/shard_map/ppermute | solution.py:510
  11.0 2.6 %collective-permute-start.4 = (f32[160,128]{1,0:T(8,128)S(1)}, f32[160,128]{1,0:T(8,128)S(1)}, u32[]{:S(2)}, u32[]{:S(2)}) collective-permute-start(f32[160,128]{1,0:T(8,128)S(1)} %get-tuple-element.43), channel_id=1, source_target_pairs={{0,2},{1,3},{2,0},{3,1},{4,6},{5,7},{6,4},{7,5},{8,10},{9,11},{10,... | collective-permute-start | bytes 245768 | tf_op jit(solution)/shard_map/ppermute | solution.py:510
  13.6 0.2 collective-permute-start.5
  13.8 4.4 %collective-permute-start = (f32[128,128]{1,0:T(8,128)S(1)}, f32[128,128]{1,0:T(8,128)S(1)}, u32[]{:S(2)}, u32[]{:S(2)}) collective-permute-start(f32[128,128]{1,0:T(8,128)S(1)} %get-tuple-element.33), channel_id=1, source_target_pairs={{0,28},{4,0},{8,4},{12,8},{16,12},{20,16},{24,20},{28,24},{1,29},{... | collective-permute-start | bytes 196616 | tf_op jit(solution)/shard_map/ppermute | solution.py:494
  18.3 0.7 %collective-permute-start.6 = (f32[128,128]{1,0:T(8,128)S(1)}, f32[128,128]{1,0:T(8,128)S(1)}, u32[]{:S(2)}, u32[]{:S(2)}) collective-permute-start(f32[128,128]{1,0:T(8,128)S(1)} %get-tuple-element.45.refs_11_), channel_id=1, source_target_pairs={{28,30},{29,31},{30,28},{31,29}} | collective-permute-start | bytes 196616 | tf_op jit(solution)/shard_map/ppermute | solution.py:478
  18.9 1.2 %collective-permute-done.refs_1_ = f32[128,128]{1,0:T(8,128)S(1)} collective-permute-done((f32[128,128]{1,0:T(8,128)S(1)}, f32[128,128]{1,0:T(8,128)S(1)}, u32[]{:S(2)}, u32[]{:S(2)}) %collective-permute-start) | collective-permute-done | bytes 65568 | tf_op jit(solution)/shard_map/ppermute | solution.py:494
  20.2 0.0 collective-permute-done.6.refs_12_
  20.2 0.0 collective-permute-done.3.refs_8_
  20.2 0.0 collective-permute-done.4.refs_9_
  20.2 0.0 collective-permute-done.5.refs_10_
  20.2 1.4 %backward.1 = (f32[4,32,128]{2,1,0:T(8,128)S(1)}, f32[4,32,128]{2,1,0:T(8,128)S(1)}, f32[4,32,128]{2,1,0:T(8,128)S(1)}, f32[4,32,128]{2,1,0:T(8,128)S(1)}, f32[32,128]{1,0:T(8,128)S(1)}) custom-call(f32[128,128]{1,0:T(8,128)S(1)} %get-tuple-element.32.refs_0_, f32[128,128]{1,0:T(8,128)S(1)} %collective-permute-done.refs_1_, ...), custom_call_target="tpu_custom_call" | custom-call | tf_op jit(solution)/shard_map/backward/pallas_call | solution.py:513
  21.6 1.2 %collective-permute-start.8 = (f32[4,32,128]{2,1,0:T(8,128)S(1)}, f32[4,32,128]{2,1,0:T(8,128)S(1)}, u32[]{:S(2)}, u32[]{:S(2)}) collective-permute-start(f32[4,32,128]{2,1,0:T(8,128)S(1)} %get-tuple-element.48), channel_id=1, source_target_pairs={{0,1},{1,0},{2,7},{3,6},{4,5},{5,4},{6,11},{7,10},{8,9},{9,8},{10,... | collective-permute-start | bytes 196616 | tf_op jit(solution)/shard_map/ppermute | solution.py:533
  22.8 0.0 collective-permute-start.9
  22.8 1.9 %collective-permute-start.10 = (f32[4,32,128]{2,1,0:T(8,128)S(1)}, f32[4,32,128]{2,1,0:T(8,128)S(1)}, u32[]{:S(2)}, u32[]{:S(2)}) collective-permute-start(f32[4,32,128]{2,1,0:T(8,128)S(1)} %get-tuple-element.50), channel_id=1, source_target_pairs={{0,7},{1,6},{2,1},{3,0},{4,11},{5,10},{6,5},{7,4},{8,15},{9,14},{1... | collective-permute-start | bytes 196616 | tf_op jit(solution)/shard_map/ppermute | solution.py:533
  24.7 0.7 %collective-permute-start.7 = (f32[4,32,128]{2,1,0:T(8,128)S(1)}, f32[4,32,128]{2,1,0:T(8,128)S(1)}, u32[]{:S(2)}, u32[]{:S(2)}) collective-permute-start(f32[4,32,128]{2,1,0:T(8,128)S(1)} %get-tuple-element.47.refs_2_), channel_id=1, source_target_pairs={{2,6},{3,7},{6,10},{7,11},{10,14},{11,15},{14,18},{15,19},{18,22},... | collective-permute-start | bytes 196616 | tf_op jit(solution)/shard_map/ppermute | solution.py:533
  25.4 0.5 %collective-permute-done.8.refs_4_ = f32[4,32,128]{2,1,0:T(8,128)S(1)} collective-permute-done((f32[4,32,128]{2,1,0:T(8,128)S(1)}, f32[4,32,128]{2,1,0:T(8,128)S(1)}, u32[]{:S(2)}, u32[]{:S(2)}) %collective-permute-start.8) | collective-permute-done | bytes 65568 | tf_op jit(solution)/shard_map/ppermute | solution.py:533
  25.9 4.7 %collective-permute-done.9.refs_5_ = f32[4,32,128]{2,1,0:T(8,128)S(1)} collective-permute-done((f32[4,32,128]{2,1,0:T(8,128)S(1)}, f32[4,32,128]{2,1,0:T(8,128)S(1)}, u32[]{:S(2)}, u32[]{:S(2)}) %collective-permute-start.9) | collective-permute-done | bytes 65568 | tf_op jit(solution)/shard_map/ppermute | solution.py:533
  30.6 0.0 collective-permute-done.10.refs_6_
  30.6 0.0 collective-permute-done.7.refs_3_
  30.7 4.2 %collective-permute-start.13 = (f32[4,32,128]{2,1,0:T(8,128)S(1)}, f32[4,32,128]{2,1,0:T(8,128)S(1)}, u32[]{:S(2)}, u32[]{:S(2)}) collective-permute-start(f32[4,32,128]{2,1,0:T(8,128)S(1)} %update.1.refs_0_), channel_id=1, source_target_pairs={{0,3},{1,2},{2,1},{3,0},{4,7},{5,6},{6,5},{7,4},{8,11},{9,10},{10,... | collective-permute-start | bytes 196616 | tf_op jit(solution)/shard_map/ppermute | solution.py:546
  34.9 0.0 collective-permute-start.12
  34.9 0.6 %collective-permute-start.11 = (f32[4,32,128]{2,1,0:T(8,128)S(1)}, f32[4,32,128]{2,1,0:T(8,128)S(1)}, u32[]{:S(2)}, u32[]{:S(2)}) collective-permute-start(f32[4,32,128]{2,1,0:T(8,128)S(1)} %update.1.refs_0_), channel_id=1, source_target_pairs={{0,1},{1,0},{2,3},{3,2},{4,5},{5,4},{6,7},{7,6},{8,9},{9,8},{10,11... | collective-permute-start | bytes 196616 | tf_op jit(solution)/shard_map/ppermute | solution.py:546
  35.6 1.9 %collective-permute-done.13.refs_3_ = f32[4,32,128]{2,1,0:T(8,128)S(1)} collective-permute-done((f32[4,32,128]{2,1,0:T(8,128)S(1)}, f32[4,32,128]{2,1,0:T(8,128)S(1)}, u32[]{:S(2)}, u32[]{:S(2)}) %collective-permute-start.13) | collective-permute-done | bytes 65568 | tf_op jit(solution)/shard_map/ppermute | solution.py:546
  37.5 2.8 %collective-permute-done.12.refs_2_ = f32[4,32,128]{2,1,0:T(8,128)S(1)} collective-permute-done((f32[4,32,128]{2,1,0:T(8,128)S(1)}, f32[4,32,128]{2,1,0:T(8,128)S(1)}, u32[]{:S(2)}, u32[]{:S(2)}) %collective-permute-start.12) | collective-permute-done | bytes 65568 | tf_op jit(solution)/shard_map/ppermute | solution.py:546
  40.3 0.0 collective-permute-done.11.refs_1_
  40.3 0.8 %join.1 = f32[4,128,128]{2,1,0:T(8,128)} custom-call(f32[4,32,128]{2,1,0:T(8,128)S(1)} %update.1.refs_0_, f32[4,32,128]{2,1,0:T(8,128)S(1)} %collective-permute-done.11.refs_1_, f32[4,32,128]{2,1,0:T(8,128)S(1)} %collective-permute-done.12.refs_2_, f32[4,32,128]{2,1,0:T(8,128)S(1)} %collective-permute-done.13.refs_3_), custom_call_target="tpu_custom_call" | custom-call | tf_op jit(solution)/shard_map/join/pallas_call | solution.py:547
  (1 shorter events, 0.0 us)
Async XLA Ops:
  0.0 7.8 %collective-permute-start.1 = (f32[4,128,128]{2,1,0:T(8,128)}, f32[4,128,128]{2,1,0:T(8,128)S(1)}, u32[]{:S(2)}, u32[]{:S(2)}) collective-permute-start(f32[4,128,128]{2,1,0:T(8,128)} %maps_any.1), channel_id=1, source_target_pairs={{0,28},{4,0},{8,4},{12,8},{16,12},{20,16},{24,20},{28,24},{1,29},{... | collective-permute-start | bytes 786440 | tf_op jit(solution)/shard_map/ppermute | solution.py:444
  6.1 1.6 %collective-permute-start.2 = (f32[128,128]{1,0:T(8,128)S(1)}, f32[128,128]{1,0:T(8,128)S(1)}, u32[]{:S(2)}, u32[]{:S(2)}) collective-permute-start(f32[128,128]{1,0:T(8,128)S(1)} %get-tuple-element.37.refs_6_), channel_id=1, source_target_pairs={{28,29},{29,28},{30,31},{31,30}} | collective-permute-start | bytes 196616 | tf_op jit(solution)/shard_map/ppermute | solution.py:478
  9.4 10.8 %collective-permute-start.3 = (f32[160,128]{1,0:T(8,128)S(1)}, f32[160,128]{1,0:T(8,128)S(1)}, u32[]{:S(2)}, u32[]{:S(2)}) collective-permute-start(f32[160,128]{1,0:T(8,128)S(1)} %get-tuple-element.42), channel_id=1, source_target_pairs={{0,1},{1,0},{2,3},{3,2},{4,5},{5,4},{6,7},{7,6},{8,9},{9,8},{10,11... | collective-permute-start | bytes 245768 | tf_op jit(solution)/shard_map/ppermute | solution.py:510
  11.0 9.2 %collective-permute-start.4 = (f32[160,128]{1,0:T(8,128)S(1)}, f32[160,128]{1,0:T(8,128)S(1)}, u32[]{:S(2)}, u32[]{:S(2)}) collective-permute-start(f32[160,128]{1,0:T(8,128)S(1)} %get-tuple-element.43), channel_id=1, source_target_pairs={{0,2},{1,3},{2,0},{3,1},{4,6},{5,7},{6,4},{7,5},{8,10},{9,11},{10,... | collective-permute-start | bytes 245768 | tf_op jit(solution)/shard_map/ppermute | solution.py:510
  13.6 6.6 %collective-permute-start.5 = (f32[160,128]{1,0:T(8,128)S(1)}, f32[160,128]{1,0:T(8,128)S(1)}, u32[]{:S(2)}, u32[]{:S(2)}) collective-permute-start(f32[160,128]{1,0:T(8,128)S(1)} %get-tuple-element.44), channel_id=1, source_target_pairs={{0,3},{1,2},{2,1},{3,0},{4,7},{5,6},{6,5},{7,4},{8,11},{9,10},{10,... | collective-permute-start | bytes 245768 | tf_op jit(solution)/shard_map/ppermute | solution.py:510
  13.8 6.3 %collective-permute-start = (f32[128,128]{1,0:T(8,128)S(1)}, f32[128,128]{1,0:T(8,128)S(1)}, u32[]{:S(2)}, u32[]{:S(2)}) collective-permute-start(f32[128,128]{1,0:T(8,128)S(1)} %get-tuple-element.33), channel_id=1, source_target_pairs={{0,28},{4,0},{8,4},{12,8},{16,12},{20,16},{24,20},{28,24},{1,29},{... | collective-permute-start | bytes 196616 | tf_op jit(solution)/shard_map/ppermute | solution.py:494
  18.3 1.9 %collective-permute-start.6 = (f32[128,128]{1,0:T(8,128)S(1)}, f32[128,128]{1,0:T(8,128)S(1)}, u32[]{:S(2)}, u32[]{:S(2)}) collective-permute-start(f32[128,128]{1,0:T(8,128)S(1)} %get-tuple-element.45.refs_11_), channel_id=1, source_target_pairs={{28,30},{29,31},{30,28},{31,29}} | collective-permute-start | bytes 196616 | tf_op jit(solution)/shard_map/ppermute | solution.py:478
  21.6 4.3 %collective-permute-start.8 = (f32[4,32,128]{2,1,0:T(8,128)S(1)}, f32[4,32,128]{2,1,0:T(8,128)S(1)}, u32[]{:S(2)}, u32[]{:S(2)}) collective-permute-start(f32[4,32,128]{2,1,0:T(8,128)S(1)} %get-tuple-element.48), channel_id=1, source_target_pairs={{0,1},{1,0},{2,7},{3,6},{4,5},{5,4},{6,11},{7,10},{8,9},{9,8},{10,... | collective-permute-start | bytes 196616 | tf_op jit(solution)/shard_map/ppermute | solution.py:533
  22.8 7.8 %collective-permute-start.9 = (f32[4,32,128]{2,1,0:T(8,128)S(1)}, f32[4,32,128]{2,1,0:T(8,128)S(1)}, u32[]{:S(2)}, u32[]{:S(2)}) collective-permute-start(f32[4,32,128]{2,1,0:T(8,128)S(1)} %get-tuple-element.49), channel_id=1, source_target_pairs={{0,6},{1,7},{2,0},{3,1},{4,10},{5,11},{6,4},{7,5},{8,14},{9,15},{1... | collective-permute-start | bytes 196616 | tf_op jit(solution)/shard_map/ppermute | solution.py:533
  22.8 7.8 %collective-permute-start.10 = (f32[4,32,128]{2,1,0:T(8,128)S(1)}, f32[4,32,128]{2,1,0:T(8,128)S(1)}, u32[]{:S(2)}, u32[]{:S(2)}) collective-permute-start(f32[4,32,128]{2,1,0:T(8,128)S(1)} %get-tuple-element.50), channel_id=1, source_target_pairs={{0,7},{1,6},{2,1},{3,0},{4,11},{5,10},{6,5},{7,4},{8,15},{9,14},{1... | collective-permute-start | bytes 196616 | tf_op jit(solution)/shard_map/ppermute | solution.py:533
  24.7 5.9 %collective-permute-start.7 = (f32[4,32,128]{2,1,0:T(8,128)S(1)}, f32[4,32,128]{2,1,0:T(8,128)S(1)}, u32[]{:S(2)}, u32[]{:S(2)}) collective-permute-start(f32[4,32,128]{2,1,0:T(8,128)S(1)} %get-tuple-element.47.refs_2_), channel_id=1, source_target_pairs={{2,6},{3,7},{6,10},{7,11},{10,14},{11,15},{14,18},{15,19},{18,22},... | collective-permute-start | bytes 196616 | tf_op jit(solution)/shard_map/ppermute | solution.py:533
  30.7 6.8 %collective-permute-start.13 = (f32[4,32,128]{2,1,0:T(8,128)S(1)}, f32[4,32,128]{2,1,0:T(8,128)S(1)}, u32[]{:S(2)}, u32[]{:S(2)}) collective-permute-start(f32[4,32,128]{2,1,0:T(8,128)S(1)} %update.1.refs_0_), channel_id=1, source_target_pairs={{0,3},{1,2},{2,1},{3,0},{4,7},{5,6},{6,5},{7,4},{8,11},{9,10},{10,... | collective-permute-start | bytes 196616 | tf_op jit(solution)/shard_map/ppermute | solution.py:546
  34.9 5.4 %collective-permute-start.12 = (f32[4,32,128]{2,1,0:T(8,128)S(1)}, f32[4,32,128]{2,1,0:T(8,128)S(1)}, u32[]{:S(2)}, u32[]{:S(2)}) collective-permute-start(f32[4,32,128]{2,1,0:T(8,128)S(1)} %update.1.refs_0_), channel_id=1, source_target_pairs={{0,2},{1,3},{2,0},{3,1},{4,6},{5,7},{6,4},{7,5},{8,10},{9,11},{10,... | collective-permute-start | bytes 196616 | tf_op jit(solution)/shard_map/ppermute | solution.py:546
  34.9 5.4 %collective-permute-start.11 = (f32[4,32,128]{2,1,0:T(8,128)S(1)}, f32[4,32,128]{2,1,0:T(8,128)S(1)}, u32[]{:S(2)}, u32[]{:S(2)}) collective-permute-start(f32[4,32,128]{2,1,0:T(8,128)S(1)} %update.1.refs_0_), channel_id=1, source_target_pairs={{0,1},{1,0},{2,3},{3,2},{4,5},{5,4},{6,7},{7,6},{8,9},{9,8},{10,11... | collective-permute-start | bytes 196616 | tf_op jit(solution)/shard_map/ppermute | solution.py:546

commit v6 on v4

--- a/solution.py
+++ b/solution.py
@@ -133,7 +133,7 @@
                 table[s, 2, at, :] = positive.astype(bf16)
         return carry
 
-    lax.fori_loop(0, slots, tables, 0, unroll=2)
+    lax.fori_loop(0, slots, tables, 0, unroll=6)
 
     for copy in copies[1:]:
         copy.wait()
@@ -158,7 +158,7 @@
                 near[s, i, half + start : half + start + CHUNK] = pltpu.roll(part, half, 1)
         return carry
 
-    lax.fori_loop(0, slots, near_object, 0, unroll=2)
+    lax.fori_loop(0, slots, near_object, 0, unroll=6)
 
     @pl.when(lax.axis_index("tile") == lax.axis_size("tile") - 1)
     def _():
@@ -296,6 +296,7 @@
         total[...] += coef[s, 4 * materials : 4 * materials + 1] * (re * re + im * im)
 
     edge = lax.axis_index("tile") == lax.axis_size("tile") - 1
+
     for joined in (False, True):
 
         @pl.when(edge == joined)
@@ -310,9 +311,13 @@
         message[length:] = piece(power, jnp.bitwise_xor(me, k), count, half_rows)
 
 
+def add_kernel(one, other, _, out):
+    out[...] = one[...] + other[...]
+
+
 def backward_kernel(tiles, count, right_root, left_root, table, coef, psi, far, far_edge, *rest):
     shares, rest = rest[:count], rest[count:]
-    edges, rest = rest[:count], rest[count:]
+    edges, rest = rest[: count // 2], rest[count // 2 :]
     sends, rest = rest[:count], rest[count:]
     scale, shortfall, gradient, back = rest
     length = right_root.shape[0]
@@ -430,6 +435,7 @@
     half = length // 2
     shape = jax.ShapeDtypeStruct
     half_rows = length // count
+    partners = [count // 2] + [k for k in range(1, count) if k != count // 2]
     square = shape((length, length), f32)
     share = shape((materials, half_rows, length), f32)
 
@@ -464,11 +470,13 @@
         cost_estimate=pl.CostEstimate(flops=10**9, bytes_accessed=2**22, transcendentals=0),
         name="tables",
     )(*map(in_hbm, (spectrum, wave_index, edge_band.T, band_first, maps, probe)))
-    edges = [total_edge]
+    both = ("tile", "wave")
     last = (tiles - 1) * count
-    for k in range(1, count):
-        pairs = [(last + w, last + (w ^ k)) for w in range(count)]
-        edges.append(lax.ppermute(total_edge, ("tile", "wave"), pairs))
+
+    def among_last(array, k):
+        return lax.ppermute(array, both, [(last + w, last + (w ^ k)) for w in range(count)])
+
+    other_edge = among_last(total_edge, 1)
     here, power, left, right_root = pl.pallas_call(
         lambda *refs: power_kernel(count, *refs),
         out_shape=(share, square, square, square),
@@ -497,13 +505,22 @@
         name="forward",
     )(near, halo, near_probe, table, coef, power)
     shares = [messages[0]]
-    for k in range(1, count):
+    for k in partners:
         shares.append(lax.ppermute(messages[k], "wave", [(w, w ^ k) for w in range(count)]))
+    pair_edge = pl.pallas_call(
+        add_kernel,
+        out_shape=square,
+        in_specs=[VM] * 3,
+        out_specs=VM,
+        compiler_params=params(),
+        name="pair",
+    )(total_edge, other_edge, messages[0])
+    edges = [pair_edge] + [among_last(pair_edge, k) for k in range(2, count, 2)]
 
     *sends, scale = pl.pallas_call(
         lambda *refs: backward_kernel(tiles, count, *refs),
         out_shape=(share,) * count + (shape((half_rows, length), f32),),
-        in_specs=[VM] * (7 + 2 * count),
+        in_specs=[VM] * (7 + count + len(edges)),
         out_specs=(VM,) * (count + 1),
         scratch_shapes=[
             pltpu.VMEM((2 * length, length), f32),
@@ -518,9 +535,9 @@
         return (t + (q >= count // 2)) % tiles * count + q
 
     arrived = []
-    for k in range(count):
+    for k in (0, *partners):
         pairs = [(t * count + w, owner(t, w ^ k)) for t in range(tiles) for w in range(count)]
-        arrived.append(lax.ppermute(sends[k], ("tile", "wave"), [p for p in pairs if p[0] != p[1]]))
+        arrived.append(lax.ppermute(sends[k], both, [p for p in pairs if p[0] != p[1]]))
 
     new = pl.pallas_call(
         lambda *refs: update_kernel(count, *refs),

time: 43.8 us -> 40.2 us (0.918)
  waiting for transfers between devices: 14.3 us -> 10.7 us
    ppermute x3, waiting for transfers between devices: 4.75 us -> 0.63 us  [per_device(): lax.ppermute(messages[k], 'wave', [(w, w ^ k) for w in range(count)])]
    ppermute x1, starting transfers between devices: 1.85 us -> 3.5 us  [per_device(): left_root = lax.ppermute(left, 'tile', ring)]
    ppermute x7 -> x6, waiting for transfers between devices: 5.44 us -> 4.21 us  [the longest x4 4.2 us: per_device(): lax.ppermute(sends[k], both, [p for p in pairs if p[0] != p[1]])]
    ppermute x1, waiting for transfers between devices: 0.01 us -> 1.22 us  [per_device(): left_root = lax.ppermute(left, 'tile', ring)]
    ppermute x3, starting transfers between devices: 6.03 us -> 5.11 us  [per_device(): parts.append(lax.ppermute(new, 'wave', [(w, w ^ k) for w in range(count)]))]
    ppermute x7 -> x6, starting transfers between devices: 5.66 us -> 5.27 us  [the longest x4 3.94 us: per_device(): lax.ppermute(sends[k], both, [p for p in pairs if p[0] != p[1]])]
  transfers between devices with their start and end apart: 15 -> 14, of which waited for: 7 -> 8; matrix products, arithmetic and copies ran while one was open for 0% -> 0% of each run, Pallas kernels for 12% -> 13%
where the time goes in v6:
time: 40.2 us; the launch traced here: 39.7 us
  starting transfers between devices  21.7 us (54%)
  waiting for transfers between devices  10.7 us (27%)
  Pallas kernels  7.29 us (18%)
    ppermute x3, starting transfers between devices, per_device(): parts.append(lax.ppermute(new, 'wave', [(w, w ^ k) for w in range(count)]))  5.11 us
    ppermute x3, waiting for transfers between devices, per_device(): parts.append(lax.ppermute(new, 'wave', [(w, w ^ k) for w in range(count)]))  4.54 us
    ppermute x3, starting transfers between devices, per_device(): lax.ppermute(messages[k], 'wave', [(w, w ^ k) for w in range(count)])  4.45 us
    ppermute x4, waiting for transfers between devices, per_device(): lax.ppermute(sends[k], both, [p for p in pairs if p[0] != p[1]])  4.2 us
    ppermute x4, starting transfers between devices, per_device(): lax.ppermute(sends[k], both, [p for p in pairs if p[0] != p[1]])  3.94 us
    ppermute x1, starting transfers between devices, per_device(): left_root = lax.ppermute(left, 'tile', ring)  3.5 us
    ppermute x1, starting transfers between devices, per_device(): halo = lax.ppermute(maps, 'tile', ring)  3.33 us
    pallas_call x1, Pallas kernels, per_device(): pl.pallas_call(first_kernel, out_shape=(shape((slots, 3, length, length),...  2.44 us
  transfers between devices with their start and end apart: 14, of which 8 were waited for; matrix products, arithmetic and copies ran while one was open for 0% of the time, Pallas kernels for 13%

profile of v6, /device:TPU:0, one launch (start us, length us, event | category | flops | bytes accessed | tf_op | source)
XLA Modules:
  0.0 39.7 jit_solution(3757565202228649837)
XLA Ops:
  0.0 3.3 %collective-permute-start.1 = (f32[4,128,128]{2,1,0:T(8,128)}, f32[4,128,128]{2,1,0:T(8,128)S(1)}, u32[]{:S(2)}, u32[]{:S(2)}) collective-permute-start(f32[4,128,128]{2,1,0:T(8,128)} %maps_any.1), channel_id=1, source_target_pairs={{0,28},{4,0},{8,4},{12,8},{16,12},{20,16},{24,20},{28,24},{1,29},{... | collective-permute-start | bytes 786440 | tf_op jit(solution)/shard_map/ppermute | solution.py:443
  3.3 2.4 %tables.1 = (bf16[12,3,128,128]{3,2,1,0:T(8,128)(2,1)S(1)}, f32[12,24,128]{2,1,0:T(8,128)S(1)}, f32[12,2,128,128]{3,2,1,0:T(8,128)S(1)}, f32[12,2,128,128]{3,2,1...) custom-call(f32[12]{0:T(128)} %spectrum_any.1, s32[12]{0:T(128)} %wave_any.1, ...), custom_call_target="tpu_custom_call" | custom-call | flops 1000000000 | bytes 4194304 | tf_op jit(solution)/shard_map/tables/pallas_call | solution.py:447
  5.8 0.7 %collective-permute-start.5 = (f32[128,128]{1,0:T(8,128)S(1)}, f32[128,128]{1,0:T(8,128)S(1)}, u32[]{:S(2)}, u32[]{:S(2)}) collective-permute-start(f32[128,128]{1,0:T(8,128)S(1)} %get-tuple-element.43.one), channel_id=1, source_target_pairs={{28,29},{29,28},{30,31},{31,30}} | collective-permute-start | bytes 196616 | tf_op jit(solution)/shard_map/ppermute | solution.py:477
  6.5 1.0 %power.1 = (f32[4,32,128]{2,1,0:T(8,128)S(1)}, f32[128,128]{1,0:T(8,128)S(1)}, f32[128,128]{1,0:T(8,128)S(1)}, f32[128,128]{1,0:T(8,128)S(1)}) custom-call(s32[2]{0:T(128)} %refs_0_.1, f32[2,128,128]{2,1,0:T(8,128)} %refs_1_.1, f32[12,24,128]{2,1,0:T(8,128)S(1)} %get-tuple-element.27.refs_2_.refs_4_.refs_3_, ...), custom_call_target="tpu_custom_call" | custom-call | tf_op jit(solution)/shard_map/power/pallas_call | solution.py:480
  7.4 0.1 collective-permute-done.1.refs_1_
  7.5 1.6 %forward.1 = (f32[12,2,128,128]{3,2,1,0:T(8,128)S(1)}, f32[12,128,256]{2,1,0:T(8,128)S(1)}, f32[160,128]{1,0:T(8,128)S(1)}, f32[160,128]{1,0:T(8,128)S(1)}, f32[...) custom-call(f32[12,2,128,128]{3,2,1,0:T(8,128)S(1)} %get-tuple-element.34.refs_0_, ...), custom_call_target="tpu_custom_call" | custom-call | tf_op jit(solution)/shard_map/forward/pallas_call | solution.py:495
  9.1 2.7 %collective-permute-start.2 = (f32[160,128]{1,0:T(8,128)S(1)}, f32[160,128]{1,0:T(8,128)S(1)}, u32[]{:S(2)}, u32[]{:S(2)}) collective-permute-start(f32[160,128]{1,0:T(8,128)S(1)} %get-tuple-element.40), channel_id=1, source_target_pairs={{0,2},{1,3},{2,0},{3,1},{4,6},{5,7},{6,4},{7,5},{8,10},{9,11},{10,... | collective-permute-start | bytes 245768 | tf_op jit(solution)/shard_map/ppermute | solution.py:509
  11.8 1.6 %collective-permute-start.3 = (f32[160,128]{1,0:T(8,128)S(1)}, f32[160,128]{1,0:T(8,128)S(1)}, u32[]{:S(2)}, u32[]{:S(2)}) collective-permute-start(f32[160,128]{1,0:T(8,128)S(1)} %get-tuple-element.41), channel_id=1, source_target_pairs={{0,1},{1,0},{2,3},{3,2},{4,5},{5,4},{6,7},{7,6},{8,9},{9,8},{10,11... | collective-permute-start | bytes 245768 | tf_op jit(solution)/shard_map/ppermute | solution.py:509
  13.4 0.2 collective-permute-start.4
  13.6 3.5 %collective-permute-start = (f32[128,128]{1,0:T(8,128)S(1)}, f32[128,128]{1,0:T(8,128)S(1)}, u32[]{:S(2)}, u32[]{:S(2)}) collective-permute-start(f32[128,128]{1,0:T(8,128)S(1)} %get-tuple-element.32), channel_id=1, source_target_pairs={{0,28},{4,0},{8,4},{12,8},{16,12},{20,16},{24,20},{28,24},{1,29},{... | collective-permute-start | bytes 196616 | tf_op jit(solution)/shard_map/ppermute | solution.py:493
  17.1 0.0 collective-permute-done.5.other
  17.1 0.7 %collective-permute-start.6 = (f32[128,128]{1,0:T(8,128)S(1)}, f32[128,128]{1,0:T(8,128)S(1)}, u32[]{:S(2)}, u32[]{:S(2)}) collective-permute-start(f32[128,128]{1,0:T(8,128)S(1)} %pair.1.refs_11_), channel_id=1, source_target_pairs={{28,30},{29,31},{30,28},{31,29}} | collective-permute-start | bytes 196616 | tf_op jit(solution)/shard_map/ppermute | solution.py:477
  17.8 1.2 %collective-permute-done.refs_1_ = f32[128,128]{1,0:T(8,128)S(1)} collective-permute-done((f32[128,128]{1,0:T(8,128)S(1)}, f32[128,128]{1,0:T(8,128)S(1)}, u32[]{:S(2)}, u32[]{:S(2)}) %collective-permute-start) | collective-permute-done | bytes 65568 | tf_op jit(solution)/shard_map/ppermute | solution.py:493
  19.0 0.0 collective-permute-done.6.refs_12_
  19.0 0.0 collective-permute-done.2.refs_8_
  19.0 0.0 collective-permute-done.3.refs_9_
  19.0 0.6 %collective-permute-done.4.refs_10_ = f32[160,128]{1,0:T(8,128)S(1)} collective-permute-done((f32[160,128]{1,0:T(8,128)S(1)}, f32[160,128]{1,0:T(8,128)S(1)}, u32[]{:S(2)}, u32[]{:S(2)}) %collective-permute-start.4) | collective-permute-done | bytes 81952 | tf_op jit(solution)/shard_map/ppermute | solution.py:509
  19.6 1.4 %backward.1 = (f32[4,32,128]{2,1,0:T(8,128)S(1)}, f32[4,32,128]{2,1,0:T(8,128)S(1)}, f32[4,32,128]{2,1,0:T(8,128)S(1)}, f32[4,32,128]{2,1,0:T(8,128)S(1)}, f32[32,128]{1,0:T(8,128)S(1)}) custom-call(f32[128,128]{1,0:T(8,128)S(1)} %get-tuple-element.31.refs_0_, f32[128,128]{1,0:T(8,128)S(1)} %collective-permute-done.refs_1_, ...), custom_call_target="tpu_custom_call" | custom-call | tf_op jit(solution)/shard_map/backward/pallas_call | solution.py:520
  21.0 1.9 %collective-permute-start.8 = (f32[4,32,128]{2,1,0:T(8,128)S(1)}, f32[4,32,128]{2,1,0:T(8,128)S(1)}, u32[]{:S(2)}, u32[]{:S(2)}) collective-permute-start(f32[4,32,128]{2,1,0:T(8,128)S(1)} %get-tuple-element.46), channel_id=1, source_target_pairs={{0,6},{1,7},{2,0},{3,1},{4,10},{5,11},{6,4},{7,5},{8,14},{9,15},{1... | collective-permute-start | bytes 196616 | tf_op jit(solution)/shard_map/ppermute | solution.py:540
  23.0 0.0 collective-permute-start.9
  23.0 1.4 %collective-permute-start.10 = (f32[4,32,128]{2,1,0:T(8,128)S(1)}, f32[4,32,128]{2,1,0:T(8,128)S(1)}, u32[]{:S(2)}, u32[]{:S(2)}) collective-permute-start(f32[4,32,128]{2,1,0:T(8,128)S(1)} %get-tuple-element.48), channel_id=1, source_target_pairs={{0,7},{1,6},{2,1},{3,0},{4,11},{5,10},{6,5},{7,4},{8,15},{9,14},{1... | collective-permute-start | bytes 196616 | tf_op jit(solution)/shard_map/ppermute | solution.py:540
  24.3 0.7 %collective-permute-start.7 = (f32[4,32,128]{2,1,0:T(8,128)S(1)}, f32[4,32,128]{2,1,0:T(8,128)S(1)}, u32[]{:S(2)}, u32[]{:S(2)}) collective-permute-start(f32[4,32,128]{2,1,0:T(8,128)S(1)} %get-tuple-element.45.refs_2_), channel_id=1, source_target_pairs={{2,6},{3,7},{6,10},{7,11},{10,14},{11,15},{14,18},{15,19},{18,22},... | collective-permute-start | bytes 196616 | tf_op jit(solution)/shard_map/ppermute | solution.py:540
  25.0 2.1 %collective-permute-done.8.refs_4_ = f32[4,32,128]{2,1,0:T(8,128)S(1)} collective-permute-done((f32[4,32,128]{2,1,0:T(8,128)S(1)}, f32[4,32,128]{2,1,0:T(8,128)S(1)}, u32[]{:S(2)}, u32[]{:S(2)}) %collective-permute-start.8) | collective-permute-done | bytes 65568 | tf_op jit(solution)/shard_map/ppermute | solution.py:540
  27.1 1.1 %collective-permute-done.9.refs_5_ = f32[4,32,128]{2,1,0:T(8,128)S(1)} collective-permute-done((f32[4,32,128]{2,1,0:T(8,128)S(1)}, f32[4,32,128]{2,1,0:T(8,128)S(1)}, u32[]{:S(2)}, u32[]{:S(2)}) %collective-permute-start.9) | collective-permute-done | bytes 65568 | tf_op jit(solution)/shard_map/ppermute | solution.py:540
  28.3 0.9 %collective-permute-done.10.refs_6_ = f32[4,32,128]{2,1,0:T(8,128)S(1)} collective-permute-done((f32[4,32,128]{2,1,0:T(8,128)S(1)}, f32[4,32,128]{2,1,0:T(8,128)S(1)}, u32[]{:S(2)}, u32[]{:S(2)}) %collective-permute-start.10) | collective-permute-done | bytes 65568 | tf_op jit(solution)/shard_map/ppermute | solution.py:540
  29.2 0.0 collective-permute-done.7.refs_3_
  29.2 4.5 %collective-permute-start.13 = (f32[4,32,128]{2,1,0:T(8,128)S(1)}, f32[4,32,128]{2,1,0:T(8,128)S(1)}, u32[]{:S(2)}, u32[]{:S(2)}) collective-permute-start(f32[4,32,128]{2,1,0:T(8,128)S(1)} %update.1.refs_0_), channel_id=1, source_target_pairs={{0,3},{1,2},{2,1},{3,0},{4,7},{5,6},{6,5},{7,4},{8,11},{9,10},{10,... | collective-permute-start | bytes 196616 | tf_op jit(solution)/shard_map/ppermute | solution.py:553
  33.7 0.0 collective-permute-start.12
  33.7 0.6 %collective-permute-start.11 = (f32[4,32,128]{2,1,0:T(8,128)S(1)}, f32[4,32,128]{2,1,0:T(8,128)S(1)}, u32[]{:S(2)}, u32[]{:S(2)}) collective-permute-start(f32[4,32,128]{2,1,0:T(8,128)S(1)} %update.1.refs_0_), channel_id=1, source_target_pairs={{0,1},{1,0},{2,3},{3,2},{4,5},{5,4},{6,7},{7,6},{8,9},{9,8},{10,11... | collective-permute-start | bytes 196616 | tf_op jit(solution)/shard_map/ppermute | solution.py:553
  34.3 1.8 %collective-permute-done.13.refs_3_ = f32[4,32,128]{2,1,0:T(8,128)S(1)} collective-permute-done((f32[4,32,128]{2,1,0:T(8,128)S(1)}, f32[4,32,128]{2,1,0:T(8,128)S(1)}, u32[]{:S(2)}, u32[]{:S(2)}) %collective-permute-start.13) | collective-permute-done | bytes 65568 | tf_op jit(solution)/shard_map/ppermute | solution.py:553
  36.1 2.8 %collective-permute-done.12.refs_2_ = f32[4,32,128]{2,1,0:T(8,128)S(1)} collective-permute-done((f32[4,32,128]{2,1,0:T(8,128)S(1)}, f32[4,32,128]{2,1,0:T(8,128)S(1)}, u32[]{:S(2)}, u32[]{:S(2)}) %collective-permute-start.12) | collective-permute-done | bytes 65568 | tf_op jit(solution)/shard_map/ppermute | solution.py:553
  38.9 0.0 collective-permute-done.11.refs_1_
  38.9 0.8 %join.1 = f32[4,128,128]{2,1,0:T(8,128)} custom-call(f32[4,32,128]{2,1,0:T(8,128)S(1)} %update.1.refs_0_, f32[4,32,128]{2,1,0:T(8,128)S(1)} %collective-permute-done.11.refs_1_, f32[4,32,128]{2,1,0:T(8,128)S(1)} %collective-permute-done.12.refs_2_, f32[4,32,128]{2,1,0:T(8,128)S(1)} %collective-permute-done.13.refs_3_), custom_call_target="tpu_custom_call" | custom-call | tf_op jit(solution)/shard_map/join/pallas_call | solution.py:554
  (2 shorter events, 0.0 us)
Async XLA Ops:
  0.0 7.5 %collective-permute-start.1 = (f32[4,128,128]{2,1,0:T(8,128)}, f32[4,128,128]{2,1,0:T(8,128)S(1)}, u32[]{:S(2)}, u32[]{:S(2)}) collective-permute-start(f32[4,128,128]{2,1,0:T(8,128)} %maps_any.1), channel_id=1, source_target_pairs={{0,28},{4,0},{8,4},{12,8},{16,12},{20,16},{24,20},{28,24},{1,29},{... | collective-permute-start | bytes 786440 | tf_op jit(solution)/shard_map/ppermute | solution.py:443
  5.8 11.3 %collective-permute-start.5 = (f32[128,128]{1,0:T(8,128)S(1)}, f32[128,128]{1,0:T(8,128)S(1)}, u32[]{:S(2)}, u32[]{:S(2)}) collective-permute-start(f32[128,128]{1,0:T(8,128)S(1)} %get-tuple-element.43.one), channel_id=1, source_target_pairs={{28,29},{29,28},{30,31},{31,30}} | collective-permute-start | bytes 196616 | tf_op jit(solution)/shard_map/ppermute | solution.py:477
  9.1 9.9 %collective-permute-start.2 = (f32[160,128]{1,0:T(8,128)S(1)}, f32[160,128]{1,0:T(8,128)S(1)}, u32[]{:S(2)}, u32[]{:S(2)}) collective-permute-start(f32[160,128]{1,0:T(8,128)S(1)} %get-tuple-element.40), channel_id=1, source_target_pairs={{0,2},{1,3},{2,0},{3,1},{4,6},{5,7},{6,4},{7,5},{8,10},{9,11},{10,... | collective-permute-start | bytes 245768 | tf_op jit(solution)/shard_map/ppermute | solution.py:509
  11.8 7.2 %collective-permute-start.3 = (f32[160,128]{1,0:T(8,128)S(1)}, f32[160,128]{1,0:T(8,128)S(1)}, u32[]{:S(2)}, u32[]{:S(2)}) collective-permute-start(f32[160,128]{1,0:T(8,128)S(1)} %get-tuple-element.41), channel_id=1, source_target_pairs={{0,1},{1,0},{2,3},{3,2},{4,5},{5,4},{6,7},{7,6},{8,9},{9,8},{10,11... | collective-permute-start | bytes 245768 | tf_op jit(solution)/shard_map/ppermute | solution.py:509
  13.4 6.3 %collective-permute-start.4 = (f32[160,128]{1,0:T(8,128)S(1)}, f32[160,128]{1,0:T(8,128)S(1)}, u32[]{:S(2)}, u32[]{:S(2)}) collective-permute-start(f32[160,128]{1,0:T(8,128)S(1)} %get-tuple-element.42), channel_id=1, source_target_pairs={{0,3},{1,2},{2,1},{3,0},{4,7},{5,6},{6,5},{7,4},{8,11},{9,10},{10,... | collective-permute-start | bytes 245768 | tf_op jit(solution)/shard_map/ppermute | solution.py:509
  13.6 5.4 %collective-permute-start = (f32[128,128]{1,0:T(8,128)S(1)}, f32[128,128]{1,0:T(8,128)S(1)}, u32[]{:S(2)}, u32[]{:S(2)}) collective-permute-start(f32[128,128]{1,0:T(8,128)S(1)} %get-tuple-element.32), channel_id=1, source_target_pairs={{0,28},{4,0},{8,4},{12,8},{16,12},{20,16},{24,20},{28,24},{1,29},{... | collective-permute-start | bytes 196616 | tf_op jit(solution)/shard_map/ppermute | solution.py:493
  17.1 1.9 %collective-permute-start.6 = (f32[128,128]{1,0:T(8,128)S(1)}, f32[128,128]{1,0:T(8,128)S(1)}, u32[]{:S(2)}, u32[]{:S(2)}) collective-permute-start(f32[128,128]{1,0:T(8,128)S(1)} %pair.1.refs_11_), channel_id=1, source_target_pairs={{28,30},{29,31},{30,28},{31,29}} | collective-permute-start | bytes 196616 | tf_op jit(solution)/shard_map/ppermute | solution.py:477
  21.0 6.1 %collective-permute-start.8 = (f32[4,32,128]{2,1,0:T(8,128)S(1)}, f32[4,32,128]{2,1,0:T(8,128)S(1)}, u32[]{:S(2)}, u32[]{:S(2)}) collective-permute-start(f32[4,32,128]{2,1,0:T(8,128)S(1)} %get-tuple-element.46), channel_id=1, source_target_pairs={{0,6},{1,7},{2,0},{3,1},{4,10},{5,11},{6,4},{7,5},{8,14},{9,15},{1... | collective-permute-start | bytes 196616 | tf_op jit(solution)/shard_map/ppermute | solution.py:540
  23.0 5.3 %collective-permute-start.9 = (f32[4,32,128]{2,1,0:T(8,128)S(1)}, f32[4,32,128]{2,1,0:T(8,128)S(1)}, u32[]{:S(2)}, u32[]{:S(2)}) collective-permute-start(f32[4,32,128]{2,1,0:T(8,128)S(1)} %get-tuple-element.47), channel_id=1, source_target_pairs={{0,1},{1,0},{2,7},{3,6},{4,5},{5,4},{6,11},{7,10},{8,9},{9,8},{10,... | collective-permute-start | bytes 196616 | tf_op jit(solution)/shard_map/ppermute | solution.py:540
  23.0 6.2 %collective-permute-start.10 = (f32[4,32,128]{2,1,0:T(8,128)S(1)}, f32[4,32,128]{2,1,0:T(8,128)S(1)}, u32[]{:S(2)}, u32[]{:S(2)}) collective-permute-start(f32[4,32,128]{2,1,0:T(8,128)S(1)} %get-tuple-element.48), channel_id=1, source_target_pairs={{0,7},{1,6},{2,1},{3,0},{4,11},{5,10},{6,5},{7,4},{8,15},{9,14},{1... | collective-permute-start | bytes 196616 | tf_op jit(solution)/shard_map/ppermute | solution.py:540
  24.3 4.9 %collective-permute-start.7 = (f32[4,32,128]{2,1,0:T(8,128)S(1)}, f32[4,32,128]{2,1,0:T(8,128)S(1)}, u32[]{:S(2)}, u32[]{:S(2)}) collective-permute-start(f32[4,32,128]{2,1,0:T(8,128)S(1)} %get-tuple-element.45.refs_2_), channel_id=1, source_target_pairs={{2,6},{3,7},{6,10},{7,11},{10,14},{11,15},{14,18},{15,19},{18,22},... | collective-permute-start | bytes 196616 | tf_op jit(solution)/shard_map/ppermute | solution.py:540
  29.2 6.9 %collective-permute-start.13 = (f32[4,32,128]{2,1,0:T(8,128)S(1)}, f32[4,32,128]{2,1,0:T(8,128)S(1)}, u32[]{:S(2)}, u32[]{:S(2)}) collective-permute-start(f32[4,32,128]{2,1,0:T(8,128)S(1)} %update.1.refs_0_), channel_id=1, source_target_pairs={{0,3},{1,2},{2,1},{3,0},{4,7},{5,6},{6,5},{7,4},{8,11},{9,10},{10,... | collective-permute-start | bytes 196616 | tf_op jit(solution)/shard_map/ppermute | solution.py:553
  33.7 5.2 %collective-permute-start.12 = (f32[4,32,128]{2,1,0:T(8,128)S(1)}, f32[4,32,128]{2,1,0:T(8,128)S(1)}, u32[]{:S(2)}, u32[]{:S(2)}) collective-permute-start(f32[4,32,128]{2,1,0:T(8,128)S(1)} %update.1.refs_0_), channel_id=1, source_target_pairs={{0,2},{1,3},{2,0},{3,1},{4,6},{5,7},{6,4},{7,5},{8,10},{9,11},{10,... | collective-permute-start | bytes 196616 | tf_op jit(solution)/shard_map/ppermute | solution.py:553
  33.7 5.2 %collective-permute-start.11 = (f32[4,32,128]{2,1,0:T(8,128)S(1)}, f32[4,32,128]{2,1,0:T(8,128)S(1)}, u32[]{:S(2)}, u32[]{:S(2)}) collective-permute-start(f32[4,32,128]{2,1,0:T(8,128)S(1)} %update.1.refs_0_), channel_id=1, source_target_pairs={{0,1},{1,0},{2,3},{3,2},{4,5},{5,4},{6,7},{7,6},{8,9},{9,8},{10,11... | collective-permute-start | bytes 196616 | tf_op jit(solution)/shard_map/ppermute | solution.py:553

commit v7 on v6

--- a/solution.py
+++ b/solution.py
@@ -81,9 +81,9 @@
 
 
 def first_kernel(
-    spectrum_any, wave_any, edge_any, band_any, maps_any, probe_any,
-    table, coef, probe, near, own, far_edge, total_edge,
-    spectrum, wave_index, edge_band, band_coef, maps, packed, sems,
+    spectrum_any, wave_any, edge_any, band_any, maps_any, probe_any, offsets_any, measured_any,
+    table, coef, probe, near, own, far_edge, total_edge, left_root, right_root,
+    spectrum, wave_index, edge_band, band_coef, maps, packed, offsets, measured, sems,
 ):
     copies = [
         pltpu.make_async_copy(source, target, sems.at[i])
@@ -95,6 +95,8 @@
                 (spectrum_any, spectrum),
                 (maps_any, maps),
                 (probe_any, probe),
+                (offsets_any, offsets),
+                (measured_any, measured),
             )
         )
     ]
@@ -146,6 +148,10 @@
             coef[s, 2 * materials + m, :] = jnp.full((length,), a, f32)
             coef[s, 3 * materials + m, :] = jnp.full((length,), b, f32)
         coef[s, 4 * materials, :] = jnp.full((length,), spectrum[s], f32)
+    left_first = offsets[0] < offsets[1]
+    first, second = jnp.sqrt(measured[0]), jnp.sqrt(measured[1])
+    left_root[...] = jnp.where(left_first, first, second)
+    right_root[...] = jnp.where(left_first, second, first)
     for m in range(materials):
         own[m] = pltpu.roll(maps[m], half, 1)
         packed[m] = halves_packed(own[m, :half], own[m, half:], False)
@@ -179,17 +185,8 @@
         lax.fori_loop(0, slots, step, 0, unroll=EDGE_UNROLL)
 
 
-def power_kernel(
-    count, offsets_any, measured_any, coef, probe, own,
-    here, power, left_root, right_root,
-    offsets, measured, sems,
-):
-    copies = [
-        pltpu.make_async_copy(source, target, sems.at[i])
-        for i, (source, target) in enumerate(((offsets_any, offsets), (measured_any, measured)))
-    ]
-    for copy in copies:
-        copy.start()
+def power_kernel(count, coef, probe, own, left_root, here, power, left_out):
+    left_out[...] = left_root[...]
     materials, length, _ = own.shape
     half = length // 2
     slots = probe.shape[0]
@@ -214,17 +211,11 @@
             weight = coef[s, 4 * materials : 4 * materials + 1]
             return total + (weight * jnp.exp2(absorb + absorb)) * (re * re + im * im)
 
-        total = lax.fori_loop(0, slots, add, jnp.zeros((CHUNK, length), f32), unroll=4)
+        total = lax.fori_loop(0, slots, add, jnp.zeros((CHUNK, length), f32), unroll=UNROLL)
         power[at] = frames * total
     half_rows = length // count
     for m in range(materials):
         here[m] = piece(own.at[m], me, count, half_rows)
-    for copy in copies:
-        copy.wait()
-    left_first = offsets[0] < offsets[1]
-    first, second = jnp.sqrt(measured[0]), jnp.sqrt(measured[1])
-    left_root[...] = jnp.where(left_first, first, second)
-    right_root[...] = jnp.where(left_first, second, first)
 
 
 def object_of(coef, s, window):
@@ -435,7 +426,8 @@
     half = length // 2
     shape = jax.ShapeDtypeStruct
     half_rows = length // count
-    partners = [count // 2] + [k for k in range(1, count) if k != count // 2]
+    rest = [k for k in range(1, count) if k != count // 2]
+    first_order, second_order = rest[::-1] + [count // 2], [count // 2] + rest
     square = shape((length, length), f32)
     share = shape((materials, half_rows, length), f32)
 
@@ -444,7 +436,7 @@
 
     band_first = jnp.transpose(band_coef, (1, 0, 2))
     field = shape((slots, length, 2 * length), f32)
-    table, coef, near_probe, near, own, far_edge, total_edge = pl.pallas_call(
+    table, coef, near_probe, near, own, far_edge, total_edge, left, right_root = pl.pallas_call(
         first_kernel,
         out_shape=(
             shape((slots, 3, length, length), bf16),
@@ -454,9 +446,11 @@
             shape(maps.shape, f32),
             field,
             square,
+            square,
+            square,
         ),
-        in_specs=[ANY] * 6,
-        out_specs=(VM,) * 7,
+        in_specs=[ANY] * 8,
+        out_specs=(VM,) * 9,
         scratch_shapes=[
             pltpu.SMEM(spectrum.shape, f32),
             pltpu.SMEM(wave_index.shape, jnp.int32),
@@ -464,12 +458,14 @@
             pltpu.SMEM(band_first.shape, f32),
             pltpu.VMEM(maps.shape, f32),
             pltpu.VMEM((materials, half, length), f32),
-            pltpu.SemaphoreType.DMA((6,)),
+            pltpu.SMEM(offsets.shape, jnp.int32),
+            pltpu.VMEM(measured.shape, f32),
+            pltpu.SemaphoreType.DMA((8,)),
         ],
         compiler_params=params(),
         cost_estimate=pl.CostEstimate(flops=10**9, bytes_accessed=2**22, transcendentals=0),
         name="tables",
-    )(*map(in_hbm, (spectrum, wave_index, edge_band.T, band_first, maps, probe)))
+    )(*map(in_hbm, (spectrum, wave_index, edge_band.T, band_first, maps, probe, offsets, measured)))
     both = ("tile", "wave")
     last = (tiles - 1) * count
 
@@ -477,19 +473,14 @@
         return lax.ppermute(array, both, [(last + w, last + (w ^ k)) for w in range(count)])
 
     other_edge = among_last(total_edge, 1)
-    here, power, left, right_root = pl.pallas_call(
+    here, power, left = pl.pallas_call(
         lambda *refs: power_kernel(count, *refs),
-        out_shape=(share, square, square, square),
-        in_specs=[ANY] * 2 + [VM] * 3,
-        out_specs=(VM,) * 4,
-        scratch_shapes=[
-            pltpu.SMEM(offsets.shape, jnp.int32),
-            pltpu.VMEM(measured.shape, f32),
-            pltpu.SemaphoreType.DMA((2,)),
-        ],
+        out_shape=(share, square, square),
+        in_specs=[VM] * 4,
+        out_specs=(VM,) * 3,
         compiler_params=params(),
         name="power",
-    )(*map(in_hbm, (offsets, measured)), coef, near_probe, own)
+    )(coef, near_probe, own, left)
     left_root = lax.ppermute(left, "tile", ring)
     message = shape((length + half_rows, length), f32)
     psi, far, *messages = pl.pallas_call(
@@ -505,7 +496,7 @@
         name="forward",
     )(near, halo, near_probe, table, coef, power)
     shares = [messages[0]]
-    for k in partners:
+    for k in first_order:
         shares.append(lax.ppermute(messages[k], "wave", [(w, w ^ k) for w in range(count)]))
     pair_edge = pl.pallas_call(
         add_kernel,
@@ -535,7 +526,7 @@
         return (t + (q >= count // 2)) % tiles * count + q
 
     arrived = []
-    for k in (0, *partners):
+    for k in (0, *second_order):
         pairs = [(t * count + w, owner(t, w ^ k)) for t in range(tiles) for w in range(count)]
         arrived.append(lax.ppermute(sends[k], both, [p for p in pairs if p[0] != p[1]]))
 

time: 40.2 us -> 39.9 us (level)
  Pallas kernels: 7.29 us -> 6.75 us
  waiting for transfers between devices: 10.7 us -> 11.2 us
    ppermute x4, starting transfers between devices: 3.94 us -> 4.71 us  [per_device(): lax.ppermute(sends[k], both, [p for p in pairs if p[0] != p[1]])]
    pallas_call x1, Pallas kernels: 0.97 us -> 0.39 us  [per_device(): pl.pallas_call(lambda *refs: power_kernel(count, *refs), out_shape=(share...]
    ppermute x1, starting transfers between devices: 3.5 us -> 2.94 us  [per_device(): left_root = lax.ppermute(left, 'tile', ring)]
    ppermute x1, waiting for transfers between devices: 0.11 us -> 0.65 us  [per_device(): halo = lax.ppermute(maps, 'tile', ring)]
  transfers between devices with their start and end apart: 14 -> 14, of which waited for: 8 -> 8; matrix products, arithmetic and copies ran while one was open for 0% -> 0% of each run, Pallas kernels for 13% -> 11%
where the time goes in v7:
time: 39.9 us; the launch traced here: 39.7 us
  starting transfers between devices  21.7 us (54%)
  waiting for transfers between devices  11.2 us (28%)
  Pallas kernels  6.75 us (17%)
    ppermute x3, starting transfers between devices, per_device(): parts.append(lax.ppermute(new, 'wave', [(w, w ^ k) for w in range(count)]))  4.97 us
    ppermute x4, starting transfers between devices, per_device(): lax.ppermute(sends[k], both, [p for p in pairs if p[0] != p[1]])  4.71 us
    ppermute x3, waiting for transfers between devices, per_device(): parts.append(lax.ppermute(new, 'wave', [(w, w ^ k) for w in range(count)]))  4.52 us
    ppermute x3, starting transfers between devices, per_device(): lax.ppermute(messages[k], 'wave', [(w, w ^ k) for w in range(count)])  4.45 us
    ppermute x4, waiting for transfers between devices, per_device(): lax.ppermute(sends[k], both, [p for p in pairs if p[0] != p[1]])  4.09 us
    ppermute x1, starting transfers between devices, per_device(): halo = lax.ppermute(maps, 'tile', ring)  3.33 us
    ppermute x1, starting transfers between devices, per_device(): left_root = lax.ppermute(left, 'tile', ring)  2.94 us
    pallas_call x1, Pallas kernels, per_device(): pl.pallas_call(first_kernel, out_shape=(shape((slots, 3, length, length),...  2.48 us
  transfers between devices with their start and end apart: 14, of which 8 were waited for; matrix products, arithmetic and copies ran while one was open for 0% of the time, Pallas kernels for 11%

profile of v7, /device:TPU:0, one launch (start us, length us, event | category | flops | bytes accessed | tf_op | source)
XLA Modules:
  0.0 39.7 jit_solution(13252276670011756983)
XLA Ops:
  0.0 3.3 %collective-permute-start.1 = (f32[4,128,128]{2,1,0:T(8,128)}, f32[4,128,128]{2,1,0:T(8,128)S(1)}, u32[]{:S(2)}, u32[]{:S(2)}) collective-permute-start(f32[4,128,128]{2,1,0:T(8,128)} %maps_any.1), channel_id=1, source_target_pairs={{0,28},{4,0},{8,4},{12,8},{16,12},{20,16},{24,20},{28,24},{1,29},{... | collective-permute-start | bytes 786440 | tf_op jit(solution)/shard_map/ppermute | solution.py:435
  3.3 2.5 %tables.1 = (bf16[12,3,128,128]{3,2,1,0:T(8,128)(2,1)S(1)}, f32[12,24,128]{2,1,0:T(8,128)S(1)}, f32[12,2,128,128]{3,2,1,0:T(8,128)S(1)}, f32[12,2,128,128]{3,2,1...) custom-call(f32[12]{0:T(128)} %spectrum_any.1, ...), custom_call_target="tpu_custom_call" | custom-call | flops 1000000000 | bytes 4194304 | tf_op jit(solution)/shard_map/tables/pallas_call | solution.py:439
  5.8 0.7 %collective-permute-start.5 = (f32[128,128]{1,0:T(8,128)S(1)}, f32[128,128]{1,0:T(8,128)S(1)}, u32[]{:S(2)}, u32[]{:S(2)}) collective-permute-start(f32[128,128]{1,0:T(8,128)S(1)} %get-tuple-element.45.one), channel_id=1, source_target_pairs={{28,29},{29,28},{30,31},{31,30}} | collective-permute-start | bytes 196616 | tf_op jit(solution)/shard_map/ppermute | solution.py:473
  6.5 0.4 power.1
  6.9 0.6 %collective-permute-done.1.refs_1_ = f32[4,128,128]{2,1,0:T(8,128)S(1)} collective-permute-done((f32[4,128,128]{2,1,0:T(8,128)}, f32[4,128,128]{2,1,0:T(8,128)S(1)}, u32[]{:S(2)}, u32[]{:S(2)}) %collective-permute-start.1) | collective-permute-done | bytes 262176 | tf_op jit(solution)/shard_map/ppermute | solution.py:435
  7.5 1.6 %forward.1 = (f32[12,2,128,128]{3,2,1,0:T(8,128)S(1)}, f32[12,128,256]{2,1,0:T(8,128)S(1)}, f32[160,128]{1,0:T(8,128)S(1)}, f32[160,128]{1,0:T(8,128)S(1)}, f32[...) custom-call(f32[12,2,128,128]{3,2,1,0:T(8,128)S(1)} %get-tuple-element.36.refs_0_, ...), custom_call_target="tpu_custom_call" | custom-call | tf_op jit(solution)/shard_map/forward/pallas_call | solution.py:486
  9.1 3.7 %collective-permute-start.2 = (f32[160,128]{1,0:T(8,128)S(1)}, f32[160,128]{1,0:T(8,128)S(1)}, u32[]{:S(2)}, u32[]{:S(2)}) collective-permute-start(f32[160,128]{1,0:T(8,128)S(1)} %get-tuple-element.42), channel_id=1, source_target_pairs={{0,3},{1,2},{2,1},{3,0},{4,7},{5,6},{6,5},{7,4},{8,11},{9,10},{10,... | collective-permute-start | bytes 245768 | tf_op jit(solution)/shard_map/ppermute | solution.py:500
  12.8 0.0 collective-permute-start.3
  12.8 0.8 %collective-permute-start.4 = (f32[160,128]{1,0:T(8,128)S(1)}, f32[160,128]{1,0:T(8,128)S(1)}, u32[]{:S(2)}, u32[]{:S(2)}) collective-permute-start(f32[160,128]{1,0:T(8,128)S(1)} %get-tuple-element.44), channel_id=1, source_target_pairs={{0,2},{1,3},{2,0},{3,1},{4,6},{5,7},{6,4},{7,5},{8,10},{9,11},{10,... | collective-permute-start | bytes 245768 | tf_op jit(solution)/shard_map/ppermute | solution.py:500
  13.6 2.9 %collective-permute-start = (f32[128,128]{1,0:T(8,128)S(1)}, f32[128,128]{1,0:T(8,128)S(1)}, u32[]{:S(2)}, u32[]{:S(2)}) collective-permute-start(f32[128,128]{1,0:T(8,128)S(1)} %get-tuple-element.34), channel_id=1, source_target_pairs={{0,28},{4,0},{8,4},{12,8},{16,12},{20,16},{24,20},{28,24},{1,29},{... | collective-permute-start | bytes 196616 | tf_op jit(solution)/shard_map/ppermute | solution.py:484
  16.5 0.0 collective-permute-done.5.other
  16.5 0.7 %collective-permute-start.6 = (f32[128,128]{1,0:T(8,128)S(1)}, f32[128,128]{1,0:T(8,128)S(1)}, u32[]{:S(2)}, u32[]{:S(2)}) collective-permute-start(f32[128,128]{1,0:T(8,128)S(1)} %pair.1.refs_11_), channel_id=1, source_target_pairs={{28,30},{29,31},{30,28},{31,29}} | collective-permute-start | bytes 196616 | tf_op jit(solution)/shard_map/ppermute | solution.py:473
  17.2 1.2 %collective-permute-done.refs_1_ = f32[128,128]{1,0:T(8,128)S(1)} collective-permute-done((f32[128,128]{1,0:T(8,128)S(1)}, f32[128,128]{1,0:T(8,128)S(1)}, u32[]{:S(2)}, u32[]{:S(2)}) %collective-permute-start) | collective-permute-done | bytes 65568 | tf_op jit(solution)/shard_map/ppermute | solution.py:484
  18.4 0.0 collective-permute-done.6.refs_12_
  18.4 0.0 collective-permute-done.2.refs_8_
  18.4 0.7 %collective-permute-done.3.refs_9_ = f32[160,128]{1,0:T(8,128)S(1)} collective-permute-done((f32[160,128]{1,0:T(8,128)S(1)}, f32[160,128]{1,0:T(8,128)S(1)}, u32[]{:S(2)}, u32[]{:S(2)}) %collective-permute-start.3) | collective-permute-done | bytes 81952 | tf_op jit(solution)/shard_map/ppermute | solution.py:500
  19.1 0.0 collective-permute-done.4.refs_10_
  19.1 1.4 %backward.1 = (f32[4,32,128]{2,1,0:T(8,128)S(1)}, f32[4,32,128]{2,1,0:T(8,128)S(1)}, f32[4,32,128]{2,1,0:T(8,128)S(1)}, f32[4,32,128]{2,1,0:T(8,128)S(1)}, f32[32,128]{1,0:T(8,128)S(1)}) custom-call(f32[128,128]{1,0:T(8,128)S(1)} %get-tuple-element.33.refs_0_, f32[128,128]{1,0:T(8,128)S(1)} %collective-permute-done.refs_1_, ...), custom_call_target="tpu_custom_call" | custom-call | tf_op jit(solution)/shard_map/backward/pallas_call | solution.py:511
  20.5 0.5 %collective-permute-start.8 = (f32[4,32,128]{2,1,0:T(8,128)S(1)}, f32[4,32,128]{2,1,0:T(8,128)S(1)}, u32[]{:S(2)}, u32[]{:S(2)}) collective-permute-start(f32[4,32,128]{2,1,0:T(8,128)S(1)} %get-tuple-element.48), channel_id=1, source_target_pairs={{0,6},{1,7},{2,0},{3,1},{4,10},{5,11},{6,4},{7,5},{8,14},{9,15},{1... | collective-permute-start | bytes 196616 | tf_op jit(solution)/shard_map/ppermute | solution.py:531
  21.0 1.7 %collective-permute-start.9 = (f32[4,32,128]{2,1,0:T(8,128)S(1)}, f32[4,32,128]{2,1,0:T(8,128)S(1)}, u32[]{:S(2)}, u32[]{:S(2)}) collective-permute-start(f32[4,32,128]{2,1,0:T(8,128)S(1)} %get-tuple-element.49), channel_id=1, source_target_pairs={{0,1},{1,0},{2,7},{3,6},{4,5},{5,4},{6,11},{7,10},{8,9},{9,8},{10,... | collective-permute-start | bytes 196616 | tf_op jit(solution)/shard_map/ppermute | solution.py:531
  22.7 1.9 %collective-permute-start.10 = (f32[4,32,128]{2,1,0:T(8,128)S(1)}, f32[4,32,128]{2,1,0:T(8,128)S(1)}, u32[]{:S(2)}, u32[]{:S(2)}) collective-permute-start(f32[4,32,128]{2,1,0:T(8,128)S(1)} %get-tuple-element.50), channel_id=1, source_target_pairs={{0,7},{1,6},{2,1},{3,0},{4,11},{5,10},{6,5},{7,4},{8,15},{9,14},{1... | collective-permute-start | bytes 196616 | tf_op jit(solution)/shard_map/ppermute | solution.py:531
  24.6 0.7 %collective-permute-start.7 = (f32[4,32,128]{2,1,0:T(8,128)S(1)}, f32[4,32,128]{2,1,0:T(8,128)S(1)}, u32[]{:S(2)}, u32[]{:S(2)}) collective-permute-start(f32[4,32,128]{2,1,0:T(8,128)S(1)} %get-tuple-element.47.refs_2_), channel_id=1, source_target_pairs={{2,6},{3,7},{6,10},{7,11},{10,14},{11,15},{14,18},{15,19},{18,22},... | collective-permute-start | bytes 196616 | tf_op jit(solution)/shard_map/ppermute | solution.py:531
  25.3 1.3 %collective-permute-done.8.refs_4_ = f32[4,32,128]{2,1,0:T(8,128)S(1)} collective-permute-done((f32[4,32,128]{2,1,0:T(8,128)S(1)}, f32[4,32,128]{2,1,0:T(8,128)S(1)}, u32[]{:S(2)}, u32[]{:S(2)}) %collective-permute-start.8) | collective-permute-done | bytes 65568 | tf_op jit(solution)/shard_map/ppermute | solution.py:531
  26.5 0.1 collective-permute-done.9.refs_5_
  26.6 2.7 %collective-permute-done.10.refs_6_ = f32[4,32,128]{2,1,0:T(8,128)S(1)} collective-permute-done((f32[4,32,128]{2,1,0:T(8,128)S(1)}, f32[4,32,128]{2,1,0:T(8,128)S(1)}, u32[]{:S(2)}, u32[]{:S(2)}) %collective-permute-start.10) | collective-permute-done | bytes 65568 | tf_op jit(solution)/shard_map/ppermute | solution.py:531
  29.4 0.0 collective-permute-done.7.refs_3_
  29.4 4.3 %collective-permute-start.13 = (f32[4,32,128]{2,1,0:T(8,128)S(1)}, f32[4,32,128]{2,1,0:T(8,128)S(1)}, u32[]{:S(2)}, u32[]{:S(2)}) collective-permute-start(f32[4,32,128]{2,1,0:T(8,128)S(1)} %update.1.refs_0_), channel_id=1, source_target_pairs={{0,3},{1,2},{2,1},{3,0},{4,7},{5,6},{6,5},{7,4},{8,11},{9,10},{10,... | collective-permute-start | bytes 196616 | tf_op jit(solution)/shard_map/ppermute | solution.py:544
  33.7 0.0 collective-permute-start.12
  33.7 0.6 %collective-permute-start.11 = (f32[4,32,128]{2,1,0:T(8,128)S(1)}, f32[4,32,128]{2,1,0:T(8,128)S(1)}, u32[]{:S(2)}, u32[]{:S(2)}) collective-permute-start(f32[4,32,128]{2,1,0:T(8,128)S(1)} %update.1.refs_0_), channel_id=1, source_target_pairs={{0,1},{1,0},{2,3},{3,2},{4,5},{5,4},{6,7},{7,6},{8,9},{9,8},{10,11... | collective-permute-start | bytes 196616 | tf_op jit(solution)/shard_map/ppermute | solution.py:544
  34.4 1.7 %collective-permute-done.13.refs_3_ = f32[4,32,128]{2,1,0:T(8,128)S(1)} collective-permute-done((f32[4,32,128]{2,1,0:T(8,128)S(1)}, f32[4,32,128]{2,1,0:T(8,128)S(1)}, u32[]{:S(2)}, u32[]{:S(2)}) %collective-permute-start.13) | collective-permute-done | bytes 65568 | tf_op jit(solution)/shard_map/ppermute | solution.py:544
  36.0 2.9 %collective-permute-done.12.refs_2_ = f32[4,32,128]{2,1,0:T(8,128)S(1)} collective-permute-done((f32[4,32,128]{2,1,0:T(8,128)S(1)}, f32[4,32,128]{2,1,0:T(8,128)S(1)}, u32[]{:S(2)}, u32[]{:S(2)}) %collective-permute-start.12) | collective-permute-done | bytes 65568 | tf_op jit(solution)/shard_map/ppermute | solution.py:544
  38.9 0.0 collective-permute-done.11.refs_1_
  38.9 0.8 %join.1 = f32[4,128,128]{2,1,0:T(8,128)} custom-call(f32[4,32,128]{2,1,0:T(8,128)S(1)} %update.1.refs_0_, f32[4,32,128]{2,1,0:T(8,128)S(1)} %collective-permute-done.11.refs_1_, f32[4,32,128]{2,1,0:T(8,128)S(1)} %collective-permute-done.12.refs_2_, f32[4,32,128]{2,1,0:T(8,128)S(1)} %collective-permute-done.13.refs_3_), custom_call_target="tpu_custom_call" | custom-call | tf_op jit(solution)/shard_map/join/pallas_call | solution.py:545
  (2 shorter events, 0.0 us)
Async XLA Ops:
  0.0 7.5 %collective-permute-start.1 = (f32[4,128,128]{2,1,0:T(8,128)}, f32[4,128,128]{2,1,0:T(8,128)S(1)}, u32[]{:S(2)}, u32[]{:S(2)}) collective-permute-start(f32[4,128,128]{2,1,0:T(8,128)} %maps_any.1), channel_id=1, source_target_pairs={{0,28},{4,0},{8,4},{12,8},{16,12},{20,16},{24,20},{28,24},{1,29},{... | collective-permute-start | bytes 786440 | tf_op jit(solution)/shard_map/ppermute | solution.py:435
  5.8 10.7 %collective-permute-start.5 = (f32[128,128]{1,0:T(8,128)S(1)}, f32[128,128]{1,0:T(8,128)S(1)}, u32[]{:S(2)}, u32[]{:S(2)}) collective-permute-start(f32[128,128]{1,0:T(8,128)S(1)} %get-tuple-element.45.one), channel_id=1, source_target_pairs={{28,29},{29,28},{30,31},{31,30}} | collective-permute-start | bytes 196616 | tf_op jit(solution)/shard_map/ppermute | solution.py:473
  9.1 9.3 %collective-permute-start.2 = (f32[160,128]{1,0:T(8,128)S(1)}, f32[160,128]{1,0:T(8,128)S(1)}, u32[]{:S(2)}, u32[]{:S(2)}) collective-permute-start(f32[160,128]{1,0:T(8,128)S(1)} %get-tuple-element.42), channel_id=1, source_target_pairs={{0,3},{1,2},{2,1},{3,0},{4,7},{5,6},{6,5},{7,4},{8,11},{9,10},{10,... | collective-permute-start | bytes 245768 | tf_op jit(solution)/shard_map/ppermute | solution.py:500
  12.8 6.3 %collective-permute-start.3 = (f32[160,128]{1,0:T(8,128)S(1)}, f32[160,128]{1,0:T(8,128)S(1)}, u32[]{:S(2)}, u32[]{:S(2)}) collective-permute-start(f32[160,128]{1,0:T(8,128)S(1)} %get-tuple-element.43), channel_id=1, source_target_pairs={{0,1},{1,0},{2,3},{3,2},{4,5},{5,4},{6,7},{7,6},{8,9},{9,8},{10,11... | collective-permute-start | bytes 245768 | tf_op jit(solution)/shard_map/ppermute | solution.py:500
  12.8 6.3 %collective-permute-start.4 = (f32[160,128]{1,0:T(8,128)S(1)}, f32[160,128]{1,0:T(8,128)S(1)}, u32[]{:S(2)}, u32[]{:S(2)}) collective-permute-start(f32[160,128]{1,0:T(8,128)S(1)} %get-tuple-element.44), channel_id=1, source_target_pairs={{0,2},{1,3},{2,0},{3,1},{4,6},{5,7},{6,4},{7,5},{8,10},{9,11},{10,... | collective-permute-start | bytes 245768 | tf_op jit(solution)/shard_map/ppermute | solution.py:500
  13.6 4.8 %collective-permute-start = (f32[128,128]{1,0:T(8,128)S(1)}, f32[128,128]{1,0:T(8,128)S(1)}, u32[]{:S(2)}, u32[]{:S(2)}) collective-permute-start(f32[128,128]{1,0:T(8,128)S(1)} %get-tuple-element.34), channel_id=1, source_target_pairs={{0,28},{4,0},{8,4},{12,8},{16,12},{20,16},{24,20},{28,24},{1,29},{... | collective-permute-start | bytes 196616 | tf_op jit(solution)/shard_map/ppermute | solution.py:484
  16.5 1.9 %collective-permute-start.6 = (f32[128,128]{1,0:T(8,128)S(1)}, f32[128,128]{1,0:T(8,128)S(1)}, u32[]{:S(2)}, u32[]{:S(2)}) collective-permute-start(f32[128,128]{1,0:T(8,128)S(1)} %pair.1.refs_11_), channel_id=1, source_target_pairs={{28,30},{29,31},{30,28},{31,29}} | collective-permute-start | bytes 196616 | tf_op jit(solution)/shard_map/ppermute | solution.py:473
  20.5 6.0 %collective-permute-start.8 = (f32[4,32,128]{2,1,0:T(8,128)S(1)}, f32[4,32,128]{2,1,0:T(8,128)S(1)}, u32[]{:S(2)}, u32[]{:S(2)}) collective-permute-start(f32[4,32,128]{2,1,0:T(8,128)S(1)} %get-tuple-element.48), channel_id=1, source_target_pairs={{0,6},{1,7},{2,0},{3,1},{4,10},{5,11},{6,4},{7,5},{8,14},{9,15},{1... | collective-permute-start | bytes 196616 | tf_op jit(solution)/shard_map/ppermute | solution.py:531
  21.0 5.6 %collective-permute-start.9 = (f32[4,32,128]{2,1,0:T(8,128)S(1)}, f32[4,32,128]{2,1,0:T(8,128)S(1)}, u32[]{:S(2)}, u32[]{:S(2)}) collective-permute-start(f32[4,32,128]{2,1,0:T(8,128)S(1)} %get-tuple-element.49), channel_id=1, source_target_pairs={{0,1},{1,0},{2,7},{3,6},{4,5},{5,4},{6,11},{7,10},{8,9},{9,8},{10,... | collective-permute-start | bytes 196616 | tf_op jit(solution)/shard_map/ppermute | solution.py:531
  22.7 6.6 %collective-permute-start.10 = (f32[4,32,128]{2,1,0:T(8,128)S(1)}, f32[4,32,128]{2,1,0:T(8,128)S(1)}, u32[]{:S(2)}, u32[]{:S(2)}) collective-permute-start(f32[4,32,128]{2,1,0:T(8,128)S(1)} %get-tuple-element.50), channel_id=1, source_target_pairs={{0,7},{1,6},{2,1},{3,0},{4,11},{5,10},{6,5},{7,4},{8,15},{9,14},{1... | collective-permute-start | bytes 196616 | tf_op jit(solution)/shard_map/ppermute | solution.py:531
  24.6 4.8 %collective-permute-start.7 = (f32[4,32,128]{2,1,0:T(8,128)S(1)}, f32[4,32,128]{2,1,0:T(8,128)S(1)}, u32[]{:S(2)}, u32[]{:S(2)}) collective-permute-start(f32[4,32,128]{2,1,0:T(8,128)S(1)} %get-tuple-element.47.refs_2_), channel_id=1, source_target_pairs={{2,6},{3,7},{6,10},{7,11},{10,14},{11,15},{14,18},{15,19},{18,22},... | collective-permute-start | bytes 196616 | tf_op jit(solution)/shard_map/ppermute | solution.py:531
  29.4 6.6 %collective-permute-start.13 = (f32[4,32,128]{2,1,0:T(8,128)S(1)}, f32[4,32,128]{2,1,0:T(8,128)S(1)}, u32[]{:S(2)}, u32[]{:S(2)}) collective-permute-start(f32[4,32,128]{2,1,0:T(8,128)S(1)} %update.1.refs_0_), channel_id=1, source_target_pairs={{0,3},{1,2},{2,1},{3,0},{4,7},{5,6},{6,5},{7,4},{8,11},{9,10},{10,... | collective-permute-start | bytes 196616 | tf_op jit(solution)/shard_map/ppermute | solution.py:544
  33.7 5.2 %collective-permute-start.12 = (f32[4,32,128]{2,1,0:T(8,128)S(1)}, f32[4,32,128]{2,1,0:T(8,128)S(1)}, u32[]{:S(2)}, u32[]{:S(2)}) collective-permute-start(f32[4,32,128]{2,1,0:T(8,128)S(1)} %update.1.refs_0_), channel_id=1, source_target_pairs={{0,2},{1,3},{2,0},{3,1},{4,6},{5,7},{6,4},{7,5},{8,10},{9,11},{10,... | collective-permute-start | bytes 196616 | tf_op jit(solution)/shard_map/ppermute | solution.py:544
  33.7 5.2 %collective-permute-start.11 = (f32[4,32,128]{2,1,0:T(8,128)S(1)}, f32[4,32,128]{2,1,0:T(8,128)S(1)}, u32[]{:S(2)}, u32[]{:S(2)}) collective-permute-start(f32[4,32,128]{2,1,0:T(8,128)S(1)} %update.1.refs_0_), channel_id=1, source_target_pairs={{0,1},{1,0},{2,3},{3,2},{4,5},{5,4},{6,7},{7,6},{8,9},{9,8},{10,11... | collective-permute-start | bytes 196616 | tf_op jit(solution)/shard_map/ppermute | solution.py:544

commit v8 on v7

--- a/solution.py
+++ b/solution.py
@@ -427,7 +427,7 @@
     shape = jax.ShapeDtypeStruct
     half_rows = length // count
     rest = [k for k in range(1, count) if k != count // 2]
-    first_order, second_order = rest[::-1] + [count // 2], [count // 2] + rest
+    first_order, second_order = rest[::-1] + [count // 2], [count // 2] + rest[::-1]
     square = shape((length, length), f32)
     share = shape((materials, half_rows, length), f32)
 

time: 39.9 us -> 39.7 us (level)
  starting transfers between devices: 21.7 us -> 20.4 us
  waiting for transfers between devices: 11.2 us -> 12.3 us
    ppermute x4, starting transfers between devices: 4.71 us -> 2.84 us  [per_device(): lax.ppermute(sends[k], both, [p for p in pairs if p[0] != p[1]])]
    ppermute x4, waiting for transfers between devices: 4.09 us -> 5.18 us  [per_device(): lax.ppermute(sends[k], both, [p for p in pairs if p[0] != p[1]])]
    ppermute x3, starting transfers between devices: 4.97 us -> 5.51 us  [per_device(): parts.append(lax.ppermute(new, 'wave', [(w, w ^ k) for w in range(count)]))]
where the time goes in v8:
time: 39.7 us; the launch traced here: 39.6 us
  starting transfers between devices  20.4 us (51%)
  waiting for transfers between devices  12.3 us (31%)
  Pallas kernels  6.75 us (17%)
    ppermute x3, starting transfers between devices, per_device(): parts.append(lax.ppermute(new, 'wave', [(w, w ^ k) for w in range(count)]))  5.51 us
    ppermute x4, waiting for transfers between devices, per_device(): lax.ppermute(sends[k], both, [p for p in pairs if p[0] != p[1]])  5.18 us
    ppermute x3, waiting for transfers between devices, per_device(): parts.append(lax.ppermute(new, 'wave', [(w, w ^ k) for w in range(count)]))  4.58 us
    ppermute x3, starting transfers between devices, per_device(): lax.ppermute(messages[k], 'wave', [(w, w ^ k) for w in range(count)])  4.45 us
    ppermute x1, starting transfers between devices, per_device(): halo = lax.ppermute(maps, 'tile', ring)  3.33 us
    ppermute x1, starting transfers between devices, per_device(): left_root = lax.ppermute(left, 'tile', ring)  2.94 us
    ppermute x4, starting transfers between devices, per_device(): lax.ppermute(sends[k], both, [p for p in pairs if p[0] != p[1]])  2.84 us
    pallas_call x1, Pallas kernels, per_device(): pl.pallas_call(first_kernel, out_shape=(shape((slots, 3, length, length),...  2.48 us
  transfers between devices with their start and end apart: 14, of which 8 were waited for; matrix products, arithmetic and copies ran while one was open for 0% of the time, Pallas kernels for 11%

profile of v8, /device:TPU:0, one launch (start us, length us, event | category | flops | bytes accessed | tf_op | source)
XLA Modules:
  0.0 39.6 jit_solution(13546676926315436850)
XLA Ops:
  0.0 3.3 %collective-permute-start.1 = (f32[4,128,128]{2,1,0:T(8,128)}, f32[4,128,128]{2,1,0:T(8,128)S(1)}, u32[]{:S(2)}, u32[]{:S(2)}) collective-permute-start(f32[4,128,128]{2,1,0:T(8,128)} %maps_any.1), channel_id=1, source_target_pairs={{0,28},{4,0},{8,4},{12,8},{16,12},{20,16},{24,20},{28,24},{1,29},{... | collective-permute-start | bytes 786440 | tf_op jit(solution)/shard_map/ppermute | solution.py:435
  3.3 2.5 %tables.1 = (bf16[12,3,128,128]{3,2,1,0:T(8,128)(2,1)S(1)}, f32[12,24,128]{2,1,0:T(8,128)S(1)}, f32[12,2,128,128]{3,2,1,0:T(8,128)S(1)}, f32[12,2,128,128]{3,2,1...) custom-call(f32[12]{0:T(128)} %spectrum_any.1, ...), custom_call_target="tpu_custom_call" | custom-call | flops 1000000000 | bytes 4194304 | tf_op jit(solution)/shard_map/tables/pallas_call | solution.py:439
  5.8 0.7 %collective-permute-start.5 = (f32[128,128]{1,0:T(8,128)S(1)}, f32[128,128]{1,0:T(8,128)S(1)}, u32[]{:S(2)}, u32[]{:S(2)}) collective-permute-start(f32[128,128]{1,0:T(8,128)S(1)} %get-tuple-element.45.one), channel_id=1, source_target_pairs={{28,29},{29,28},{30,31},{31,30}} | collective-permute-start | bytes 196616 | tf_op jit(solution)/shard_map/ppermute | solution.py:473
  6.5 0.4 power.1
  6.9 0.6 %collective-permute-done.1.refs_1_ = f32[4,128,128]{2,1,0:T(8,128)S(1)} collective-permute-done((f32[4,128,128]{2,1,0:T(8,128)}, f32[4,128,128]{2,1,0:T(8,128)S(1)}, u32[]{:S(2)}, u32[]{:S(2)}) %collective-permute-start.1) | collective-permute-done | bytes 262176 | tf_op jit(solution)/shard_map/ppermute | solution.py:435
  7.5 1.6 %forward.1 = (f32[12,2,128,128]{3,2,1,0:T(8,128)S(1)}, f32[12,128,256]{2,1,0:T(8,128)S(1)}, f32[160,128]{1,0:T(8,128)S(1)}, f32[160,128]{1,0:T(8,128)S(1)}, f32[...) custom-call(f32[12,2,128,128]{3,2,1,0:T(8,128)S(1)} %get-tuple-element.36.refs_0_, ...), custom_call_target="tpu_custom_call" | custom-call | tf_op jit(solution)/shard_map/forward/pallas_call | solution.py:486
  9.1 3.7 %collective-permute-start.2 = (f32[160,128]{1,0:T(8,128)S(1)}, f32[160,128]{1,0:T(8,128)S(1)}, u32[]{:S(2)}, u32[]{:S(2)}) collective-permute-start(f32[160,128]{1,0:T(8,128)S(1)} %get-tuple-element.42), channel_id=1, source_target_pairs={{0,3},{1,2},{2,1},{3,0},{4,7},{5,6},{6,5},{7,4},{8,11},{9,10},{10,... | collective-permute-start | bytes 245768 | tf_op jit(solution)/shard_map/ppermute | solution.py:500
  12.8 0.0 collective-permute-start.3
  12.8 0.8 %collective-permute-start.4 = (f32[160,128]{1,0:T(8,128)S(1)}, f32[160,128]{1,0:T(8,128)S(1)}, u32[]{:S(2)}, u32[]{:S(2)}) collective-permute-start(f32[160,128]{1,0:T(8,128)S(1)} %get-tuple-element.44), channel_id=1, source_target_pairs={{0,2},{1,3},{2,0},{3,1},{4,6},{5,7},{6,4},{7,5},{8,10},{9,11},{10,... | collective-permute-start | bytes 245768 | tf_op jit(solution)/shard_map/ppermute | solution.py:500
  13.6 2.9 %collective-permute-start = (f32[128,128]{1,0:T(8,128)S(1)}, f32[128,128]{1,0:T(8,128)S(1)}, u32[]{:S(2)}, u32[]{:S(2)}) collective-permute-start(f32[128,128]{1,0:T(8,128)S(1)} %get-tuple-element.34), channel_id=1, source_target_pairs={{0,28},{4,0},{8,4},{12,8},{16,12},{20,16},{24,20},{28,24},{1,29},{... | collective-permute-start | bytes 196616 | tf_op jit(solution)/shard_map/ppermute | solution.py:484
  16.5 0.0 collective-permute-done.5.other
  16.5 0.7 %collective-permute-start.6 = (f32[128,128]{1,0:T(8,128)S(1)}, f32[128,128]{1,0:T(8,128)S(1)}, u32[]{:S(2)}, u32[]{:S(2)}) collective-permute-start(f32[128,128]{1,0:T(8,128)S(1)} %pair.1.refs_11_), channel_id=1, source_target_pairs={{28,30},{29,31},{30,28},{31,29}} | collective-permute-start | bytes 196616 | tf_op jit(solution)/shard_map/ppermute | solution.py:473
  17.2 1.2 %collective-permute-done.refs_1_ = f32[128,128]{1,0:T(8,128)S(1)} collective-permute-done((f32[128,128]{1,0:T(8,128)S(1)}, f32[128,128]{1,0:T(8,128)S(1)}, u32[]{:S(2)}, u32[]{:S(2)}) %collective-permute-start) | collective-permute-done | bytes 65568 | tf_op jit(solution)/shard_map/ppermute | solution.py:484
  18.4 0.0 collective-permute-done.6.refs_12_
  18.4 0.0 collective-permute-done.2.refs_8_
  18.4 0.7 %collective-permute-done.3.refs_9_ = f32[160,128]{1,0:T(8,128)S(1)} collective-permute-done((f32[160,128]{1,0:T(8,128)S(1)}, f32[160,128]{1,0:T(8,128)S(1)}, u32[]{:S(2)}, u32[]{:S(2)}) %collective-permute-start.3) | collective-permute-done | bytes 81952 | tf_op jit(solution)/shard_map/ppermute | solution.py:500
  19.1 0.0 collective-permute-done.4.refs_10_
  19.1 1.4 %backward.1 = (f32[4,32,128]{2,1,0:T(8,128)S(1)}, f32[4,32,128]{2,1,0:T(8,128)S(1)}, f32[4,32,128]{2,1,0:T(8,128)S(1)}, f32[4,32,128]{2,1,0:T(8,128)S(1)}, f32[32,128]{1,0:T(8,128)S(1)}) custom-call(f32[128,128]{1,0:T(8,128)S(1)} %get-tuple-element.33.refs_0_, f32[128,128]{1,0:T(8,128)S(1)} %collective-permute-done.refs_1_, ...), custom_call_target="tpu_custom_call" | custom-call | tf_op jit(solution)/shard_map/backward/pallas_call | solution.py:511
  20.5 0.5 %collective-permute-start.8 = (f32[4,32,128]{2,1,0:T(8,128)S(1)}, f32[4,32,128]{2,1,0:T(8,128)S(1)}, u32[]{:S(2)}, u32[]{:S(2)}) collective-permute-start(f32[4,32,128]{2,1,0:T(8,128)S(1)} %get-tuple-element.48), channel_id=1, source_target_pairs={{0,6},{1,7},{2,0},{3,1},{4,10},{5,11},{6,4},{7,5},{8,14},{9,15},{1... | collective-permute-start | bytes 196616 | tf_op jit(solution)/shard_map/ppermute | solution.py:531
  21.0 1.2 %collective-permute-start.9 = (f32[4,32,128]{2,1,0:T(8,128)S(1)}, f32[4,32,128]{2,1,0:T(8,128)S(1)}, u32[]{:S(2)}, u32[]{:S(2)}) collective-permute-start(f32[4,32,128]{2,1,0:T(8,128)S(1)} %get-tuple-element.49), channel_id=1, source_target_pairs={{0,7},{1,6},{2,1},{3,0},{4,11},{5,10},{6,5},{7,4},{8,15},{9,14},{1... | collective-permute-start | bytes 196616 | tf_op jit(solution)/shard_map/ppermute | solution.py:531
  22.2 0.5 %collective-permute-start.10 = (f32[4,32,128]{2,1,0:T(8,128)S(1)}, f32[4,32,128]{2,1,0:T(8,128)S(1)}, u32[]{:S(2)}, u32[]{:S(2)}) collective-permute-start(f32[4,32,128]{2,1,0:T(8,128)S(1)} %get-tuple-element.50), channel_id=1, source_target_pairs={{0,1},{1,0},{2,7},{3,6},{4,5},{5,4},{6,11},{7,10},{8,9},{9,8},{10,... | collective-permute-start | bytes 196616 | tf_op jit(solution)/shard_map/ppermute | solution.py:531
  22.7 0.7 %collective-permute-start.7 = (f32[4,32,128]{2,1,0:T(8,128)S(1)}, f32[4,32,128]{2,1,0:T(8,128)S(1)}, u32[]{:S(2)}, u32[]{:S(2)}) collective-permute-start(f32[4,32,128]{2,1,0:T(8,128)S(1)} %get-tuple-element.47.refs_2_), channel_id=1, source_target_pairs={{2,6},{3,7},{6,10},{7,11},{10,14},{11,15},{14,18},{15,19},{18,22},... | collective-permute-start | bytes 196616 | tf_op jit(solution)/shard_map/ppermute | solution.py:531
  23.4 4.6 %collective-permute-done.8.refs_4_ = f32[4,32,128]{2,1,0:T(8,128)S(1)} collective-permute-done((f32[4,32,128]{2,1,0:T(8,128)S(1)}, f32[4,32,128]{2,1,0:T(8,128)S(1)}, u32[]{:S(2)}, u32[]{:S(2)}) %collective-permute-start.8) | collective-permute-done | bytes 65568 | tf_op jit(solution)/shard_map/ppermute | solution.py:531
  28.0 0.0 collective-permute-done.9.refs_5_
  28.0 0.6 %collective-permute-done.10.refs_6_ = f32[4,32,128]{2,1,0:T(8,128)S(1)} collective-permute-done((f32[4,32,128]{2,1,0:T(8,128)S(1)}, f32[4,32,128]{2,1,0:T(8,128)S(1)}, u32[]{:S(2)}, u32[]{:S(2)}) %collective-permute-start.10) | collective-permute-done | bytes 65568 | tf_op jit(solution)/shard_map/ppermute | solution.py:531
  28.6 0.0 collective-permute-done.7.refs_3_
  28.6 4.3 %collective-permute-start.13 = (f32[4,32,128]{2,1,0:T(8,128)S(1)}, f32[4,32,128]{2,1,0:T(8,128)S(1)}, u32[]{:S(2)}, u32[]{:S(2)}) collective-permute-start(f32[4,32,128]{2,1,0:T(8,128)S(1)} %update.1.refs_0_), channel_id=1, source_target_pairs={{0,3},{1,2},{2,1},{3,0},{4,7},{5,6},{6,5},{7,4},{8,11},{9,10},{10,... | collective-permute-start | bytes 196616 | tf_op jit(solution)/shard_map/ppermute | solution.py:544
  32.9 0.8 %collective-permute-start.12 = (f32[4,32,128]{2,1,0:T(8,128)S(1)}, f32[4,32,128]{2,1,0:T(8,128)S(1)}, u32[]{:S(2)}, u32[]{:S(2)}) collective-permute-start(f32[4,32,128]{2,1,0:T(8,128)S(1)} %update.1.refs_0_), channel_id=1, source_target_pairs={{0,2},{1,3},{2,0},{3,1},{4,6},{5,7},{6,4},{7,5},{8,10},{9,11},{10,... | collective-permute-start | bytes 196616 | tf_op jit(solution)/shard_map/ppermute | solution.py:544
  33.6 0.5 %collective-permute-start.11 = (f32[4,32,128]{2,1,0:T(8,128)S(1)}, f32[4,32,128]{2,1,0:T(8,128)S(1)}, u32[]{:S(2)}, u32[]{:S(2)}) collective-permute-start(f32[4,32,128]{2,1,0:T(8,128)S(1)} %update.1.refs_0_), channel_id=1, source_target_pairs={{0,1},{1,0},{2,3},{3,2},{4,5},{5,4},{6,7},{7,6},{8,9},{9,8},{10,11... | collective-permute-start | bytes 196616 | tf_op jit(solution)/shard_map/ppermute | solution.py:544
  34.1 1.1 %collective-permute-done.13.refs_3_ = f32[4,32,128]{2,1,0:T(8,128)S(1)} collective-permute-done((f32[4,32,128]{2,1,0:T(8,128)S(1)}, f32[4,32,128]{2,1,0:T(8,128)S(1)}, u32[]{:S(2)}, u32[]{:S(2)}) %collective-permute-start.13) | collective-permute-done | bytes 65568 | tf_op jit(solution)/shard_map/ppermute | solution.py:544
  35.2 3.0 %collective-permute-done.12.refs_2_ = f32[4,32,128]{2,1,0:T(8,128)S(1)} collective-permute-done((f32[4,32,128]{2,1,0:T(8,128)S(1)}, f32[4,32,128]{2,1,0:T(8,128)S(1)}, u32[]{:S(2)}, u32[]{:S(2)}) %collective-permute-start.12) | collective-permute-done | bytes 65568 | tf_op jit(solution)/shard_map/ppermute | solution.py:544
  38.2 0.5 %collective-permute-done.11.refs_1_ = f32[4,32,128]{2,1,0:T(8,128)S(1)} collective-permute-done((f32[4,32,128]{2,1,0:T(8,128)S(1)}, f32[4,32,128]{2,1,0:T(8,128)S(1)}, u32[]{:S(2)}, u32[]{:S(2)}) %collective-permute-start.11) | collective-permute-done | bytes 65568 | tf_op jit(solution)/shard_map/ppermute | solution.py:544
  38.7 0.8 %join.1 = f32[4,128,128]{2,1,0:T(8,128)} custom-call(f32[4,32,128]{2,1,0:T(8,128)S(1)} %update.1.refs_0_, f32[4,32,128]{2,1,0:T(8,128)S(1)} %collective-permute-done.11.refs_1_, f32[4,32,128]{2,1,0:T(8,128)S(1)} %collective-permute-done.12.refs_2_, f32[4,32,128]{2,1,0:T(8,128)S(1)} %collective-permute-done.13.refs_3_), custom_call_target="tpu_custom_call" | custom-call | tf_op jit(solution)/shard_map/join/pallas_call | solution.py:545
  (2 shorter events, 0.0 us)
Async XLA Ops:
  0.0 7.5 %collective-permute-start.1 = (f32[4,128,128]{2,1,0:T(8,128)}, f32[4,128,128]{2,1,0:T(8,128)S(1)}, u32[]{:S(2)}, u32[]{:S(2)}) collective-permute-start(f32[4,128,128]{2,1,0:T(8,128)} %maps_any.1), channel_id=1, source_target_pairs={{0,28},{4,0},{8,4},{12,8},{16,12},{20,16},{24,20},{28,24},{1,29},{... | collective-permute-start | bytes 786440 | tf_op jit(solution)/shard_map/ppermute | solution.py:435
  5.8 10.7 %collective-permute-start.5 = (f32[128,128]{1,0:T(8,128)S(1)}, f32[128,128]{1,0:T(8,128)S(1)}, u32[]{:S(2)}, u32[]{:S(2)}) collective-permute-start(f32[128,128]{1,0:T(8,128)S(1)} %get-tuple-element.45.one), channel_id=1, source_target_pairs={{28,29},{29,28},{30,31},{31,30}} | collective-permute-start | bytes 196616 | tf_op jit(solution)/shard_map/ppermute | solution.py:473
  9.1 9.3 %collective-permute-start.2 = (f32[160,128]{1,0:T(8,128)S(1)}, f32[160,128]{1,0:T(8,128)S(1)}, u32[]{:S(2)}, u32[]{:S(2)}) collective-permute-start(f32[160,128]{1,0:T(8,128)S(1)} %get-tuple-element.42), channel_id=1, source_target_pairs={{0,3},{1,2},{2,1},{3,0},{4,7},{5,6},{6,5},{7,4},{8,11},{9,10},{10,... | collective-permute-start | bytes 245768 | tf_op jit(solution)/shard_map/ppermute | solution.py:500
  12.8 6.3 %collective-permute-start.3 = (f32[160,128]{1,0:T(8,128)S(1)}, f32[160,128]{1,0:T(8,128)S(1)}, u32[]{:S(2)}, u32[]{:S(2)}) collective-permute-start(f32[160,128]{1,0:T(8,128)S(1)} %get-tuple-element.43), channel_id=1, source_target_pairs={{0,1},{1,0},{2,3},{3,2},{4,5},{5,4},{6,7},{7,6},{8,9},{9,8},{10,11... | collective-permute-start | bytes 245768 | tf_op jit(solution)/shard_map/ppermute | solution.py:500
  12.8 6.3 %collective-permute-start.4 = (f32[160,128]{1,0:T(8,128)S(1)}, f32[160,128]{1,0:T(8,128)S(1)}, u32[]{:S(2)}, u32[]{:S(2)}) collective-permute-start(f32[160,128]{1,0:T(8,128)S(1)} %get-tuple-element.44), channel_id=1, source_target_pairs={{0,2},{1,3},{2,0},{3,1},{4,6},{5,7},{6,4},{7,5},{8,10},{9,11},{10,... | collective-permute-start | bytes 245768 | tf_op jit(solution)/shard_map/ppermute | solution.py:500
  13.6 4.8 %collective-permute-start = (f32[128,128]{1,0:T(8,128)S(1)}, f32[128,128]{1,0:T(8,128)S(1)}, u32[]{:S(2)}, u32[]{:S(2)}) collective-permute-start(f32[128,128]{1,0:T(8,128)S(1)} %get-tuple-element.34), channel_id=1, source_target_pairs={{0,28},{4,0},{8,4},{12,8},{16,12},{20,16},{24,20},{28,24},{1,29},{... | collective-permute-start | bytes 196616 | tf_op jit(solution)/shard_map/ppermute | solution.py:484
  16.5 1.9 %collective-permute-start.6 = (f32[128,128]{1,0:T(8,128)S(1)}, f32[128,128]{1,0:T(8,128)S(1)}, u32[]{:S(2)}, u32[]{:S(2)}) collective-permute-start(f32[128,128]{1,0:T(8,128)S(1)} %pair.1.refs_11_), channel_id=1, source_target_pairs={{28,30},{29,31},{30,28},{31,29}} | collective-permute-start | bytes 196616 | tf_op jit(solution)/shard_map/ppermute | solution.py:473
  20.5 7.5 %collective-permute-start.8 = (f32[4,32,128]{2,1,0:T(8,128)S(1)}, f32[4,32,128]{2,1,0:T(8,128)S(1)}, u32[]{:S(2)}, u32[]{:S(2)}) collective-permute-start(f32[4,32,128]{2,1,0:T(8,128)S(1)} %get-tuple-element.48), channel_id=1, source_target_pairs={{0,6},{1,7},{2,0},{3,1},{4,10},{5,11},{6,4},{7,5},{8,14},{9,15},{1... | collective-permute-start | bytes 196616 | tf_op jit(solution)/shard_map/ppermute | solution.py:531
  21.0 7.0 %collective-permute-start.9 = (f32[4,32,128]{2,1,0:T(8,128)S(1)}, f32[4,32,128]{2,1,0:T(8,128)S(1)}, u32[]{:S(2)}, u32[]{:S(2)}) collective-permute-start(f32[4,32,128]{2,1,0:T(8,128)S(1)} %get-tuple-element.49), channel_id=1, source_target_pairs={{0,7},{1,6},{2,1},{3,0},{4,11},{5,10},{6,5},{7,4},{8,15},{9,14},{1... | collective-permute-start | bytes 196616 | tf_op jit(solution)/shard_map/ppermute | solution.py:531
  22.2 6.3 %collective-permute-start.10 = (f32[4,32,128]{2,1,0:T(8,128)S(1)}, f32[4,32,128]{2,1,0:T(8,128)S(1)}, u32[]{:S(2)}, u32[]{:S(2)}) collective-permute-start(f32[4,32,128]{2,1,0:T(8,128)S(1)} %get-tuple-element.50), channel_id=1, source_target_pairs={{0,1},{1,0},{2,7},{3,6},{4,5},{5,4},{6,11},{7,10},{8,9},{9,8},{10,... | collective-permute-start | bytes 196616 | tf_op jit(solution)/shard_map/ppermute | solution.py:531
  22.7 5.8 %collective-permute-start.7 = (f32[4,32,128]{2,1,0:T(8,128)S(1)}, f32[4,32,128]{2,1,0:T(8,128)S(1)}, u32[]{:S(2)}, u32[]{:S(2)}) collective-permute-start(f32[4,32,128]{2,1,0:T(8,128)S(1)} %get-tuple-element.47.refs_2_), channel_id=1, source_target_pairs={{2,6},{3,7},{6,10},{7,11},{10,14},{11,15},{14,18},{15,19},{18,22},... | collective-permute-start | bytes 196616 | tf_op jit(solution)/shard_map/ppermute | solution.py:531
  28.6 6.6 %collective-permute-start.13 = (f32[4,32,128]{2,1,0:T(8,128)S(1)}, f32[4,32,128]{2,1,0:T(8,128)S(1)}, u32[]{:S(2)}, u32[]{:S(2)}) collective-permute-start(f32[4,32,128]{2,1,0:T(8,128)S(1)} %update.1.refs_0_), channel_id=1, source_target_pairs={{0,3},{1,2},{2,1},{3,0},{4,7},{5,6},{6,5},{7,4},{8,11},{9,10},{10,... | collective-permute-start | bytes 196616 | tf_op jit(solution)/shard_map/ppermute | solution.py:544
  32.9 5.3 %collective-permute-start.12 = (f32[4,32,128]{2,1,0:T(8,128)S(1)}, f32[4,32,128]{2,1,0:T(8,128)S(1)}, u32[]{:S(2)}, u32[]{:S(2)}) collective-permute-start(f32[4,32,128]{2,1,0:T(8,128)S(1)} %update.1.refs_0_), channel_id=1, source_target_pairs={{0,2},{1,3},{2,0},{3,1},{4,6},{5,7},{6,4},{7,5},{8,10},{9,11},{10,... | collective-permute-start | bytes 196616 | tf_op jit(solution)/shard_map/ppermute | solution.py:544
  33.6 5.1 %collective-permute-start.11 = (f32[4,32,128]{2,1,0:T(8,128)S(1)}, f32[4,32,128]{2,1,0:T(8,128)S(1)}, u32[]{:S(2)}, u32[]{:S(2)}) collective-permute-start(f32[4,32,128]{2,1,0:T(8,128)S(1)} %update.1.refs_0_), channel_id=1, source_target_pairs={{0,1},{1,0},{2,3},{3,2},{4,5},{5,4},{6,7},{7,6},{8,9},{9,8},{10,11... | collective-permute-start | bytes 196616 | tf_op jit(solution)/shard_map/ppermute | solution.py:544

commit v9 on v8

--- a/solution.py
+++ b/solution.py
@@ -389,7 +389,7 @@
 
 
 def join_kernel(count, *refs):
-    shares, out = refs[:count], refs[count]
+    shares, (whole, out, sems) = refs[:count], refs[count:]
     materials, length, _ = out.shape
     half = length // 2
     me = lax.axis_index("wave")
@@ -401,15 +401,19 @@
         @pl.when(me == position)
         def _():
             held = lambda q: shares[q ^ position]
-            for g in range(groups):
-                right, left = held(g), held(g + groups)
-                start = g * 2 * half_rows
-                for m in range(materials):
+            for m in range(materials):
+                for g in range(groups):
+                    right, left = held(g), held(g + groups)
+                    start = g * 2 * half_rows
                     r, l = right[m], left[m]
                     out[m, start : start + half_rows] = jnp.where(low, l, pltpu.roll(r, half, 1))
                     out[m, start + half_rows : start + 2 * half_rows] = jnp.where(
                         low, pltpu.roll(l, half, 1), r
                     )
+                pltpu.make_async_copy(out.at[m], whole.at[m], sems.at[m]).start()
+
+    for m in range(materials):
+        pltpu.make_async_copy(out.at[m], whole.at[m], sems.at[m]).wait()
 
 
 def in_hbm(array):
@@ -546,7 +550,11 @@
         lambda *refs: join_kernel(count, *refs),
         out_shape=shape((materials, length, length), f32),
         in_specs=[VM] * count,
-        out_specs=VM,
+        out_specs=ANY,
+        scratch_shapes=[
+            pltpu.VMEM((materials, length, length), f32),
+            pltpu.SemaphoreType.DMA((materials,)),
+        ],
         compiler_params=params(),
         name="join",
     )(*parts)

time: 39.7 us -> 39.7 us (level)
  no operation moved by 1% of the time
where the time goes in v9:
time: 39.7 us; the launch traced here: 39.5 us
  starting transfers between devices  20.4 us (51%)
  waiting for transfers between devices  12.3 us (31%)
  Pallas kernels  6.71 us (17%)
    ppermute x3, starting transfers between devices, per_device(): parts.append(lax.ppermute(new, 'wave', [(w, w ^ k) for w in range(count)]))  5.51 us
    ppermute x4, waiting for transfers between devices, per_device(): lax.ppermute(sends[k], both, [p for p in pairs if p[0] != p[1]])  5.18 us
    ppermute x3, waiting for transfers between devices, per_device(): parts.append(lax.ppermute(new, 'wave', [(w, w ^ k) for w in range(count)]))  4.58 us
    ppermute x3, starting transfers between devices, per_device(): lax.ppermute(messages[k], 'wave', [(w, w ^ k) for w in range(count)])  4.45 us
    ppermute x1, starting transfers between devices, per_device(): halo = lax.ppermute(maps, 'tile', ring)  3.33 us
    ppermute x1, starting transfers between devices, per_device(): left_root = lax.ppermute(left, 'tile', ring)  2.94 us
    ppermute x4, starting transfers between devices, per_device(): lax.ppermute(sends[k], both, [p for p in pairs if p[0] != p[1]])  2.84 us
    pallas_call x1, Pallas kernels, per_device(): pl.pallas_call(first_kernel, out_shape=(shape((slots, 3, length, length),...  2.48 us
  transfers between devices with their start and end apart: 14, of which 8 were waited for; matrix products, arithmetic and copies ran while one was open for 0% of the time, Pallas kernels for 11%

profile of v9, /device:TPU:0, one launch (start us, length us, event | category | flops | bytes accessed | tf_op | source)
XLA Modules:
  0.0 39.5 jit_solution(2355263955012396227)
XLA Ops:
  0.0 3.3 %collective-permute-start.1 = (f32[4,128,128]{2,1,0:T(8,128)}, f32[4,128,128]{2,1,0:T(8,128)S(1)}, u32[]{:S(2)}, u32[]{:S(2)}) collective-permute-start(f32[4,128,128]{2,1,0:T(8,128)} %maps_any.1), channel_id=1, source_target_pairs={{0,28},{4,0},{8,4},{12,8},{16,12},{20,16},{24,20},{28,24},{1,29},{... | collective-permute-start | bytes 786440 | tf_op jit(solution)/shard_map/ppermute | solution.py:439
  3.3 2.5 %tables.1 = (bf16[12,3,128,128]{3,2,1,0:T(8,128)(2,1)S(1)}, f32[12,24,128]{2,1,0:T(8,128)S(1)}, f32[12,2,128,128]{3,2,1,0:T(8,128)S(1)}, f32[12,2,128,128]{3,2,1...) custom-call(f32[12]{0:T(128)} %spectrum_any.1, ...), custom_call_target="tpu_custom_call" | custom-call | flops 1000000000 | bytes 4194304 | tf_op jit(solution)/shard_map/tables/pallas_call | solution.py:443
  5.8 0.7 %collective-permute-start.5 = (f32[128,128]{1,0:T(8,128)S(1)}, f32[128,128]{1,0:T(8,128)S(1)}, u32[]{:S(2)}, u32[]{:S(2)}) collective-permute-start(f32[128,128]{1,0:T(8,128)S(1)} %get-tuple-element.45.one), channel_id=1, source_target_pairs={{28,29},{29,28},{30,31},{31,30}} | collective-permute-start | bytes 196616 | tf_op jit(solution)/shard_map/ppermute | solution.py:477
  6.5 0.4 power.1
  6.9 0.6 %collective-permute-done.1.refs_1_ = f32[4,128,128]{2,1,0:T(8,128)S(1)} collective-permute-done((f32[4,128,128]{2,1,0:T(8,128)}, f32[4,128,128]{2,1,0:T(8,128)S(1)}, u32[]{:S(2)}, u32[]{:S(2)}) %collective-permute-start.1) | collective-permute-done | bytes 262176 | tf_op jit(solution)/shard_map/ppermute | solution.py:439
  7.5 1.6 %forward.1 = (f32[12,2,128,128]{3,2,1,0:T(8,128)S(1)}, f32[12,128,256]{2,1,0:T(8,128)S(1)}, f32[160,128]{1,0:T(8,128)S(1)}, f32[160,128]{1,0:T(8,128)S(1)}, f32[...) custom-call(f32[12,2,128,128]{3,2,1,0:T(8,128)S(1)} %get-tuple-element.36.refs_0_, ...), custom_call_target="tpu_custom_call" | custom-call | tf_op jit(solution)/shard_map/forward/pallas_call | solution.py:490
  9.1 3.7 %collective-permute-start.2 = (f32[160,128]{1,0:T(8,128)S(1)}, f32[160,128]{1,0:T(8,128)S(1)}, u32[]{:S(2)}, u32[]{:S(2)}) collective-permute-start(f32[160,128]{1,0:T(8,128)S(1)} %get-tuple-element.42), channel_id=1, source_target_pairs={{0,3},{1,2},{2,1},{3,0},{4,7},{5,6},{6,5},{7,4},{8,11},{9,10},{10,... | collective-permute-start | bytes 245768 | tf_op jit(solution)/shard_map/ppermute | solution.py:504
  12.8 0.0 collective-permute-start.3
  12.8 0.8 %collective-permute-start.4 = (f32[160,128]{1,0:T(8,128)S(1)}, f32[160,128]{1,0:T(8,128)S(1)}, u32[]{:S(2)}, u32[]{:S(2)}) collective-permute-start(f32[160,128]{1,0:T(8,128)S(1)} %get-tuple-element.44), channel_id=1, source_target_pairs={{0,2},{1,3},{2,0},{3,1},{4,6},{5,7},{6,4},{7,5},{8,10},{9,11},{10,... | collective-permute-start | bytes 245768 | tf_op jit(solution)/shard_map/ppermute | solution.py:504
  13.6 2.9 %collective-permute-start = (f32[128,128]{1,0:T(8,128)S(1)}, f32[128,128]{1,0:T(8,128)S(1)}, u32[]{:S(2)}, u32[]{:S(2)}) collective-permute-start(f32[128,128]{1,0:T(8,128)S(1)} %get-tuple-element.34), channel_id=1, source_target_pairs={{0,28},{4,0},{8,4},{12,8},{16,12},{20,16},{24,20},{28,24},{1,29},{... | collective-permute-start | bytes 196616 | tf_op jit(solution)/shard_map/ppermute | solution.py:488
  16.5 0.0 collective-permute-done.5.other
  16.5 0.7 %collective-permute-start.6 = (f32[128,128]{1,0:T(8,128)S(1)}, f32[128,128]{1,0:T(8,128)S(1)}, u32[]{:S(2)}, u32[]{:S(2)}) collective-permute-start(f32[128,128]{1,0:T(8,128)S(1)} %pair.1.refs_11_), channel_id=1, source_target_pairs={{28,30},{29,31},{30,28},{31,29}} | collective-permute-start | bytes 196616 | tf_op jit(solution)/shard_map/ppermute | solution.py:477
  17.2 1.2 %collective-permute-done.refs_1_ = f32[128,128]{1,0:T(8,128)S(1)} collective-permute-done((f32[128,128]{1,0:T(8,128)S(1)}, f32[128,128]{1,0:T(8,128)S(1)}, u32[]{:S(2)}, u32[]{:S(2)}) %collective-permute-start) | collective-permute-done | bytes 65568 | tf_op jit(solution)/shard_map/ppermute | solution.py:488
  18.4 0.0 collective-permute-done.6.refs_12_
  18.4 0.0 collective-permute-done.2.refs_8_
  18.4 0.7 %collective-permute-done.3.refs_9_ = f32[160,128]{1,0:T(8,128)S(1)} collective-permute-done((f32[160,128]{1,0:T(8,128)S(1)}, f32[160,128]{1,0:T(8,128)S(1)}, u32[]{:S(2)}, u32[]{:S(2)}) %collective-permute-start.3) | collective-permute-done | bytes 81952 | tf_op jit(solution)/shard_map/ppermute | solution.py:504
  19.1 0.0 collective-permute-done.4.refs_10_
  19.1 1.4 %backward.1 = (f32[4,32,128]{2,1,0:T(8,128)S(1)}, f32[4,32,128]{2,1,0:T(8,128)S(1)}, f32[4,32,128]{2,1,0:T(8,128)S(1)}, f32[4,32,128]{2,1,0:T(8,128)S(1)}, f32[32,128]{1,0:T(8,128)S(1)}) custom-call(f32[128,128]{1,0:T(8,128)S(1)} %get-tuple-element.33.refs_0_, f32[128,128]{1,0:T(8,128)S(1)} %collective-permute-done.refs_1_, ...), custom_call_target="tpu_custom_call" | custom-call | tf_op jit(solution)/shard_map/backward/pallas_call | solution.py:515
  20.5 0.5 %collective-permute-start.8 = (f32[4,32,128]{2,1,0:T(8,128)S(1)}, f32[4,32,128]{2,1,0:T(8,128)S(1)}, u32[]{:S(2)}, u32[]{:S(2)}) collective-permute-start(f32[4,32,128]{2,1,0:T(8,128)S(1)} %get-tuple-element.48), channel_id=1, source_target_pairs={{0,6},{1,7},{2,0},{3,1},{4,10},{5,11},{6,4},{7,5},{8,14},{9,15},{1... | collective-permute-start | bytes 196616 | tf_op jit(solution)/shard_map/ppermute | solution.py:535
  21.0 1.2 %collective-permute-start.9 = (f32[4,32,128]{2,1,0:T(8,128)S(1)}, f32[4,32,128]{2,1,0:T(8,128)S(1)}, u32[]{:S(2)}, u32[]{:S(2)}) collective-permute-start(f32[4,32,128]{2,1,0:T(8,128)S(1)} %get-tuple-element.49), channel_id=1, source_target_pairs={{0,7},{1,6},{2,1},{3,0},{4,11},{5,10},{6,5},{7,4},{8,15},{9,14},{1... | collective-permute-start | bytes 196616 | tf_op jit(solution)/shard_map/ppermute | solution.py:535
  22.2 0.5 %collective-permute-start.10 = (f32[4,32,128]{2,1,0:T(8,128)S(1)}, f32[4,32,128]{2,1,0:T(8,128)S(1)}, u32[]{:S(2)}, u32[]{:S(2)}) collective-permute-start(f32[4,32,128]{2,1,0:T(8,128)S(1)} %get-tuple-element.50), channel_id=1, source_target_pairs={{0,1},{1,0},{2,7},{3,6},{4,5},{5,4},{6,11},{7,10},{8,9},{9,8},{10,... | collective-permute-start | bytes 196616 | tf_op jit(solution)/shard_map/ppermute | solution.py:535
  22.7 0.7 %collective-permute-start.7 = (f32[4,32,128]{2,1,0:T(8,128)S(1)}, f32[4,32,128]{2,1,0:T(8,128)S(1)}, u32[]{:S(2)}, u32[]{:S(2)}) collective-permute-start(f32[4,32,128]{2,1,0:T(8,128)S(1)} %get-tuple-element.47.refs_2_), channel_id=1, source_target_pairs={{2,6},{3,7},{6,10},{7,11},{10,14},{11,15},{14,18},{15,19},{18,22},... | collective-permute-start | bytes 196616 | tf_op jit(solution)/shard_map/ppermute | solution.py:535
  23.4 4.6 %collective-permute-done.8.refs_4_ = f32[4,32,128]{2,1,0:T(8,128)S(1)} collective-permute-done((f32[4,32,128]{2,1,0:T(8,128)S(1)}, f32[4,32,128]{2,1,0:T(8,128)S(1)}, u32[]{:S(2)}, u32[]{:S(2)}) %collective-permute-start.8) | collective-permute-done | bytes 65568 | tf_op jit(solution)/shard_map/ppermute | solution.py:535
  28.0 0.0 collective-permute-done.9.refs_5_
  28.0 0.6 %collective-permute-done.10.refs_6_ = f32[4,32,128]{2,1,0:T(8,128)S(1)} collective-permute-done((f32[4,32,128]{2,1,0:T(8,128)S(1)}, f32[4,32,128]{2,1,0:T(8,128)S(1)}, u32[]{:S(2)}, u32[]{:S(2)}) %collective-permute-start.10) | collective-permute-done | bytes 65568 | tf_op jit(solution)/shard_map/ppermute | solution.py:535
  28.6 0.0 collective-permute-done.7.refs_3_
  28.6 4.3 %collective-permute-start.13 = (f32[4,32,128]{2,1,0:T(8,128)S(1)}, f32[4,32,128]{2,1,0:T(8,128)S(1)}, u32[]{:S(2)}, u32[]{:S(2)}) collective-permute-start(f32[4,32,128]{2,1,0:T(8,128)S(1)} %update.1.refs_0_), channel_id=1, source_target_pairs={{0,3},{1,2},{2,1},{3,0},{4,7},{5,6},{6,5},{7,4},{8,11},{9,10},{10,... | collective-permute-start | bytes 196616 | tf_op jit(solution)/shard_map/ppermute | solution.py:548
  32.9 0.8 %collective-permute-start.12 = (f32[4,32,128]{2,1,0:T(8,128)S(1)}, f32[4,32,128]{2,1,0:T(8,128)S(1)}, u32[]{:S(2)}, u32[]{:S(2)}) collective-permute-start(f32[4,32,128]{2,1,0:T(8,128)S(1)} %update.1.refs_0_), channel_id=1, source_target_pairs={{0,2},{1,3},{2,0},{3,1},{4,6},{5,7},{6,4},{7,5},{8,10},{9,11},{10,... | collective-permute-start | bytes 196616 | tf_op jit(solution)/shard_map/ppermute | solution.py:548
  33.6 0.5 %collective-permute-start.11 = (f32[4,32,128]{2,1,0:T(8,128)S(1)}, f32[4,32,128]{2,1,0:T(8,128)S(1)}, u32[]{:S(2)}, u32[]{:S(2)}) collective-permute-start(f32[4,32,128]{2,1,0:T(8,128)S(1)} %update.1.refs_0_), channel_id=1, source_target_pairs={{0,1},{1,0},{2,3},{3,2},{4,5},{5,4},{6,7},{7,6},{8,9},{9,8},{10,11... | collective-permute-start | bytes 196616 | tf_op jit(solution)/shard_map/ppermute | solution.py:548
  34.1 1.1 %collective-permute-done.13.refs_3_ = f32[4,32,128]{2,1,0:T(8,128)S(1)} collective-permute-done((f32[4,32,128]{2,1,0:T(8,128)S(1)}, f32[4,32,128]{2,1,0:T(8,128)S(1)}, u32[]{:S(2)}, u32[]{:S(2)}) %collective-permute-start.13) | collective-permute-done | bytes 65568 | tf_op jit(solution)/shard_map/ppermute | solution.py:548
  35.2 3.0 %collective-permute-done.12.refs_2_ = f32[4,32,128]{2,1,0:T(8,128)S(1)} collective-permute-done((f32[4,32,128]{2,1,0:T(8,128)S(1)}, f32[4,32,128]{2,1,0:T(8,128)S(1)}, u32[]{:S(2)}, u32[]{:S(2)}) %collective-permute-start.12) | collective-permute-done | bytes 65568 | tf_op jit(solution)/shard_map/ppermute | solution.py:548
  38.2 0.5 %collective-permute-done.11.refs_1_ = f32[4,32,128]{2,1,0:T(8,128)S(1)} collective-permute-done((f32[4,32,128]{2,1,0:T(8,128)S(1)}, f32[4,32,128]{2,1,0:T(8,128)S(1)}, u32[]{:S(2)}, u32[]{:S(2)}) %collective-permute-start.11) | collective-permute-done | bytes 65568 | tf_op jit(solution)/shard_map/ppermute | solution.py:548
  38.7 0.8 %join.1 = f32[4,128,128]{2,1,0:T(8,128)} custom-call(f32[4,32,128]{2,1,0:T(8,128)S(1)} %update.1.refs_0_, f32[4,32,128]{2,1,0:T(8,128)S(1)} %collective-permute-done.11.refs_1_, f32[4,32,128]{2,1,0:T(8,128)S(1)} %collective-permute-done.12.refs_2_, f32[4,32,128]{2,1,0:T(8,128)S(1)} %collective-permute-done.13.refs_3_), custom_call_target="tpu_custom_call" | custom-call | tf_op jit(solution)/shard_map/join/pallas_call | solution.py:549
  (2 shorter events, 0.0 us)
Async XLA Ops:
  0.0 7.5 %collective-permute-start.1 = (f32[4,128,128]{2,1,0:T(8,128)}, f32[4,128,128]{2,1,0:T(8,128)S(1)}, u32[]{:S(2)}, u32[]{:S(2)}) collective-permute-start(f32[4,128,128]{2,1,0:T(8,128)} %maps_any.1), channel_id=1, source_target_pairs={{0,28},{4,0},{8,4},{12,8},{16,12},{20,16},{24,20},{28,24},{1,29},{... | collective-permute-start | bytes 786440 | tf_op jit(solution)/shard_map/ppermute | solution.py:439
  5.8 10.7 %collective-permute-start.5 = (f32[128,128]{1,0:T(8,128)S(1)}, f32[128,128]{1,0:T(8,128)S(1)}, u32[]{:S(2)}, u32[]{:S(2)}) collective-permute-start(f32[128,128]{1,0:T(8,128)S(1)} %get-tuple-element.45.one), channel_id=1, source_target_pairs={{28,29},{29,28},{30,31},{31,30}} | collective-permute-start | bytes 196616 | tf_op jit(solution)/shard_map/ppermute | solution.py:477
  9.1 9.3 %collective-permute-start.2 = (f32[160,128]{1,0:T(8,128)S(1)}, f32[160,128]{1,0:T(8,128)S(1)}, u32[]{:S(2)}, u32[]{:S(2)}) collective-permute-start(f32[160,128]{1,0:T(8,128)S(1)} %get-tuple-element.42), channel_id=1, source_target_pairs={{0,3},{1,2},{2,1},{3,0},{4,7},{5,6},{6,5},{7,4},{8,11},{9,10},{10,... | collective-permute-start | bytes 245768 | tf_op jit(solution)/shard_map/ppermute | solution.py:504
  12.8 6.3 %collective-permute-start.3 = (f32[160,128]{1,0:T(8,128)S(1)}, f32[160,128]{1,0:T(8,128)S(1)}, u32[]{:S(2)}, u32[]{:S(2)}) collective-permute-start(f32[160,128]{1,0:T(8,128)S(1)} %get-tuple-element.43), channel_id=1, source_target_pairs={{0,1},{1,0},{2,3},{3,2},{4,5},{5,4},{6,7},{7,6},{8,9},{9,8},{10,11... | collective-permute-start | bytes 245768 | tf_op jit(solution)/shard_map/ppermute | solution.py:504
  12.8 6.3 %collective-permute-start.4 = (f32[160,128]{1,0:T(8,128)S(1)}, f32[160,128]{1,0:T(8,128)S(1)}, u32[]{:S(2)}, u32[]{:S(2)}) collective-permute-start(f32[160,128]{1,0:T(8,128)S(1)} %get-tuple-element.44), channel_id=1, source_target_pairs={{0,2},{1,3},{2,0},{3,1},{4,6},{5,7},{6,4},{7,5},{8,10},{9,11},{10,... | collective-permute-start | bytes 245768 | tf_op jit(solution)/shard_map/ppermute | solution.py:504
  13.6 4.8 %collective-permute-start = (f32[128,128]{1,0:T(8,128)S(1)}, f32[128,128]{1,0:T(8,128)S(1)}, u32[]{:S(2)}, u32[]{:S(2)}) collective-permute-start(f32[128,128]{1,0:T(8,128)S(1)} %get-tuple-element.34), channel_id=1, source_target_pairs={{0,28},{4,0},{8,4},{12,8},{16,12},{20,16},{24,20},{28,24},{1,29},{... | collective-permute-start | bytes 196616 | tf_op jit(solution)/shard_map/ppermute | solution.py:488
  16.5 1.9 %collective-permute-start.6 = (f32[128,128]{1,0:T(8,128)S(1)}, f32[128,128]{1,0:T(8,128)S(1)}, u32[]{:S(2)}, u32[]{:S(2)}) collective-permute-start(f32[128,128]{1,0:T(8,128)S(1)} %pair.1.refs_11_), channel_id=1, source_target_pairs={{28,30},{29,31},{30,28},{31,29}} | collective-permute-start | bytes 196616 | tf_op jit(solution)/shard_map/ppermute | solution.py:477
  20.5 7.5 %collective-permute-start.8 = (f32[4,32,128]{2,1,0:T(8,128)S(1)}, f32[4,32,128]{2,1,0:T(8,128)S(1)}, u32[]{:S(2)}, u32[]{:S(2)}) collective-permute-start(f32[4,32,128]{2,1,0:T(8,128)S(1)} %get-tuple-element.48), channel_id=1, source_target_pairs={{0,6},{1,7},{2,0},{3,1},{4,10},{5,11},{6,4},{7,5},{8,14},{9,15},{1... | collective-permute-start | bytes 196616 | tf_op jit(solution)/shard_map/ppermute | solution.py:535
  21.0 7.0 %collective-permute-start.9 = (f32[4,32,128]{2,1,0:T(8,128)S(1)}, f32[4,32,128]{2,1,0:T(8,128)S(1)}, u32[]{:S(2)}, u32[]{:S(2)}) collective-permute-start(f32[4,32,128]{2,1,0:T(8,128)S(1)} %get-tuple-element.49), channel_id=1, source_target_pairs={{0,7},{1,6},{2,1},{3,0},{4,11},{5,10},{6,5},{7,4},{8,15},{9,14},{1... | collective-permute-start | bytes 196616 | tf_op jit(solution)/shard_map/ppermute | solution.py:535
  22.2 6.3 %collective-permute-start.10 = (f32[4,32,128]{2,1,0:T(8,128)S(1)}, f32[4,32,128]{2,1,0:T(8,128)S(1)}, u32[]{:S(2)}, u32[]{:S(2)}) collective-permute-start(f32[4,32,128]{2,1,0:T(8,128)S(1)} %get-tuple-element.50), channel_id=1, source_target_pairs={{0,1},{1,0},{2,7},{3,6},{4,5},{5,4},{6,11},{7,10},{8,9},{9,8},{10,... | collective-permute-start | bytes 196616 | tf_op jit(solution)/shard_map/ppermute | solution.py:535
  22.7 5.8 %collective-permute-start.7 = (f32[4,32,128]{2,1,0:T(8,128)S(1)}, f32[4,32,128]{2,1,0:T(8,128)S(1)}, u32[]{:S(2)}, u32[]{:S(2)}) collective-permute-start(f32[4,32,128]{2,1,0:T(8,128)S(1)} %get-tuple-element.47.refs_2_), channel_id=1, source_target_pairs={{2,6},{3,7},{6,10},{7,11},{10,14},{11,15},{14,18},{15,19},{18,22},... | collective-permute-start | bytes 196616 | tf_op jit(solution)/shard_map/ppermute | solution.py:535
  28.6 6.6 %collective-permute-start.13 = (f32[4,32,128]{2,1,0:T(8,128)S(1)}, f32[4,32,128]{2,1,0:T(8,128)S(1)}, u32[]{:S(2)}, u32[]{:S(2)}) collective-permute-start(f32[4,32,128]{2,1,0:T(8,128)S(1)} %update.1.refs_0_), channel_id=1, source_target_pairs={{0,3},{1,2},{2,1},{3,0},{4,7},{5,6},{6,5},{7,4},{8,11},{9,10},{10,... | collective-permute-start | bytes 196616 | tf_op jit(solution)/shard_map/ppermute | solution.py:548
  32.9 5.3 %collective-permute-start.12 = (f32[4,32,128]{2,1,0:T(8,128)S(1)}, f32[4,32,128]{2,1,0:T(8,128)S(1)}, u32[]{:S(2)}, u32[]{:S(2)}) collective-permute-start(f32[4,32,128]{2,1,0:T(8,128)S(1)} %update.1.refs_0_), channel_id=1, source_target_pairs={{0,2},{1,3},{2,0},{3,1},{4,6},{5,7},{6,4},{7,5},{8,10},{9,11},{10,... | collective-permute-start | bytes 196616 | tf_op jit(solution)/shard_map/ppermute | solution.py:548
  33.6 5.1 %collective-permute-start.11 = (f32[4,32,128]{2,1,0:T(8,128)S(1)}, f32[4,32,128]{2,1,0:T(8,128)S(1)}, u32[]{:S(2)}, u32[]{:S(2)}) collective-permute-start(f32[4,32,128]{2,1,0:T(8,128)S(1)} %update.1.refs_0_), channel_id=1, source_target_pairs={{0,1},{1,0},{2,3},{3,2},{4,5},{5,4},{6,7},{7,6},{8,9},{9,8},{10,11... | collective-permute-start | bytes 196616 | tf_op jit(solution)/shard_map/ppermute | solution.py:548
